TPU v7x, 512 devices: a whole 4x8x8 slice. The times are simulated.
512 devices in a mesh: tgt: 128 (over x, z, y_hi, core), src: 4 (over y_lo).
Axes of the slice: x: 4, y: 8 (y_hi: 2, y_lo: 4; y = y_hi * 4 + y_lo), z: 8, core: 2. Of those that a mesh axis runs over, the one named last changes fastest.
Arguments:
- fibre_points: float32 [3, 1024, 64], P(None, ('tgt', 'src')), may hold values from -6 to 6
- shell_points: float32 [3, 128, 64], P(None, 'tgt', 'src'), may hold values from -7 to 7, as said below
- bending: float32 [64, 64], replicated, may hold values from -0.12 to 0.12
- shell_inverse: bfloat16 [3, 128, 64, 3, 64, 128], P(None, 'tgt', None, None, 'src'), may hold values from -0.0390625 to 0.0390625
Outputs:
- fibre_velocity: float32 [3, 1024, 64], P(None, ('tgt', 'src'))
- shell_density: float32 [3, 128, 64], P(None, 'tgt', 'src')
Inputs may be any that keep to these rules, and one draw needn't show every extreme that they name: `shell_points`: every shell node lies on the sphere of radius 7 about the anchor.
All inputs are finite; a program needn't handle non-finite values.
Results may differ from a plain program's by a relative error of at most 0.0029.
Values may be sent and summed in bfloat16 or wider, within the bound.
No kernel may reach another device: no remote copies, remote signals or barrier semaphores. Data moves between devices by JAX's collectives and lax.ppermute only.
A program may use at most 64 MiB of HBM per device.

v0:
```python
import math

import jax
import jax.numpy as jnp
from jax import lax
from jax.sharding import Mesh
from jax.sharding import PartitionSpec as P

TGT = ("tgt_0", "tgt_1", "tgt_2", "tgt_3")
TGT_SRC = ("tgt_0", "tgt_1", "tgt_2", "tgt_3", "src")


mobility = 1.0 / (8.0 * math.pi)
soften_sq = 0.0025


def laid_out(pieces, dim):
    lengths = list(pieces.shape[1:])
    lengths[dim] *= pieces.shape[0]
    return jnp.moveaxis(pieces, 0, dim).reshape(lengths)


def sent_to_all(x, axis):
    length = lax.axis_size(axis)
    return lax.all_to_all(jnp.broadcast_to(x[None], (length, *x.shape)), axis, 0, 0, tiled=True)


def gathered_copies(x, axis, dim):
    return laid_out(sent_to_all(x, axis), dim)


def whole_of(x, axes, dim):
    far, near = axes
    pieces = sent_to_all(sent_to_all(x, far), near)
    return laid_out(pieces.swapaxes(0, 1).reshape(-1, *x.shape), dim)


def sent_together(arrays, axis, dim, along):
    ends, at = ([], 0)
    for a in arrays[:-1]:
        at += a.shape[along]
        ends.append(at)
    both = jnp.concatenate(arrays, axis=along)
    return tuple(jnp.split(whole_of(both, axis, dim), ends, axis=along))


def split_up(x, dim, length):
    before, after = (x.shape[:dim], x.shape[dim + 1 :])
    return jnp.moveaxis(x.reshape(*before, length, -1, *after), dim, 0)


def sum_at_owner(x, axis, dim):
    length = lax.axis_size(axis)
    pieces = lax.all_to_all(split_up(x, dim, length), axis, 0, 0, tiled=True)
    return jnp.sum(pieces, axis=0)


def stokes_flow(targets, sources, strength):
    delta_x = targets[0][:, None] - sources[0][None, :]
    delta_y = targets[1][:, None] - sources[1][None, :]
    delta_z = targets[2][:, None] - sources[2][None, :]
    dist_sq = delta_x * delta_x + delta_y * delta_y + delta_z * delta_z
    inv_root = lax.rsqrt(dist_sq + soften_sq)
    inv_cubed = inv_root * inv_root * inv_root
    projection = (
        delta_x * strength[0][None, :]
        + delta_y * strength[1][None, :]
        + delta_z * strength[2][None, :]
    ) * inv_cubed
    diagonal_part = (dist_sq + 2.0 * soften_sq) * inv_cubed
    flow_x = jnp.sum(diagonal_part * strength[0][None, :] + projection * delta_x, axis=1)
    flow_y = jnp.sum(diagonal_part * strength[1][None, :] + projection * delta_y, axis=1)
    flow_z = jnp.sum(diagonal_part * strength[2][None, :] + projection * delta_z, axis=1)
    return mobility * jnp.stack([flow_x, flow_y, flow_z])


def block_width(column_count, target_count):
    widest = 128
    while widest * 2 * target_count <= 1 << 20:
        widest = widest * 2
    return math.gcd(column_count, widest)


def source_sum(running, targets, places, pushes):
    block_size = block_width(places.shape[1], targets.shape[1])
    turns = places.shape[1] // block_size

    def add_block(counter, partial_value):
        offset = counter * block_size
        part_places = lax.dynamic_slice_in_dim(places, offset, block_size, 1)
        part_pushes = lax.dynamic_slice_in_dim(pushes, offset, block_size, 1)
        return partial_value + stokes_flow(targets, part_places, part_pushes)

    return lax.fori_loop(0, turns, add_block, running)


def fibre_fold(targets, running, pieces):
    return source_sum(running, targets, pieces[0].reshape(3, -1), pieces[1].reshape(3, -1))


def per_device(fibre_points, shell_points, bending, shell_inverse):
    shell_rows = gathered_copies(shell_points, "src", 2)
    columns_pos = whole_of(shell_points, (("tgt_0", "tgt_1", "tgt_2"), "tgt_3"), 1)
    forces = -jnp.einsum("cfm,nm->cfn", fibre_points, bending, precision=lax.Precision.HIGHEST)
    fibre_block = gathered_copies(fibre_points, "src", 1)
    block_flat = fibre_block.reshape(3, -1)
    targets = jnp.concatenate([block_flat, shell_rows.reshape(3, -1)], axis=1)
    zeros_flow = jnp.zeros(targets.shape, jnp.float32)
    flow_all = fibre_fold(
        targets,
        zeros_flow,
        sent_together((fibre_points, forces), (("tgt_0", "tgt_1", "tgt_2"), "tgt_3"), 1, 0),
    )
    block_count = block_flat.shape[1]
    fibre_part = flow_all[:, :block_count].reshape(fibre_block.shape)
    shell_part = flow_all[:, block_count:].reshape(shell_rows.shape)
    fibre_flow = sum_at_owner(fibre_part, "src", 1)
    shell_flow = sum_at_owner(shell_part, "src", 2)
    columns = whole_of(shell_flow.astype(jnp.bfloat16), (("tgt_0", "tgt_1", "tgt_2"), "tgt_3"), 1)
    density_rows = -jnp.einsum(
        "xaqcbn,cnb->xaq", shell_inverse, columns, preferred_element_type=jnp.float32
    )
    density = sum_at_owner(density_rows, "src", 2)
    column_density = whole_of(density, (("tgt_0", "tgt_1", "tgt_2"), "tgt_3"), 1)
    zeros_back = jnp.zeros(block_flat.shape, jnp.float32)
    back_block = source_sum(
        zeros_back, block_flat, columns_pos.reshape(3, -1), column_density.reshape(3, -1)
    )
    shell_back = sum_at_owner(back_block.reshape(fibre_block.shape), "src", 1)
    velocity = fibre_flow + shell_back
    return (velocity, density)


def solution(mesh):
    torus = Mesh(
        mesh.devices.reshape(4, 8, 2, 2, mesh.shape["src"]),
        ("tgt_0", "tgt_1", "tgt_2", "tgt_3", "src"),
    )
    in_specs = (
        P(None, TGT_SRC, None),
        P(None, TGT, "src"),
        P(),
        P(None, TGT, None, None, "src", None),
    )
    out_specs = (P(None, TGT_SRC, None), P(None, TGT, "src"))
    return jax.shard_map(
        per_device, mesh=torus, in_specs=in_specs, out_specs=out_specs, check_vma=False
    )
```

profile of v0, /device:TPU:1, one launch (start us, length us, event | category | flops | bytes accessed | tf_op | source)
XLA Modules:
  0.0 233.4 jit_solution(7889073819214115765)
XLA Ops:
  0.6 0.8 copy.104
  2.1 5.4 %all-to-all-start.1 = ((f32[4,3,1,16]{3,2,1,0:T(1,128)}), f32[4,3,1,16]{3,2,1,0:T(1,128)S(1)}, u32[]{:S(2)}, u32[]{:S(2)}) async-start(f32[4,3,1,16]{3,2,1,0:T(1,128)} %broadcast_in_dim.33), calls=%async_computation.1 | async-start | bytes 12288 | tf_op jit(solution)/shard_map/all_to_all | solution.py:25
  8.9 3.1 %all-to-all-done.1 = f32[4,3,1,16]{3,2,1,0:T(1,128)S(1)} async-done(((f32[4,3,1,16]{3,2,1,0:T(1,128)}), f32[4,3,1,16]{3,2,1,0:T(1,128)S(1)}, u32[]{:S(2)}, u32[]{:S(2)}) %all-to-all-start.1) | async-done | bytes 800 | tf_op jit(solution)/shard_map/all_to_all | solution.py:25
  11.9 3.2 %all-to-all-start = ((f32[4,1,384]{2,1,0:T(1,128)}), f32[4,1,384]{2,1,0:T(1,128)S(1)}, u32[]{:S(2)}, u32[]{:S(2)}) async-start(f32[4,1,384]{2,1,0:T(1,128)} %reshape.114), calls=%async_computation | async-start | bytes 12288 | tf_op jit(solution)/shard_map/all_to_all | solution.py:25
  15.2 0.9 convolution_negate_fusion
  16.8 2.8 %all-to-all-done = f32[4,1,384]{2,1,0:T(1,128)S(1)} async-done(((f32[4,1,384]{2,1,0:T(1,128)}), f32[4,1,384]{2,1,0:T(1,128)S(1)}, u32[]{:S(2)}, u32[]{:S(2)}) %all-to-all-start) | async-done | bytes 6176 | tf_op jit(solution)/shard_map/all_to_all | solution.py:25
  20.3 17.4 %all-to-all-start.5 = ((f32[64,3,1,16]{3,2,1,0:T(1,128)}), f32[64,3,1,16]{3,2,1,0:T(1,128)S(1)}, u32[]{:S(2)}, u32[]{:S(2)}) async-start(f32[64,3,1,16]{3,2,1,0:T(1,128)} %broadcast_in_dim.36), calls=%async_computation.5 | async-start | bytes 196608 | tf_op jit(solution)/shard_map/all_to_all | solution.py:25
  37.8 1.1 reshape.116
  38.9 12.0 %all-to-all-done.5 = f32[64,3,1,16]{3,2,1,0:T(1,128)S(1)} async-done(((f32[64,3,1,16]{3,2,1,0:T(1,128)}), f32[64,3,1,16]{3,2,1,0:T(1,128)S(1)}, u32[]{:S(2)}, u32[]{:S(2)}) %all-to-all-start.5) | async-done | bytes 12320 | tf_op jit(solution)/shard_map/all_to_all | solution.py:25
  50.9 4.6 %all-to-all-start.2 = ((f32[64,1,768]{2,1,0:T(1,128)}), f32[64,1,768]{2,1,0:T(1,128)S(1)}, u32[]{:S(2)}, u32[]{:S(2)}) async-start(f32[64,1,768]{2,1,0:T(1,128)} %reshape.116), calls=%async_computation.2 | async-start | bytes 393216 | tf_op jit(solution)/shard_map/all_to_all | solution.py:25
  58.3 10.8 %all-to-all-done.2 = f32[64,1,768]{2,1,0:T(1,128)S(1)} async-done(((f32[64,1,768]{2,1,0:T(1,128)}), f32[64,1,768]{2,1,0:T(1,128)S(1)}, u32[]{:S(2)}, u32[]{:S(2)}) %all-to-all-start.2) | async-done | bytes 196640 | tf_op jit(solution)/shard_map/all_to_all | solution.py:25
  69.1 1.1 reduce.9
  71.8 9.2 %all_to_all.70 = f32[2,1,49152]{2,1,0:T(1,128)S(1)} all-to-all(f32[2,1,49152]{2,1,0:T(1,128)S(1)} %reshape.118), channel_id=1, replica_groups=mesh['tgt_0'=4,'tgt_1'=8,'tgt_2'=2,'tgt_3'=2,'src'=4] {'tgt_3'}, dimensions={0} | all-to-all | bytes 786432 | tf_op jit(solution)/shard_map/all_to_all | solution.py:25
  80.9 1.9 reduce.10
  85.7 53.6 %while.9 = (s32[]{:T(128)}, f32[3,576]{1,0:T(4,128)S(1)}, f32[3,576]{1,0:T(4,128)S(1)}, f32[3,16384]{1,0:T(4,128)S(1)}, f32[3,16384]{1,0:T(4,128)S(1)}, /*index=...) while((s32[]{:T(128)}, f32[3,576]{1,0:T(4,128)S(1)}, ...), condition=%wide.region_4.0_spmd.clone, body=%wide.region_0.0_spmd.clone.sunk | while | flops 18291464 | bytes 136137 | solution.py:94
  85.8 3.1 %fusion.48 = (f32[576]{0:T(1024)S(1)}, f32[576]{0:T(1024)S(1)}, f32[576]{0:T(1024)S(1)}) fusion(f32[1024]{0:T(1024)S(1)} %bitcast.117, f32[1024]{0:T(1024)S(1)} %bitcast.120, f32[576]{0:T(1024)S(1)} %get-tuple-element.229, f32[1024]{0:T(1024)S(1)} %bitcast.119, f32[576]{0:T(1024)S(1)} %get-tuple-element.231, f32[1024]{0:T(1024)S(1)} %bitcast.121, ...), kind=kLoop, calls=%fused_computation.16.clone.1 | loop fusion | flops 18282816 | bytes 38400 | tf_op jit(solution)/shard_map/while/body/eval_jaxpr/reduce_sum | solution.py:71
  89.2 3.1 %fusion.48 = (f32[576]{0:T(1024)S(1)}, f32[576]{0:T(1024)S(1)}, f32[576]{0:T(1024)S(1)}) fusion(f32[1024]{0:T(1024)S(1)} %bitcast.117, f32[1024]{0:T(1024)S(1)} %bitcast.120, f32[576]{0:T(1024)S(1)} %get-tuple-element.229, f32[1024]{0:T(1024)S(1)} %bitcast.119, f32[576]{0:T(1024)S(1)} %get-tuple-element.231, f32[1024]{0:T(1024)S(1)} %bitcast.121, ...), kind=kLoop, calls=%fused_computation.16.clone.1 | loop fusion | flops 18282816 | bytes 38400 | tf_op jit(solution)/shard_map/while/body/eval_jaxpr/reduce_sum | solution.py:71
  92.5 3.1 %fusion.48 = (f32[576]{0:T(1024)S(1)}, f32[576]{0:T(1024)S(1)}, f32[576]{0:T(1024)S(1)}) fusion(f32[1024]{0:T(1024)S(1)} %bitcast.117, f32[1024]{0:T(1024)S(1)} %bitcast.120, f32[576]{0:T(1024)S(1)} %get-tuple-element.229, f32[1024]{0:T(1024)S(1)} %bitcast.119, f32[576]{0:T(1024)S(1)} %get-tuple-element.231, f32[1024]{0:T(1024)S(1)} %bitcast.121, ...), kind=kLoop, calls=%fused_computation.16.clone.1 | loop fusion | flops 18282816 | bytes 38400 | tf_op jit(solution)/shard_map/while/body/eval_jaxpr/reduce_sum | solution.py:71
  95.9 3.1 %fusion.48 = (f32[576]{0:T(1024)S(1)}, f32[576]{0:T(1024)S(1)}, f32[576]{0:T(1024)S(1)}) fusion(f32[1024]{0:T(1024)S(1)} %bitcast.117, f32[1024]{0:T(1024)S(1)} %bitcast.120, f32[576]{0:T(1024)S(1)} %get-tuple-element.229, f32[1024]{0:T(1024)S(1)} %bitcast.119, f32[576]{0:T(1024)S(1)} %get-tuple-element.231, f32[1024]{0:T(1024)S(1)} %bitcast.121, ...), kind=kLoop, calls=%fused_computation.16.clone.1 | loop fusion | flops 18282816 | bytes 38400 | tf_op jit(solution)/shard_map/while/body/eval_jaxpr/reduce_sum | solution.py:71
  99.3 3.1 %fusion.48 = (f32[576]{0:T(1024)S(1)}, f32[576]{0:T(1024)S(1)}, f32[576]{0:T(1024)S(1)}) fusion(f32[1024]{0:T(1024)S(1)} %bitcast.117, f32[1024]{0:T(1024)S(1)} %bitcast.120, f32[576]{0:T(1024)S(1)} %get-tuple-element.229, f32[1024]{0:T(1024)S(1)} %bitcast.119, f32[576]{0:T(1024)S(1)} %get-tuple-element.231, f32[1024]{0:T(1024)S(1)} %bitcast.121, ...), kind=kLoop, calls=%fused_computation.16.clone.1 | loop fusion | flops 18282816 | bytes 38400 | tf_op jit(solution)/shard_map/while/body/eval_jaxpr/reduce_sum | solution.py:71
  102.6 3.1 %fusion.48 = (f32[576]{0:T(1024)S(1)}, f32[576]{0:T(1024)S(1)}, f32[576]{0:T(1024)S(1)}) fusion(f32[1024]{0:T(1024)S(1)} %bitcast.117, f32[1024]{0:T(1024)S(1)} %bitcast.120, f32[576]{0:T(1024)S(1)} %get-tuple-element.229, f32[1024]{0:T(1024)S(1)} %bitcast.119, f32[576]{0:T(1024)S(1)} %get-tuple-element.231, f32[1024]{0:T(1024)S(1)} %bitcast.121, ...), kind=kLoop, calls=%fused_computation.16.clone.1 | loop fusion | flops 18282816 | bytes 38400 | tf_op jit(solution)/shard_map/while/body/eval_jaxpr/reduce_sum | solution.py:71
  106.0 3.1 %fusion.48 = (f32[576]{0:T(1024)S(1)}, f32[576]{0:T(1024)S(1)}, f32[576]{0:T(1024)S(1)}) fusion(f32[1024]{0:T(1024)S(1)} %bitcast.117, f32[1024]{0:T(1024)S(1)} %bitcast.120, f32[576]{0:T(1024)S(1)} %get-tuple-element.229, f32[1024]{0:T(1024)S(1)} %bitcast.119, f32[576]{0:T(1024)S(1)} %get-tuple-element.231, f32[1024]{0:T(1024)S(1)} %bitcast.121, ...), kind=kLoop, calls=%fused_computation.16.clone.1 | loop fusion | flops 18282816 | bytes 38400 | tf_op jit(solution)/shard_map/while/body/eval_jaxpr/reduce_sum | solution.py:71
  109.3 3.1 %fusion.48 = (f32[576]{0:T(1024)S(1)}, f32[576]{0:T(1024)S(1)}, f32[576]{0:T(1024)S(1)}) fusion(f32[1024]{0:T(1024)S(1)} %bitcast.117, f32[1024]{0:T(1024)S(1)} %bitcast.120, f32[576]{0:T(1024)S(1)} %get-tuple-element.229, f32[1024]{0:T(1024)S(1)} %bitcast.119, f32[576]{0:T(1024)S(1)} %get-tuple-element.231, f32[1024]{0:T(1024)S(1)} %bitcast.121, ...), kind=kLoop, calls=%fused_computation.16.clone.1 | loop fusion | flops 18282816 | bytes 38400 | tf_op jit(solution)/shard_map/while/body/eval_jaxpr/reduce_sum | solution.py:71
  112.7 3.1 %fusion.48 = (f32[576]{0:T(1024)S(1)}, f32[576]{0:T(1024)S(1)}, f32[576]{0:T(1024)S(1)}) fusion(f32[1024]{0:T(1024)S(1)} %bitcast.117, f32[1024]{0:T(1024)S(1)} %bitcast.120, f32[576]{0:T(1024)S(1)} %get-tuple-element.229, f32[1024]{0:T(1024)S(1)} %bitcast.119, f32[576]{0:T(1024)S(1)} %get-tuple-element.231, f32[1024]{0:T(1024)S(1)} %bitcast.121, ...), kind=kLoop, calls=%fused_computation.16.clone.1 | loop fusion | flops 18282816 | bytes 38400 | tf_op jit(solution)/shard_map/while/body/eval_jaxpr/reduce_sum | solution.py:71
  116.0 3.1 %fusion.48 = (f32[576]{0:T(1024)S(1)}, f32[576]{0:T(1024)S(1)}, f32[576]{0:T(1024)S(1)}) fusion(f32[1024]{0:T(1024)S(1)} %bitcast.117, f32[1024]{0:T(1024)S(1)} %bitcast.120, f32[576]{0:T(1024)S(1)} %get-tuple-element.229, f32[1024]{0:T(1024)S(1)} %bitcast.119, f32[576]{0:T(1024)S(1)} %get-tuple-element.231, f32[1024]{0:T(1024)S(1)} %bitcast.121, ...), kind=kLoop, calls=%fused_computation.16.clone.1 | loop fusion | flops 18282816 | bytes 38400 | tf_op jit(solution)/shard_map/while/body/eval_jaxpr/reduce_sum | solution.py:71
  119.4 3.1 %fusion.48 = (f32[576]{0:T(1024)S(1)}, f32[576]{0:T(1024)S(1)}, f32[576]{0:T(1024)S(1)}) fusion(f32[1024]{0:T(1024)S(1)} %bitcast.117, f32[1024]{0:T(1024)S(1)} %bitcast.120, f32[576]{0:T(1024)S(1)} %get-tuple-element.229, f32[1024]{0:T(1024)S(1)} %bitcast.119, f32[576]{0:T(1024)S(1)} %get-tuple-element.231, f32[1024]{0:T(1024)S(1)} %bitcast.121, ...), kind=kLoop, calls=%fused_computation.16.clone.1 | loop fusion | flops 18282816 | bytes 38400 | tf_op jit(solution)/shard_map/while/body/eval_jaxpr/reduce_sum | solution.py:71
  122.7 3.1 %fusion.48 = (f32[576]{0:T(1024)S(1)}, f32[576]{0:T(1024)S(1)}, f32[576]{0:T(1024)S(1)}) fusion(f32[1024]{0:T(1024)S(1)} %bitcast.117, f32[1024]{0:T(1024)S(1)} %bitcast.120, f32[576]{0:T(1024)S(1)} %get-tuple-element.229, f32[1024]{0:T(1024)S(1)} %bitcast.119, f32[576]{0:T(1024)S(1)} %get-tuple-element.231, f32[1024]{0:T(1024)S(1)} %bitcast.121, ...), kind=kLoop, calls=%fused_computation.16.clone.1 | loop fusion | flops 18282816 | bytes 38400 | tf_op jit(solution)/shard_map/while/body/eval_jaxpr/reduce_sum | solution.py:71
  126.1 3.1 %fusion.48 = (f32[576]{0:T(1024)S(1)}, f32[576]{0:T(1024)S(1)}, f32[576]{0:T(1024)S(1)}) fusion(f32[1024]{0:T(1024)S(1)} %bitcast.117, f32[1024]{0:T(1024)S(1)} %bitcast.120, f32[576]{0:T(1024)S(1)} %get-tuple-element.229, f32[1024]{0:T(1024)S(1)} %bitcast.119, f32[576]{0:T(1024)S(1)} %get-tuple-element.231, f32[1024]{0:T(1024)S(1)} %bitcast.121, ...), kind=kLoop, calls=%fused_computation.16.clone.1 | loop fusion | flops 18282816 | bytes 38400 | tf_op jit(solution)/shard_map/while/body/eval_jaxpr/reduce_sum | solution.py:71
  129.4 3.1 %fusion.48 = (f32[576]{0:T(1024)S(1)}, f32[576]{0:T(1024)S(1)}, f32[576]{0:T(1024)S(1)}) fusion(f32[1024]{0:T(1024)S(1)} %bitcast.117, f32[1024]{0:T(1024)S(1)} %bitcast.120, f32[576]{0:T(1024)S(1)} %get-tuple-element.229, f32[1024]{0:T(1024)S(1)} %bitcast.119, f32[576]{0:T(1024)S(1)} %get-tuple-element.231, f32[1024]{0:T(1024)S(1)} %bitcast.121, ...), kind=kLoop, calls=%fused_computation.16.clone.1 | loop fusion | flops 18282816 | bytes 38400 | tf_op jit(solution)/shard_map/while/body/eval_jaxpr/reduce_sum | solution.py:71
  132.8 3.1 %fusion.48 = (f32[576]{0:T(1024)S(1)}, f32[576]{0:T(1024)S(1)}, f32[576]{0:T(1024)S(1)}) fusion(f32[1024]{0:T(1024)S(1)} %bitcast.117, f32[1024]{0:T(1024)S(1)} %bitcast.120, f32[576]{0:T(1024)S(1)} %get-tuple-element.229, f32[1024]{0:T(1024)S(1)} %bitcast.119, f32[576]{0:T(1024)S(1)} %get-tuple-element.231, f32[1024]{0:T(1024)S(1)} %bitcast.121, ...), kind=kLoop, calls=%fused_computation.16.clone.1 | loop fusion | flops 18282816 | bytes 38400 | tf_op jit(solution)/shard_map/while/body/eval_jaxpr/reduce_sum | solution.py:71
  136.1 3.1 %fusion.48 = (f32[576]{0:T(1024)S(1)}, f32[576]{0:T(1024)S(1)}, f32[576]{0:T(1024)S(1)}) fusion(f32[1024]{0:T(1024)S(1)} %bitcast.117, f32[1024]{0:T(1024)S(1)} %bitcast.120, f32[576]{0:T(1024)S(1)} %get-tuple-element.229, f32[1024]{0:T(1024)S(1)} %bitcast.119, f32[576]{0:T(1024)S(1)} %get-tuple-element.231, f32[1024]{0:T(1024)S(1)} %bitcast.121, ...), kind=kLoop, calls=%fused_computation.16.clone.1 | loop fusion | flops 18282816 | bytes 38400 | tf_op jit(solution)/shard_map/while/body/eval_jaxpr/reduce_sum | solution.py:71
  140.0 3.2 %all-to-all-start.7 = ((f32[4,3,1,16]{3,2,1,0:T(1,128)}), f32[4,3,1,16]{3,2,1,0:T(1,128)S(1)}, u32[]{:S(2)}, u32[]{:S(2)}) async-start(f32[4,3,1,16]{3,2,1,0:T(1,128)} %copy.82), calls=%async_computation.7 | async-start | bytes 12288 | tf_op jit(solution)/shard_map/all_to_all | solution.py:54
  143.9 3.7 %all-to-all-done.7 = f32[4,3,1,16]{3,2,1,0:T(1,128)S(1)} async-done(((f32[4,3,1,16]{3,2,1,0:T(1,128)}), f32[4,3,1,16]{3,2,1,0:T(1,128)S(1)}, u32[]{:S(2)}, u32[]{:S(2)}) %all-to-all-start.7) | async-done | bytes 800 | tf_op jit(solution)/shard_map/all_to_all | solution.py:54
  147.6 4.7 %all-to-all-start.6 = ((f32[2,1,3072]{2,1,0:T(1,128)}), f32[2,1,3072]{2,1,0:T(1,128)S(1)}, u32[]{:S(2)}, u32[]{:S(2)}) async-start(f32[2,1,3072]{2,1,0:T(1,128)} %reshape.126), calls=%async_computation.6 | async-start | bytes 49152 | tf_op jit(solution)/shard_map/all_to_all | solution.py:25
  152.4 1.0 all-to-all-done.6
  154.0 5.1 %all-to-all-start.8 = ((bf16[64,3,1,16]{3,1,2,0:T(4,128)(2,1)}), bf16[64,3,1,16]{3,1,2,0:T(4,128)(2,1)S(1)}, u32[]{:S(2)}, u32[]{:S(2)}) async-start(bf16[64,3,1,16]{3,1,2,0:T(4,128)(2,1)} %broadcast_in_dim.39), calls=%async_computation.8 | async-start | bytes 131072 | tf_op jit(solution)/shard_map/all_to_all | solution.py:25
  160.2 12.1 %all-to-all-done.8 = bf16[64,3,1,16]{3,1,2,0:T(4,128)(2,1)S(1)} async-done(((bf16[64,3,1,16]{3,1,2,0:T(4,128)(2,1)}), bf16[64,3,1,16]{3,1,2,0:T(4,128)(2,1)S(1)}, u32[]{:S(2)}, u32[]{:S(2)}) %all-to-all-start.8) | async-done | bytes 6176 | tf_op jit(solution)/shard_map/all_to_all | solution.py:25
  172.5 5.1 %all_to_all.71 = bf16[2,2,1536]{2,1,0:T(2,128)(2,1)S(1)} all-to-all(bf16[2,2,1536]{2,1,0:T(2,128)(2,1)S(1)} %reshape.122), channel_id=1, replica_groups=mesh['tgt_0'=4,'tgt_1'=8,'tgt_2'=2,'tgt_3'=2,'src'=4] {'tgt_3'}, dimensions={0} | all-to-all | bytes 24576 | tf_op jit(solution)/shard_map/all_to_all | solution.py:25
  177.9 0.9 fusion.31
  179.6 3.2 %all-to-all-start.10 = ((f32[4,3,1,16]{3,2,1,0:T(1,128)}), f32[4,3,1,16]{3,2,1,0:T(1,128)S(1)}, u32[]{:S(2)}, u32[]{:S(2)}) async-start(f32[4,3,1,16]{3,2,1,0:T(1,128)} %copy.86), calls=%async_computation.10 | async-start | bytes 12288 | tf_op jit(solution)/shard_map/all_to_all | solution.py:54
  183.0 4.3 %all-to-all-done.10 = f32[4,3,1,16]{3,2,1,0:T(1,128)S(1)} async-done(((f32[4,3,1,16]{3,2,1,0:T(1,128)}), f32[4,3,1,16]{3,2,1,0:T(1,128)S(1)}, u32[]{:S(2)}, u32[]{:S(2)}) %all-to-all-start.10) | async-done | bytes 800 | tf_op jit(solution)/shard_map/all_to_all | solution.py:54
  187.9 4.6 %all-to-all-start.11 = ((f32[64,3,1,16]{3,2,1,0:T(1,128)}), f32[64,3,1,16]{3,2,1,0:T(1,128)S(1)}, u32[]{:S(2)}, u32[]{:S(2)}) async-start(f32[64,3,1,16]{3,2,1,0:T(1,128)} %broadcast_in_dim.84), calls=%async_computation.11 | async-start | bytes 196608 | tf_op jit(solution)/shard_map/all_to_all | solution.py:25
  193.6 12.2 %all-to-all-done.11 = f32[64,3,1,16]{3,2,1,0:T(1,128)S(1)} async-done(((f32[64,3,1,16]{3,2,1,0:T(1,128)}), f32[64,3,1,16]{3,2,1,0:T(1,128)S(1)}, u32[]{:S(2)}, u32[]{:S(2)}) %all-to-all-start.11) | async-done | bytes 12320 | tf_op jit(solution)/shard_map/all_to_all | solution.py:25
  206.0 6.0 %all_to_all.72 = f32[2,1,3072]{2,1,0:T(1,128)S(1)} all-to-all(f32[2,1,3072]{2,1,0:T(1,128)S(1)} %reshape.124), channel_id=1, replica_groups=mesh['tgt_0'=4,'tgt_1'=8,'tgt_2'=2,'tgt_3'=2,'src'=4] {'tgt_3'}, dimensions={0} | all-to-all | bytes 49152 | tf_op jit(solution)/shard_map/all_to_all | solution.py:25
  212.1 3.2 %all-to-all-start.4 = ((f32[4,1,384]{2,1,0:T(1,128)}), f32[4,1,384]{2,1,0:T(1,128)S(1)}, u32[]{:S(2)}, u32[]{:S(2)}) async-start(f32[4,1,384]{2,1,0:T(1,128)} %reshape.120), calls=%async_computation.4 | async-start | bytes 12288 | tf_op jit(solution)/shard_map/all_to_all | solution.py:54
  216.5 5.6 %fusion.22 = (f32[512]{0:T(512)S(1)}, f32[512]{0:T(512)S(1)}, f32[512]{0:T(512)S(1)}) fusion(f32[2048]{0:T(1024)S(1)} %mul.302, f32[2048]{0:T(1024)S(1)} %sub.197, f32[512]{0:T(512)S(1)} %sub.195, f32[2048]{0:T(1024)S(1)} %sub.207, f32[512]{0:T(512)S(1)} %sub.205, f32[2048]{0:T(1024)S(1)} %sub.202, f32[512]{0:T(512)S(1)} %sub.200, f32[2048]{0:T(1024)S(1)} %mul.309, ...), kind=kLoop, calls=%fused_computation.48 | loop fusion | flops 32504320 | bytes 61440 | tf_op jit(solution)/shard_map/while/body/eval_jaxpr/reduce_sum | solution.py:71
  223.1 4.5 %all-to-all-start.13 = ((f32[4,1,384]{2,1,0:T(1,128)}), f32[4,1,384]{2,1,0:T(1,128)S(1)}, u32[]{:S(2)}, u32[]{:S(2)}) async-start(f32[4,1,384]{2,1,0:T(1,128)} %reshape.128), calls=%async_computation.13 | async-start | bytes 12288 | tf_op jit(solution)/shard_map/all_to_all | solution.py:54
  228.9 3.1 %all-to-all-done.13 = f32[4,1,384]{2,1,0:T(1,128)S(1)} async-done(((f32[4,1,384]{2,1,0:T(1,128)}), f32[4,1,384]{2,1,0:T(1,128)S(1)}, u32[]{:S(2)}, u32[]{:S(2)}) %all-to-all-start.13) | async-done | bytes 6176 | tf_op jit(solution)/shard_map/all_to_all | solution.py:54
  (195 shorter events, 24.6 us)
Async XLA Ops:
  0.6 177.3 %copy-start = (bf16[3,1,64,3,16,128]{5,4,3,2,1,0:T(8,128)(2,1)S(1)}, bf16[3,1,64,3,16,128]{5,4,3,2,1,0:T(8,128)(2,1)}, u32[]{:S(2)}) copy-start(bf16[3,1,64,3,16,128]{5,4,3,2,1,0:T(8,128)(2,1)} %param.9) | copy-start | bytes 7077892
  2.1 9.9 %all-to-all-start.1 = ((f32[4,3,1,16]{3,2,1,0:T(1,128)}), f32[4,3,1,16]{3,2,1,0:T(1,128)S(1)}, u32[]{:S(2)}, u32[]{:S(2)}) async-start(f32[4,3,1,16]{3,2,1,0:T(1,128)} %broadcast_in_dim.33), calls=%async_computation.1 | async-start | bytes 12288 | tf_op jit(solution)/shard_map/all_to_all | solution.py:25
  11.9 7.6 %all-to-all-start = ((f32[4,1,384]{2,1,0:T(1,128)}), f32[4,1,384]{2,1,0:T(1,128)S(1)}, u32[]{:S(2)}, u32[]{:S(2)}) async-start(f32[4,1,384]{2,1,0:T(1,128)} %reshape.114), calls=%async_computation | async-start | bytes 12288 | tf_op jit(solution)/shard_map/all_to_all | solution.py:25
  20.3 30.7 %all-to-all-start.5 = ((f32[64,3,1,16]{3,2,1,0:T(1,128)}), f32[64,3,1,16]{3,2,1,0:T(1,128)S(1)}, u32[]{:S(2)}, u32[]{:S(2)}) async-start(f32[64,3,1,16]{3,2,1,0:T(1,128)} %broadcast_in_dim.36), calls=%async_computation.5 | async-start | bytes 196608 | tf_op jit(solution)/shard_map/all_to_all | solution.py:25
  50.9 18.2 %all-to-all-start.2 = ((f32[64,1,768]{2,1,0:T(1,128)}), f32[64,1,768]{2,1,0:T(1,128)S(1)}, u32[]{:S(2)}, u32[]{:S(2)}) async-start(f32[64,1,768]{2,1,0:T(1,128)} %reshape.116), calls=%async_computation.2 | async-start | bytes 393216 | tf_op jit(solution)/shard_map/all_to_all | solution.py:25
  56.9 1.4 copy-start.2
  84.2 1.4 copy-start.1
  85.7 57.6 %copy-start.4 = (f32[64,3,1,16]{0,3,2,1:T(8,128)S(1)}, f32[64,3,1,16]{0,3,2,1:T(8,128)}, u32[]{:S(2)}) copy-start(f32[64,3,1,16]{0,3,2,1:T(8,128)} %copy.80) | copy-start | bytes 36868
  85.7 73.4 %copy-start.3 = (f32[4,3,2,64]{3,2,1,0:T(2,128)S(1)}, f32[4,3,2,64]{3,2,1,0:T(2,128)}, u32[]{:S(2)}) copy-start(f32[4,3,2,64]{3,2,1,0:T(2,128)} %copy-done.2) | copy-start | bytes 18436
  140.0 7.6 %all-to-all-start.7 = ((f32[4,3,1,16]{3,2,1,0:T(1,128)}), f32[4,3,1,16]{3,2,1,0:T(1,128)S(1)}, u32[]{:S(2)}, u32[]{:S(2)}) async-start(f32[4,3,1,16]{3,2,1,0:T(1,128)} %copy.82), calls=%async_computation.7 | async-start | bytes 12288 | tf_op jit(solution)/shard_map/all_to_all | solution.py:54
  147.6 5.7 %all-to-all-start.6 = ((f32[2,1,3072]{2,1,0:T(1,128)}), f32[2,1,3072]{2,1,0:T(1,128)S(1)}, u32[]{:S(2)}, u32[]{:S(2)}) async-start(f32[2,1,3072]{2,1,0:T(1,128)} %reshape.126), calls=%async_computation.6 | async-start | bytes 49152 | tf_op jit(solution)/shard_map/all_to_all | solution.py:25
  154.0 18.3 %all-to-all-start.8 = ((bf16[64,3,1,16]{3,1,2,0:T(4,128)(2,1)}), bf16[64,3,1,16]{3,1,2,0:T(4,128)(2,1)S(1)}, u32[]{:S(2)}, u32[]{:S(2)}) async-start(bf16[64,3,1,16]{3,1,2,0:T(4,128)(2,1)} %broadcast_in_dim.39), calls=%async_computation.8 | async-start | bytes 131072 | tf_op jit(solution)/shard_map/all_to_all | solution.py:25
  179.6 7.7 %all-to-all-start.10 = ((f32[4,3,1,16]{3,2,1,0:T(1,128)}), f32[4,3,1,16]{3,2,1,0:T(1,128)S(1)}, u32[]{:S(2)}, u32[]{:S(2)}) async-start(f32[4,3,1,16]{3,2,1,0:T(1,128)} %copy.86), calls=%async_computation.10 | async-start | bytes 12288 | tf_op jit(solution)/shard_map/all_to_all | solution.py:54
  187.9 17.9 %all-to-all-start.11 = ((f32[64,3,1,16]{3,2,1,0:T(1,128)}), f32[64,3,1,16]{3,2,1,0:T(1,128)S(1)}, u32[]{:S(2)}, u32[]{:S(2)}) async-start(f32[64,3,1,16]{3,2,1,0:T(1,128)} %broadcast_in_dim.84), calls=%async_computation.11 | async-start | bytes 196608 | tf_op jit(solution)/shard_map/all_to_all | solution.py:25
  212.1 11.0 %all-to-all-start.4 = ((f32[4,1,384]{2,1,0:T(1,128)}), f32[4,1,384]{2,1,0:T(1,128)S(1)}, u32[]{:S(2)}, u32[]{:S(2)}) async-start(f32[4,1,384]{2,1,0:T(1,128)} %reshape.120), calls=%async_computation.4 | async-start | bytes 12288 | tf_op jit(solution)/shard_map/all_to_all | solution.py:54
  223.1 8.9 %all-to-all-start.13 = ((f32[4,1,384]{2,1,0:T(1,128)}), f32[4,1,384]{2,1,0:T(1,128)S(1)}, u32[]{:S(2)}, u32[]{:S(2)}) async-start(f32[4,1,384]{2,1,0:T(1,128)} %reshape.128), calls=%async_computation.13 | async-start | bytes 12288 | tf_op jit(solution)/shard_map/all_to_all | solution.py:54
where the time goes:
time: 234 us; the launch traced here: 233 us
  waiting for transfers between devices  65 us (28%)
  other arithmetic  63.5 us (27%)
  starting transfers between devices  59.3 us (25%)
  local copies, waits for them, and re-layouts  21.3 us (9%)
  blocking collectives  20.3 us (9%)
    reduce_sum x17, other arithmetic, stokes_flow(): jnp.sum(diagonal_part * strength[0][None, :] + projection * delta_x, axis=1)  55.4 us
    all_to_all x7, waiting for transfers between devices, sent_to_all(): lax.all_to_all(jnp.broadcast_to(x[None], (length, *x.shape)), axis, 0, 0,...  53.9 us
    all_to_all x7, starting transfers between devices, sent_to_all(): lax.all_to_all(jnp.broadcast_to(x[None], (length, *x.shape)), axis, 0, 0,...  45 us
    all_to_all x3, blocking collectives, sent_to_all(): lax.all_to_all(jnp.broadcast_to(x[None], (length, *x.shape)), axis, 0, 0,...  20.3 us
    all_to_all x4, starting transfers between devices, sum_at_owner(): pieces = lax.all_to_all(split_up(x, dim, length), axis, 0, 0, tiled=True)  14.2 us
    all_to_all x4, waiting for transfers between devices, sum_at_owner(): pieces = lax.all_to_all(split_up(x, dim, length), axis, 0, 0, tiled=True)  11 us
    unnamed x33, local copies, waits for them, and re-layouts  8.94 us
    all_to_all x5, other arithmetic, sent_to_all(): lax.all_to_all(jnp.broadcast_to(x[None], (length, *x.shape)), axis, 0, 0,...  5.07 us
  transfers between devices with their start and end apart: 11, of which 10 were waited for; matrix products, arithmetic and copies ran while one was open for 8% of the time, Pallas kernels for 0%

commit v1 on v0

v1 whole, which is shorter than its diff:
```python
import math

import jax
import jax.numpy as jnp
from jax import lax
from jax.experimental import pallas as pl
from jax.experimental.pallas import tpu as pltpu
from jax.sharding import Mesh
from jax.sharding import PartitionSpec as P

AXES = ("tgt_0", "tgt_1", "tgt_2", "tgt_3", "src")
TGT = AXES[:4]
LINE = ("tgt_2", "tgt_3", "src")
PLANE = ("tgt_0", "tgt_1")
N_LINE = 16
N_PLANE = 32
SOURCES = N_PLANE * 128
SHELL_SOURCES = N_PLANE * 16
CHUNKS = 4
STEP = 512

F32 = jnp.float32
BF16 = jnp.bfloat16
scale = 20.0
mobility = scale / (8.0 * math.pi)


def three_parts(x):
    high = x.astype(BF16).astype(F32)
    rest = x - high
    middle = rest.astype(BF16).astype(F32)
    low = (rest - middle).astype(BF16).astype(F32)
    return high, middle, low


def left_rows(x):
    a, b, c = three_parts(x)
    return jnp.concatenate([a, a, b, b, a, c], axis=0).astype(BF16)


def right_rows(x):
    a, b, c = three_parts(x)
    return jnp.concatenate([a, b, a, b, c, a], axis=0).T.astype(BF16)


def rows_of(x):
    return lax.broadcasted_iota(jnp.int32, x.shape, 0)


def source_features(places, pushes):
    row = rows_of(places)
    places = jnp.where(row < 3, places * scale, 0.0)
    pushes = jnp.where(row < 3, pushes, 0.0)
    square = jnp.sum(places * places, axis=0, keepdims=True)
    along = jnp.sum(places * pushes, axis=0, keepdims=True)
    dist = jnp.where(row < 3, -2.0 * places, jnp.where(row == 3, 1.0, jnp.where(row == 4, square, 0.0)))
    proj = jnp.where(row == 4, -along, pushes)
    a, b, _ = three_parts(pushes)
    push_rows = jnp.concatenate([a, b], axis=0).astype(BF16)
    a, b, c = three_parts(jnp.where(row == 3, 1.0, places))
    place_rows = jnp.concatenate([a, b, c, jnp.zeros_like(a)], axis=0).astype(BF16)
    return right_rows(dist), right_rows(proj), push_rows, place_rows


def pair_sums(targets, count, dist_ref, proj_ref, push_ref, place_ref, unroll, fine):
    row = rows_of(targets)
    x = jnp.where(row < 3, targets * scale, 0.0)
    square = jnp.sum(x * x, axis=0, keepdims=True) + 1.0
    features = left_rows(jnp.where(row == 3, square, jnp.where(row == 4, 1.0, x)))
    width = targets.shape[1]
    step = min(STEP, count)

    def add_block(k, sums):
        diag_sum, proj_sum = sums
        part = pl.ds(pl.multiple_of(k * step, step), step)
        dist_sq = jnp.dot(dist_ref[part, :], features, preferred_element_type=F32)
        along = jnp.dot(proj_ref[part, :], features, preferred_element_type=F32)
        inv_root = lax.rsqrt(dist_sq)
        inv_cubed = inv_root * inv_root * inv_root
        diag = inv_root + inv_cubed
        high = diag.astype(BF16)
        low = (diag - high.astype(F32)).astype(BF16)
        diag_sum += jnp.dot(push_ref[:, part], high, preferred_element_type=F32)
        diag_sum += jnp.dot(push_ref[:, part], low, preferred_element_type=F32)
        proj = along * inv_cubed
        high = proj.astype(BF16)
        proj_sum += jnp.dot(place_ref[:, part], high, preferred_element_type=F32)
        if fine:
            low = (proj - high.astype(F32)).astype(BF16)
            proj_sum += jnp.dot(place_ref[:, part], low, preferred_element_type=F32)
        return diag_sum, proj_sum

    start = (jnp.zeros((16, width), F32), jnp.zeros((32, width), F32))
    diag_sum, proj_sum = lax.fori_loop(0, count // step, add_block, start, unroll=unroll)
    moved = proj_sum[0:8] + proj_sum[8:16] + proj_sum[16:24]
    return (diag_sum[0:8] + diag_sum[8:16] + x * moved[3:4] - moved) * mobility


def side_by_side(ref, first, count):
    return jnp.concatenate([ref[first + i] for i in range(count)], axis=1)


def packed(tiles, first_row):
    row = rows_of(tiles[0])
    lane = lax.broadcasted_iota(jnp.int32, tiles[0].shape, 1)
    keep = (row >= first_row) & (row < first_row + 3) & (lane < 16)
    blocks = []
    for start in range(0, len(tiles), 8):
        block = jnp.zeros_like(tiles[0])
        for i, tile in enumerate(tiles[start : start + 8]):
            piece = jnp.where(keep, tile, 0.0)
            block += pltpu.roll(piece, 16 * i, 1) if i else piece
        blocks.append(pltpu.roll(block, 8 - first_row, 0) if first_row else block)
    return jnp.concatenate(blocks, axis=1)


def own_kernel(fibre_ref, shell_ref, line_ref, plane_ref):
    fibre = jnp.concatenate([fibre_ref[:, 0, :], fibre_ref[:, 1, :]], axis=1)
    shell = jnp.concatenate([shell_ref[:, 0, :], jnp.zeros((3, 112), F32)], axis=1)
    tile = jnp.concatenate([fibre, shell, jnp.zeros((2, 128), F32)], axis=0)
    line_ref[...] = jnp.broadcast_to(tile[None], line_ref.shape)
    plane_ref[...] = jnp.broadcast_to(tile[None], plane_ref.shape)


def shell_kernel(line_ref, plane_ref, bending_ref, part_ref, dist_ref, proj_ref, push_ref, place_ref, shell_ref):
    square = bending_ref[...]
    zero = jnp.zeros_like(square)
    both = jnp.concatenate(
        [jnp.concatenate([square, zero], axis=1), jnp.concatenate([zero, square], axis=1)], axis=0
    )
    places = plane_ref[...].reshape(N_PLANE * 8, 128)
    pushes = -lax.dot_general(
        places, both, (((1,), (1,)), ((), ())), precision=lax.Precision.HIGHEST, preferred_element_type=F32
    )
    pushes = jnp.concatenate([pushes[8 * i : 8 * i + 8] for i in range(N_PLANE)], axis=1)
    places = side_by_side(plane_ref, 0, N_PLANE)
    dist_ref[...], proj_ref[...], push_ref[...], place_ref[...] = source_features(places, pushes)
    shell_ref[...] = packed([plane_ref[i] for i in range(N_PLANE)], 3)
    order = [pair * 4 + src for src in range(4) for pair in range(4)]
    targets = packed([line_ref[i] for i in order], 3)
    flow = pair_sums(targets, SOURCES, dist_ref, proj_ref, push_ref, place_ref, 4, True)
    for src in range(4):
        half = flow[:, 128 * (src // 2) : 128 * (src // 2) + 128]
        piece = pltpu.roll(half, 64, 1) if src % 2 else half
        for pair in range(4):
            part_ref[pair * 4 + src] = piece


def fibre_kernel(line_ref, dist_ref, proj_ref, push_ref, place_ref, flow_ref):
    count = N_LINE // CHUNKS
    flow = pair_sums(
        side_by_side(line_ref, 0, count), SOURCES, dist_ref, proj_ref, push_ref, place_ref, 4, False
    )
    for i in range(count):
        flow_ref[i] = flow[:, 128 * i : 128 * i + 128]


def sum_kernel(parts_ref, out_ref):
    total = parts_ref[0]
    for i in range(1, parts_ref.shape[0]):
        total += parts_ref[i]
    out_ref[...] = jnp.broadcast_to(total[None], out_ref.shape)


def back_kernel(line_ref, shell_ref, density_ref, *refs):
    flows, (part_ref, dist_ref, proj_ref, push_ref, place_ref) = refs[:CHUNKS], refs[CHUNKS:]
    pushes = packed([density_ref[i] for i in range(N_PLANE)], 0)
    dist_ref[...], proj_ref[...], push_ref[...], place_ref[...] = source_features(shell_ref[...], pushes)
    count = N_LINE // CHUNKS
    for chunk in range(CHUNKS):
        flow = pair_sums(
            side_by_side(line_ref, chunk * count, count),
            SHELL_SOURCES,
            dist_ref,
            proj_ref,
            push_ref,
            place_ref,
            1,
            False,
        )
        for i in range(count):
            part_ref[chunk * count + i] = flow[:, 128 * i : 128 * i + 128] + flows[chunk][i]


def tiles(count):
    return jax.ShapeDtypeStruct((count, 8, 128), F32)


def cost(pairs):
    return pl.CostEstimate(flops=pairs * 400, bytes_accessed=1 << 20, transcendentals=pairs)


def params():
    return pltpu.CompilerParams(vmem_limit_bytes=24 << 20)


def feature_shapes(count):
    return [((count, 48), BF16), ((count, 48), BF16), ((16, count), BF16), ((32, count), BF16)]


def exchange(x, axes):
    return lax.all_to_all(x, axes, 0, 0, tiled=True)


def per_device(fibre_points, shell_points, bending, shell_inverse):
    own_line, own_plane = pl.pallas_call(own_kernel, out_shape=[tiles(N_LINE), tiles(N_PLANE)])(
        fibre_points, shell_points
    )
    plane = exchange(own_plane, PLANE)
    line = exchange(own_line, LINE)
    features = [jax.ShapeDtypeStruct(s, t) for s, t in feature_shapes(SOURCES)]
    shell_part, *features, shell_places = pl.pallas_call(
        shell_kernel,
        out_shape=[tiles(N_LINE), *features, jax.ShapeDtypeStruct((8, SHELL_SOURCES), F32)],
        compiler_params=params(),
        cost_estimate=cost(256 * SOURCES),
    )(line, plane, bending)
    count = N_LINE // CHUNKS

    def fibre_chunk(chunk, after):
        held, _ = lax.optimization_barrier((line, after))
        return pl.pallas_call(
            fibre_kernel,
            out_shape=tiles(count),
            grid=(1,),
            in_specs=[pl.BlockSpec((count, 8, 128), lambda i: (chunk, 0, 0))]
            + [pl.BlockSpec(s, lambda i: (0, 0)) for s, _ in feature_shapes(SOURCES)],
            out_specs=pl.BlockSpec((count, 8, 128), lambda i: (0, 0, 0)),
            compiler_params=params(),
            cost_estimate=cost(count * 128 * SOURCES),
        )(held, *features)

    flows = []

    def exchange_beside(x, axes):
        flow = fibre_chunk(len(flows), x)
        x, flow = lax.optimization_barrier((exchange(x, axes), flow))
        flows.append(flow)
        return x

    shell_parts = exchange_beside(shell_part, LINE)
    shell_own = pl.pallas_call(sum_kernel, out_shape=tiles(N_PLANE))(shell_parts)
    shell_all = exchange_beside(shell_own, PLANE)
    columns = shell_all[:, :3, :64].astype(BF16).reshape(N_PLANE, 3, 4, 16)
    columns = columns.transpose(1, 3, 0, 2).reshape(3, 16, 128)
    density_rows = -jnp.einsum(
        "xaqcbn,cbn->xaq", shell_inverse, columns, preferred_element_type=F32
    )
    pieces = density_rows.reshape(3, 4, 16).transpose(1, 0, 2)
    pieces = jnp.pad(pieces, ((0, 0), (0, 5), (0, 112)))
    density_own = pl.pallas_call(sum_kernel, out_shape=tiles(N_PLANE))(exchange_beside(pieces, "src"))
    density = density_own[0, :3, None, :16]
    density_all = exchange_beside(density_own, PLANE)
    part = pl.pallas_call(
        back_kernel,
        out_shape=tiles(N_LINE),
        scratch_shapes=[pltpu.VMEM(s, t) for s, t in feature_shapes(SHELL_SOURCES)],
        compiler_params=params(),
        cost_estimate=cost(N_LINE * 128 * SHELL_SOURCES),
    )(line, shell_places, density_all, *flows)
    velocity = jnp.sum(exchange(part, LINE)[:, :3], axis=0)
    return velocity.reshape(3, 2, 64), density


def solution(mesh):
    torus = Mesh(mesh.devices.reshape(4, 8, 2, 2, mesh.shape["src"]), AXES)
    in_specs = (P(None, AXES, None), P(None, TGT, "src"), P(), P(None, TGT, None, None, "src", None))
    out_specs = (P(None, AXES, None), P(None, TGT, "src"))
    return jax.shard_map(per_device, mesh=torus, in_specs=in_specs, out_specs=out_specs, check_vma=False)
```

time: 234 us -> 130 us (0.56)
  other arithmetic: 63.5 us -> 1.55 us
  waiting for transfers between devices: 65 us -> 10.4 us
  Pallas kernels: 0 us -> 31.1 us
  starting transfers between devices: 59.3 us -> 29.2 us
  blocking collectives: 20.3 us -> 38.2 us
  local copies, waits for them, and re-layouts: 21.3 us -> 16.7 us
    reduce_sum x21 -> x1, other arithmetic: 55.4 us -> 0.02 us  [per_device(): velocity = jnp.sum(exchange(part, LINE)[:, :3], axis=0)]
    all_to_all x11 -> x5, waiting for transfers between devices: 65 us -> 10.4 us  [exchange(): return lax.all_to_all(x, axes, 0, 0, tiled=True)]
    pallas_call x0 -> x9, Pallas kernels: none -> 31.1 us  [the longest x4 18.7 us: fibre_chunk(): pl.pallas_call(fibre_kernel, out_shape=tiles(count), grid=(1,), in_specs=...]
    all_to_all x11 -> x5, starting transfers between devices: 59.3 us -> 29.2 us  [exchange(): return lax.all_to_all(x, axes, 0, 0, tiled=True)]
    all_to_all x3 -> x2, blocking collectives: 20.3 us -> 38.2 us  [exchange(): return lax.all_to_all(x, axes, 0, 0, tiled=True)]
    all_to_all x7 -> x0, other arithmetic: 6.42 us -> none  [the longest x5 5.07 us: sent_to_all(): lax.all_to_all(jnp.broadcast_to(x[None], (length, *x.shape)), axis, 0, 0,...]
    unnamed x33 -> x28, local copies, waits for them, and re-layouts: 8.94 us -> 13.7 us
    broadcast_in_dim x6 -> x0, local copies, waits for them, and re-layouts: 3.39 us -> none  [sent_to_all(): jnp.broadcast_to(x[None], (length, *x.shape))]
  transfers between devices with their start and end apart: 11 -> 5, of which waited for: 10 -> 4; matrix products, arithmetic and copies ran while one was open for 8% -> 1% of each run, Pallas kernels for 0% -> 15%
where the time goes in v1:
time: 130 us; the launch traced here: 129 us
  blocking collectives  38.2 us (29%)
  Pallas kernels  31.1 us (24%)
  starting transfers between devices  29.2 us (22%)
  local copies, waits for them, and re-layouts  16.7 us (13%)
  waiting for transfers between devices  10.4 us (8%)
  other arithmetic  1.55 us (1%)
    all_to_all x2, blocking collectives, exchange(): return lax.all_to_all(x, axes, 0, 0, tiled=True)  38.2 us
    all_to_all x5, starting transfers between devices, exchange(): return lax.all_to_all(x, axes, 0, 0, tiled=True)  29.2 us
    pallas_call x4, Pallas kernels, fibre_chunk(): pl.pallas_call(fibre_kernel, out_shape=tiles(count), grid=(1,), in_specs=...  18.7 us
    unnamed x28, local copies, waits for them, and re-layouts  13.7 us
    all_to_all x5, waiting for transfers between devices, exchange(): return lax.all_to_all(x, axes, 0, 0, tiled=True)  10.4 us
    pallas_call x1, Pallas kernels, per_device(): pl.pallas_call(shell_kernel, out_shape=[tiles(N_LINE), *features, jax.Sha...  4.64 us
    pallas_call x1, Pallas kernels, per_device(): pl.pallas_call(back_kernel, out_shape=tiles(N_LINE), scratch_shapes=[pltp...  3.32 us
  transfers between devices with their start and end apart: 5, of which 4 were waited for; matrix products, arithmetic and copies ran while one was open for 1% of the time, Pallas kernels for 15%

profile of v1, /device:TPU:1, one launch (start us, length us, event | category | flops | bytes accessed | tf_op | source)
XLA Modules:
  0.0 128.9 jit_solution(13632725192494027036)
XLA Ops:
  0.6 0.0 copy-start
  0.6 1.6 %shard_map.59 = (f32[16,8,128]{2,1,0:T(8,128)}, f32[32,8,128]{2,1,0:T(8,128)}) custom-call(f32[3,2,64]{2,1,0:T(2,128)} %fibre_ref.1, f32[3,1,16]{2,1,0:T(1,128)} %shell_ref.1), custom_call_target="tpu_custom_call" | custom-call | tf_op jit(solution)/shard_map/pallas_call | solution.py:206
  2.2 17.8 %all_to_all.35.line_ref = f32[16,8,128]{2,1,0:T(8,128)S(1)} all-to-all(f32[16,8,128]{2,1,0:T(8,128)} %get-tuple-element.22), channel_id=1, replica_groups=mesh['tgt_0'=4,'tgt_1'=8,'tgt_2'=2,'tgt_3'=2,'src'=4] {'tgt_2','tgt_3','..., dimensions={0} | all-to-all | bytes 131072 | tf_op jit(solution)/shard_map/all_to_all | solution.py:202
  20.0 20.5 %all_to_all.36.plane_ref = f32[32,8,128]{2,1,0:T(8,128)S(1)} all-to-all(f32[32,8,128]{2,1,0:T(8,128)} %get-tuple-element.23), channel_id=1, replica_groups=mesh['tgt_0'=4,'tgt_1'=8,'tgt_2'=2,'tgt_3'=2,'src'=4] {'tgt_0','tgt_1'}, dimensions={0} | all-to-all | bytes 262144 | tf_op jit(solution)/shard_map/all_to_all | solution.py:202
  40.5 0.8 copy-done.1
  41.2 4.6 %shard_map.60 = (f32[16,8,128]{2,1,0:T(8,128)}, bf16[4096,48]{1,0:T(8,128)(2,1)S(1)}, bf16[4096,48]{1,0:T(8,128)(2,1)S(1)}, bf16[16,4096]{1,0:T(8,128)(2,1)S(1)}...) custom-call(f32[16,8,128]{2,1,0:T(8,128)S(1)} %all_to_all.35.line_ref, f32[32,8,128]{2,1,0:T(8,128)S(1)} %all_to_all.36.plane_ref, ...), custom_call_target="tpu_custom_call" | custom-call | flops 419430400 | bytes 1048576 | tf_op jit(solution)/shard_map/pallas_call | solution.py:212
  45.9 1.0 copy-done.2
  46.9 1.0 copy-done.7
  47.8 5.4 %all-to-all-start.2 = ((f32[16,8,128]{2,1,0:T(8,128)}), f32[16,8,128]{2,1,0:T(8,128)S(1)}, u32[]{:S(2)}, u32[]{:S(2)}) async-start(f32[16,8,128]{2,1,0:T(8,128)} %get-tuple-element.25), calls=%async_computation.2 | async-start | bytes 131072 | tf_op jit(solution)/shard_map/all_to_all | solution.py:202
  53.2 1.2 copy-done.3
  54.5 1.2 copy-done.8
  55.7 4.7 %shard_map.61.refs_0_ = f32[4,8,128]{2,1,0:T(8,128)S(1)} custom-call(f32[16,8,128]{2,1,0:T(8,128)S(1)} %all_to_all.35.line_ref, bf16[4096,48]{1,0:T(8,128)(2,1)S(1)} %copy-done.3, bf16[4096,48]{1,0:T(8,128)(2,1)S(1)} %copy-done.8, bf16[16,4096]{1,0:T(8,128)(2,1)S(1)} %get-tuple-element.29.push_ref, bf16[32,4096]{1,0:T(8,128)(2,1)S(1)} %get-tuple-element.30.place_ref), custom_call_target="tpu_custom_call" | custom-call | flops 838860800 | bytes 1048576 | tf_op jit(solution)/shard_map/pallas_call | solution.py:222
  60.4 0.5 all-to-all-done.2.parts_ref
  60.8 0.6 copy-done.12
  61.4 1.5 %shard_map.62 = f32[32,8,128]{2,1,0:T(8,128)} custom-call(f32[16,8,128]{2,1,0:T(8,128)} %copy-done.12), custom_call_target="tpu_custom_call" | custom-call | tf_op jit(solution)/shard_map/pallas_call | solution.py:242
  63.0 1.5 %convert.5 = bf16[32,8,128]{2,1,0:T(8,128)(2,1)} convert(f32[32,8,128]{2,1,0:T(8,128)} %shard_map.62) | non-fusion elementwise | flops 32768 | bytes 196608
  64.5 3.8 %all-to-all-start.3 = ((bf16[32,8,128]{2,1,0:T(8,128)(2,1)}), bf16[32,8,128]{2,1,0:T(8,128)(2,1)S(1)}, u32[]{:S(2)}, u32[]{:S(2)}) async-start(bf16[32,8,128]{2,1,0:T(8,128)(2,1)} %convert.5), calls=%async_computation.3 | async-start | bytes 131072 | tf_op jit(solution)/shard_map/all_to_all | solution.py:202
  68.3 0.0 copy-start.4
  68.3 1.2 copy-done.4
  69.6 1.2 copy-done.9
  70.8 4.7 %shard_map.63.refs_1_ = f32[4,8,128]{2,1,0:T(8,128)S(1)} custom-call(f32[16,8,128]{2,1,0:T(8,128)S(1)} %all_to_all.35.line_ref, bf16[4096,48]{1,0:T(8,128)(2,1)S(1)} %copy-done.4, bf16[4096,48]{1,0:T(8,128)(2,1)S(1)} %copy-done.9, bf16[16,4096]{1,0:T(8,128)(2,1)S(1)} %get-tuple-element.29.push_ref, bf16[32,4096]{1,0:T(8,128)(2,1)S(1)} %get-tuple-element.30.place_ref), custom_call_target="tpu_custom_call" | custom-call | flops 838860800 | bytes 1048576 | tf_op jit(solution)/shard_map/pallas_call | solution.py:222
  75.5 1.7 %all-to-all-done.3 = bf16[32,8,128]{2,1,0:T(8,128)(2,1)S(1)} async-done(((bf16[32,8,128]{2,1,0:T(8,128)(2,1)}), bf16[32,8,128]{2,1,0:T(8,128)(2,1)S(1)}, u32[]{:S(2)}, u32[]{:S(2)}) %all-to-all-start.3) | async-done | bytes 65568 | tf_op jit(solution)/shard_map/all_to_all | solution.py:202
  77.2 0.1 copy.6
  77.3 0.1 copy.7
  77.5 0.1 copy.9
  77.6 0.0 copy-done
  77.6 0.9 fusion
  78.5 0.1 reshape.25
  78.6 0.6 pad.4
  79.2 4.0 %all-to-all-start.4 = ((f32[4,8,128]{2,1,0:T(8,128)}), f32[4,8,128]{2,1,0:T(8,128)S(1)}, u32[]{:S(2)}, u32[]{:S(2)}) async-start(f32[4,8,128]{2,1,0:T(8,128)} %pad.4), calls=%async_computation.4 | async-start | bytes 32768 | tf_op jit(solution)/shard_map/all_to_all | solution.py:202
  83.2 1.2 copy-done.5
  84.5 1.2 copy-done.10
  85.7 4.7 %shard_map.64.refs_2_ = f32[4,8,128]{2,1,0:T(8,128)S(1)} custom-call(f32[16,8,128]{2,1,0:T(8,128)S(1)} %all_to_all.35.line_ref, bf16[4096,48]{1,0:T(8,128)(2,1)S(1)} %copy-done.5, bf16[4096,48]{1,0:T(8,128)(2,1)S(1)} %copy-done.10, bf16[16,4096]{1,0:T(8,128)(2,1)S(1)} %get-tuple-element.29.push_ref, bf16[32,4096]{1,0:T(8,128)(2,1)S(1)} %get-tuple-element.30.place_ref), custom_call_target="tpu_custom_call" | custom-call | flops 838860800 | bytes 1048576 | tf_op jit(solution)/shard_map/pallas_call | solution.py:222
  90.4 0.0 all-to-all-done.4.parts_ref
  90.4 0.0 copy-start.13
  90.4 0.6 copy-done.13
  91.0 1.4 %shard_map.65 = f32[32,8,128]{2,1,0:T(8,128)} custom-call(f32[4,8,128]{2,1,0:T(8,128)} %copy-done.13), custom_call_target="tpu_custom_call" | custom-call | tf_op jit(solution)/shard_map/pallas_call | solution.py:251
  92.4 7.7 %all-to-all-start.5 = ((f32[32,8,128]{2,1,0:T(8,128)}), f32[32,8,128]{2,1,0:T(8,128)S(1)}, u32[]{:S(2)}, u32[]{:S(2)}) async-start(f32[32,8,128]{2,1,0:T(8,128)} %shard_map.65), calls=%async_computation.5 | async-start | bytes 262144 | tf_op jit(solution)/shard_map/all_to_all | solution.py:202
  100.1 1.2 copy-done.6
  101.3 1.2 copy-done.11
  102.5 4.7 %shard_map.66.refs_3_ = f32[4,8,128]{2,1,0:T(8,128)S(1)} custom-call(f32[16,8,128]{2,1,0:T(8,128)S(1)} %all_to_all.35.line_ref, bf16[4096,48]{1,0:T(8,128)(2,1)S(1)} %copy-done.6, bf16[4096,48]{1,0:T(8,128)(2,1)S(1)} %copy-done.11, bf16[16,4096]{1,0:T(8,128)(2,1)S(1)} %get-tuple-element.29.push_ref, bf16[32,4096]{1,0:T(8,128)(2,1)S(1)} %get-tuple-element.30.place_ref), custom_call_target="tpu_custom_call" | custom-call | flops 838860800 | bytes 1048576 | tf_op jit(solution)/shard_map/pallas_call | solution.py:222
  107.2 1.8 %all-to-all-done.5.density_ref = f32[32,8,128]{2,1,0:T(8,128)S(1)} async-done(((f32[32,8,128]{2,1,0:T(8,128)}), f32[32,8,128]{2,1,0:T(8,128)S(1)}, u32[]{:S(2)}, u32[]{:S(2)}) %all-to-all-start.5) | async-done | bytes 131104 | tf_op jit(solution)/shard_map/all_to_all | solution.py:202
  109.0 3.3 %shard_map.67 = f32[16,8,128]{2,1,0:T(8,128)} custom-call(f32[16,8,128]{2,1,0:T(8,128)S(1)} %all_to_all.35.line_ref, f32[8,512]{1,0:T(8,128)S(1)} %get-tuple-element.24.shell_ref, f32[32,8,128]{2,1,0:T(8,128)S(1)} %all-to-all-done.5.density_ref, f32[4,8,128]{2,1,0:T(8,128)S(1)} %shard_map.61.refs_0_, f32[4,8,128]{2,1,0:T(8,128)S(1)} %shard_map.63.refs_1_, ...), custom_call_target="tpu_custom_call" | custom-call | flops 419430400 | bytes 1048576 | tf_op jit(solution)/shard_map/pallas_call | solution.py:254
  112.3 8.3 %all-to-all-start.6 = ((f32[16,8,128]{2,1,0:T(8,128)}), f32[16,8,128]{2,1,0:T(8,128)S(1)}, u32[]{:S(2)}, u32[]{:S(2)}) async-start(f32[16,8,128]{2,1,0:T(8,128)} %shard_map.67), calls=%async_computation.6 | async-start | bytes 131072 | tf_op jit(solution)/shard_map/all_to_all | solution.py:202
  120.6 0.7 slice.15
  121.3 0.6 broadcast_in_dim_squeeze.3
  121.9 6.3 %all-to-all-done.6 = f32[16,8,128]{2,1,0:T(8,128)S(1)} async-done(((f32[16,8,128]{2,1,0:T(8,128)}), f32[16,8,128]{2,1,0:T(8,128)S(1)}, u32[]{:S(2)}, u32[]{:S(2)}) %all-to-all-start.6) | async-done | bytes 65568 | tf_op jit(solution)/shard_map/all_to_all | solution.py:202
  128.2 0.7 reshape.26
  (15 shorter events, 0.1 us)
Async XLA Ops:
  0.6 76.9 %copy-start = (bf16[3,1,64,3,16,128]{5,4,3,2,1,0:T(8,128)(2,1)S(1)}, bf16[3,1,64,3,16,128]{5,4,3,2,1,0:T(8,128)(2,1)}, u32[]{:S(2)}) copy-start(bf16[3,1,64,3,16,128]{5,4,3,2,1,0:T(8,128)(2,1)} %param.7) | copy-start | bytes 7077892
  40.5 0.8 copy-start.1
  45.9 1.0 copy-start.2
  46.9 1.0 copy-start.7
  47.8 13.0 %all-to-all-start.2 = ((f32[16,8,128]{2,1,0:T(8,128)}), f32[16,8,128]{2,1,0:T(8,128)S(1)}, u32[]{:S(2)}, u32[]{:S(2)}) async-start(f32[16,8,128]{2,1,0:T(8,128)} %get-tuple-element.25), calls=%async_computation.2 | async-start | bytes 131072 | tf_op jit(solution)/shard_map/all_to_all | solution.py:202
  53.2 1.2 copy-start.3
  54.5 1.2 copy-start.8
  60.8 0.6 copy-start.12
  64.5 12.7 %all-to-all-start.3 = ((bf16[32,8,128]{2,1,0:T(8,128)(2,1)}), bf16[32,8,128]{2,1,0:T(8,128)(2,1)S(1)}, u32[]{:S(2)}, u32[]{:S(2)}) async-start(bf16[32,8,128]{2,1,0:T(8,128)(2,1)} %convert.5), calls=%async_computation.3 | async-start | bytes 131072 | tf_op jit(solution)/shard_map/all_to_all | solution.py:202
  68.3 1.2 copy-start.4
  69.6 1.2 copy-start.9
  79.2 11.1 %all-to-all-start.4 = ((f32[4,8,128]{2,1,0:T(8,128)}), f32[4,8,128]{2,1,0:T(8,128)S(1)}, u32[]{:S(2)}, u32[]{:S(2)}) async-start(f32[4,8,128]{2,1,0:T(8,128)} %pad.4), calls=%async_computation.4 | async-start | bytes 32768 | tf_op jit(solution)/shard_map/all_to_all | solution.py:202
  83.2 1.2 copy-start.5
  84.5 1.2 copy-start.10
  90.4 0.6 copy-start.13
  92.4 16.7 %all-to-all-start.5 = ((f32[32,8,128]{2,1,0:T(8,128)}), f32[32,8,128]{2,1,0:T(8,128)S(1)}, u32[]{:S(2)}, u32[]{:S(2)}) async-start(f32[32,8,128]{2,1,0:T(8,128)} %shard_map.65), calls=%async_computation.5 | async-start | bytes 262144 | tf_op jit(solution)/shard_map/all_to_all | solution.py:202
  100.0 1.2 copy-start.6
  101.3 1.2 copy-start.11
  112.3 15.9 %all-to-all-start.6 = ((f32[16,8,128]{2,1,0:T(8,128)}), f32[16,8,128]{2,1,0:T(8,128)S(1)}, u32[]{:S(2)}, u32[]{:S(2)}) async-start(f32[16,8,128]{2,1,0:T(8,128)} %shard_map.67), calls=%async_computation.6 | async-start | bytes 131072 | tf_op jit(solution)/shard_map/all_to_all | solution.py:202

commit v2 on v1

--- a/solution.py
+++ b/solution.py
@@ -18,6 +18,7 @@
 SHELL_SOURCES = N_PLANE * 16
 CHUNKS = 4
 STEP = 512
+ROWS = (((0,), (0,)), ((), ()))
 
 F32 = jnp.float32
 BF16 = jnp.bfloat16
@@ -33,18 +34,26 @@
     return high, middle, low
 
 
-def left_rows(x):
-    a, b, c = three_parts(x)
-    return jnp.concatenate([a, a, b, b, a, c], axis=0).astype(BF16)
-
-
-def right_rows(x):
-    a, b, c = three_parts(x)
-    return jnp.concatenate([a, b, a, b, c, a], axis=0).T.astype(BF16)
-
-
 def rows_of(x):
     return lax.broadcasted_iota(jnp.int32, x.shape, 0)
+
+
+def left_rows(x, level):
+    row = rows_of(x)
+    a, b, c = three_parts(x)
+    p, q, r = three_parts(level)
+    first = jnp.where(row < 3, a, jnp.where(row == 3, p, jnp.where(row == 4, q, jnp.where(row == 5, r, 1.0))))
+    second = jnp.where(row < 3, a, jnp.where(row == 3, 1.0, pltpu.roll(b, 4, 0)))
+    return jnp.concatenate([first, second, b + pltpu.roll(a, 4, 0), c], axis=0).astype(BF16)
+
+
+def right_rows(x, ones, level):
+    row = rows_of(x)
+    a, b, c = three_parts(x)
+    p, q, r = three_parts(level)
+    first = jnp.where(row < 3, a, jnp.where(row < 6, ones, jnp.where(row == 6, p, q)))
+    second = jnp.where(row < 3, b, jnp.where(row == 3, r, pltpu.roll(a, 4, 0)))
+    return jnp.concatenate([first, second, b + pltpu.roll(c, 4, 0), a], axis=0).astype(BF16)
 
 
 def source_features(places, pushes):
@@ -53,28 +62,26 @@
     pushes = jnp.where(row < 3, pushes, 0.0)
     square = jnp.sum(places * places, axis=0, keepdims=True)
     along = jnp.sum(places * pushes, axis=0, keepdims=True)
-    dist = jnp.where(row < 3, -2.0 * places, jnp.where(row == 3, 1.0, jnp.where(row == 4, square, 0.0)))
-    proj = jnp.where(row == 4, -along, pushes)
     a, b, _ = three_parts(pushes)
     push_rows = jnp.concatenate([a, b], axis=0).astype(BF16)
     a, b, c = three_parts(jnp.where(row == 3, 1.0, places))
-    place_rows = jnp.concatenate([a, b, c, jnp.zeros_like(a)], axis=0).astype(BF16)
-    return right_rows(dist), right_rows(proj), push_rows, place_rows
+    place_rows = jnp.concatenate([a, b + pltpu.roll(c, 4, 0)], axis=0).astype(BF16)
+    return right_rows(-2.0 * places, 1.0, square), right_rows(pushes, 0.0, -along), push_rows, place_rows
 
 
 def pair_sums(targets, count, dist_ref, proj_ref, push_ref, place_ref, unroll, fine):
     row = rows_of(targets)
     x = jnp.where(row < 3, targets * scale, 0.0)
     square = jnp.sum(x * x, axis=0, keepdims=True) + 1.0
-    features = left_rows(jnp.where(row == 3, square, jnp.where(row == 4, 1.0, x)))
+    features = left_rows(x, square)
     width = targets.shape[1]
     step = min(STEP, count)
 
     def add_block(k, sums):
         diag_sum, proj_sum = sums
         part = pl.ds(pl.multiple_of(k * step, step), step)
-        dist_sq = jnp.dot(dist_ref[part, :], features, preferred_element_type=F32)
-        along = jnp.dot(proj_ref[part, :], features, preferred_element_type=F32)
+        dist_sq = lax.dot_general(dist_ref[:, part], features, ROWS, preferred_element_type=F32)
+        along = lax.dot_general(proj_ref[:, part], features, ROWS, preferred_element_type=F32)
         inv_root = lax.rsqrt(dist_sq)
         inv_cubed = inv_root * inv_root * inv_root
         diag = inv_root + inv_cubed
@@ -90,9 +97,10 @@
             proj_sum += jnp.dot(place_ref[:, part], low, preferred_element_type=F32)
         return diag_sum, proj_sum
 
-    start = (jnp.zeros((16, width), F32), jnp.zeros((32, width), F32))
+    start = (jnp.zeros((16, width), F32), jnp.zeros((16, width), F32))
     diag_sum, proj_sum = lax.fori_loop(0, count // step, add_block, start, unroll=unroll)
-    moved = proj_sum[0:8] + proj_sum[8:16] + proj_sum[16:24]
+    rest = proj_sum[8:16]
+    moved = proj_sum[0:8] + rest + pltpu.roll(rest, 4, 0)
     return (diag_sum[0:8] + diag_sum[8:16] + x * moved[3:4] - moved) * mobility
 
 
@@ -122,7 +130,7 @@
     plane_ref[...] = jnp.broadcast_to(tile[None], plane_ref.shape)
 
 
-def shell_kernel(line_ref, plane_ref, bending_ref, part_ref, dist_ref, proj_ref, push_ref, place_ref, shell_ref):
+def source_kernel(plane_ref, bending_ref, dist_ref, proj_ref, push_ref, place_ref, shell_ref):
     square = bending_ref[...]
     zero = jnp.zeros_like(square)
     both = jnp.concatenate(
@@ -136,6 +144,9 @@
     places = side_by_side(plane_ref, 0, N_PLANE)
     dist_ref[...], proj_ref[...], push_ref[...], place_ref[...] = source_features(places, pushes)
     shell_ref[...] = packed([plane_ref[i] for i in range(N_PLANE)], 3)
+
+
+def shell_kernel(line_ref, dist_ref, proj_ref, push_ref, place_ref, part_ref):
     order = [pair * 4 + src for src in range(4) for pair in range(4)]
     targets = packed([line_ref[i] for i in order], 3)
     flow = pair_sums(targets, SOURCES, dist_ref, proj_ref, push_ref, place_ref, 4, True)
@@ -155,11 +166,29 @@
         flow_ref[i] = flow[:, 128 * i : 128 * i + 128]
 
 
-def sum_kernel(parts_ref, out_ref):
+def total_of(parts_ref):
     total = parts_ref[0]
     for i in range(1, parts_ref.shape[0]):
         total += parts_ref[i]
+    return total
+
+
+def columns_kernel(parts_ref, out_ref):
+    total = total_of(parts_ref)
+    total = jnp.concatenate([total, jnp.zeros_like(total)], axis=0).astype(BF16)
     out_ref[...] = jnp.broadcast_to(total[None], out_ref.shape)
+
+
+def density_kernel(parts_ref, out_ref, density_ref):
+    total = total_of(parts_ref)
+    out_ref[...] = jnp.broadcast_to(total[None], out_ref.shape)
+    density_ref[:, 0, :] = total[0:3, 0:16]
+
+
+def velocity_kernel(parts_ref, out_ref):
+    total = total_of(parts_ref)
+    out_ref[:, 0, :] = total[0:3, 0:64]
+    out_ref[:, 1, :] = total[0:3, 64:128]
 
 
 def back_kernel(line_ref, shell_ref, density_ref, *refs):
@@ -190,12 +219,12 @@
     return pl.CostEstimate(flops=pairs * 400, bytes_accessed=1 << 20, transcendentals=pairs)
 
 
-def params():
-    return pltpu.CompilerParams(vmem_limit_bytes=24 << 20)
+def params(mib):
+    return pltpu.CompilerParams(vmem_limit_bytes=mib << 20)
 
 
 def feature_shapes(count):
-    return [((count, 48), BF16), ((count, 48), BF16), ((16, count), BF16), ((32, count), BF16)]
+    return [((32, count), BF16), ((32, count), BF16), ((16, count), BF16), ((16, count), BF16)]
 
 
 def exchange(x, axes):
@@ -203,18 +232,25 @@
 
 
 def per_device(fibre_points, shell_points, bending, shell_inverse):
-    own_line, own_plane = pl.pallas_call(own_kernel, out_shape=[tiles(N_LINE), tiles(N_PLANE)])(
-        fibre_points, shell_points
-    )
+    own_line, own_plane = pl.pallas_call(
+        own_kernel, out_shape=[tiles(N_LINE), tiles(N_PLANE)], compiler_params=params(2)
+    )(fibre_points, shell_points)
     plane = exchange(own_plane, PLANE)
-    line = exchange(own_line, LINE)
+    own_line, _ = lax.optimization_barrier((own_line, plane))
     features = [jax.ShapeDtypeStruct(s, t) for s, t in feature_shapes(SOURCES)]
-    shell_part, *features, shell_places = pl.pallas_call(
+    *features, shell_places = pl.pallas_call(
+        source_kernel,
+        out_shape=[*features, jax.ShapeDtypeStruct((8, SHELL_SOURCES), F32)],
+        compiler_params=params(24),
+        cost_estimate=cost(64 * SOURCES),
+    )(plane, bending)
+    line, features = lax.optimization_barrier((exchange(own_line, LINE), features))
+    shell_part = pl.pallas_call(
         shell_kernel,
-        out_shape=[tiles(N_LINE), *features, jax.ShapeDtypeStruct((8, SHELL_SOURCES), F32)],
-        compiler_params=params(),
+        out_shape=tiles(N_LINE),
+        compiler_params=params(24),
         cost_estimate=cost(256 * SOURCES),
-    )(line, plane, bending)
+    )(line, *features)
     count = N_LINE // CHUNKS
 
     def fibre_chunk(chunk, after):
@@ -226,7 +262,7 @@
             in_specs=[pl.BlockSpec((count, 8, 128), lambda i: (chunk, 0, 0))]
             + [pl.BlockSpec(s, lambda i: (0, 0)) for s, _ in feature_shapes(SOURCES)],
             out_specs=pl.BlockSpec((count, 8, 128), lambda i: (0, 0, 0)),
-            compiler_params=params(),
+            compiler_params=params(24),
             cost_estimate=cost(count * 128 * SOURCES),
         )(held, *features)
 
@@ -239,27 +275,36 @@
         return x
 
     shell_parts = exchange_beside(shell_part, LINE)
-    shell_own = pl.pallas_call(sum_kernel, out_shape=tiles(N_PLANE))(shell_parts)
+    shell_own = pl.pallas_call(
+        columns_kernel,
+        out_shape=jax.ShapeDtypeStruct((N_PLANE, 16, 128), BF16),
+        compiler_params=params(2),
+    )(shell_parts)
     shell_all = exchange_beside(shell_own, PLANE)
-    columns = shell_all[:, :3, :64].astype(BF16).reshape(N_PLANE, 3, 4, 16)
+    columns = shell_all[:, :3, :64].reshape(N_PLANE, 3, 4, 16)
     columns = columns.transpose(1, 3, 0, 2).reshape(3, 16, 128)
     density_rows = -jnp.einsum(
         "xaqcbn,cbn->xaq", shell_inverse, columns, preferred_element_type=F32
     )
     pieces = density_rows.reshape(3, 4, 16).transpose(1, 0, 2)
     pieces = jnp.pad(pieces, ((0, 0), (0, 5), (0, 112)))
-    density_own = pl.pallas_call(sum_kernel, out_shape=tiles(N_PLANE))(exchange_beside(pieces, "src"))
-    density = density_own[0, :3, None, :16]
+    density_own, density = pl.pallas_call(
+        density_kernel,
+        out_shape=[tiles(N_PLANE), jax.ShapeDtypeStruct((3, 1, 16), F32)],
+        compiler_params=params(2),
+    )(exchange_beside(pieces, "src"))
     density_all = exchange_beside(density_own, PLANE)
     part = pl.pallas_call(
         back_kernel,
         out_shape=tiles(N_LINE),
         scratch_shapes=[pltpu.VMEM(s, t) for s, t in feature_shapes(SHELL_SOURCES)],
-        compiler_params=params(),
+        compiler_params=params(24),
         cost_estimate=cost(N_LINE * 128 * SHELL_SOURCES),
     )(line, shell_places, density_all, *flows)
-    velocity = jnp.sum(exchange(part, LINE)[:, :3], axis=0)
-    return velocity.reshape(3, 2, 64), density
+    velocity = pl.pallas_call(
+        velocity_kernel, out_shape=jax.ShapeDtypeStruct((3, 2, 64), F32), compiler_params=params(2)
+    )(exchange(part, LINE))
+    return velocity, density
 
 
 def solution(mesh):

time: 130 us -> 115 us (0.88)
  local copies, waits for them, and re-layouts: 16.7 us -> 3.34 us
  waiting for transfers between devices: 10.4 us -> 17.8 us
  starting transfers between devices: 29.2 us -> 25 us
  Pallas kernels: 31.1 us -> 28.9 us
  other arithmetic: 1.55 us -> 0.01 us
    unnamed x28 -> x8, local copies, waits for them, and re-layouts: 13.7 us -> 2.28 us
    all_to_all x5, waiting for transfers between devices: 10.4 us -> 17.8 us  [exchange(): return lax.all_to_all(x, axes, 0, 0, tiled=True)]
    all_to_all x5, starting transfers between devices: 29.2 us -> 25 us  [exchange(): return lax.all_to_all(x, axes, 0, 0, tiled=True)]
    pallas_call x4 -> x6, Pallas kernels: 9.13 us -> 7.45 us  [the longest x1 4.13 us: per_device(): pl.pallas_call(shell_kernel, out_shape=tiles(N_LINE), compiler_params=par...]
    unnamed x1 -> x0, other arithmetic: 1.52 us -> none
  transfers between devices with their start and end apart: 5 -> 5, of which waited for: 4 -> 4; matrix products, arithmetic and copies ran while one was open for 1% -> 0% of each run, Pallas kernels for 15% -> 17%
where the time goes in v2:
time: 115 us; the launch traced here: 114 us
  blocking collectives  37.5 us (33%)
  Pallas kernels  28.9 us (25%)
  starting transfers between devices  25 us (22%)
  waiting for transfers between devices  17.8 us (15%)
  local copies, waits for them, and re-layouts  3.34 us (3%)
    all_to_all x2, blocking collectives, exchange(): return lax.all_to_all(x, axes, 0, 0, tiled=True)  37.5 us
    all_to_all x5, starting transfers between devices, exchange(): return lax.all_to_all(x, axes, 0, 0, tiled=True)  25 us
    pallas_call x4, Pallas kernels, fibre_chunk(): pl.pallas_call(fibre_kernel, out_shape=tiles(count), grid=(1,), in_specs=...  18.9 us
    all_to_all x5, waiting for transfers between devices, exchange(): return lax.all_to_all(x, axes, 0, 0, tiled=True)  17.8 us
    pallas_call x1, Pallas kernels, per_device(): pl.pallas_call(shell_kernel, out_shape=tiles(N_LINE), compiler_params=par...  4.13 us
    pallas_call x1, Pallas kernels, per_device(): pl.pallas_call(back_kernel, out_shape=tiles(N_LINE), scratch_shapes=[pltp...  2.56 us
  transfers between devices with their start and end apart: 5, of which 4 were waited for; matrix products, arithmetic and copies ran while one was open for 0% of the time, Pallas kernels for 17%

profile of v2, /device:TPU:1, one launch (start us, length us, event | category | flops | bytes accessed | tf_op | source)
XLA Modules:
  0.0 114.2 jit_solution(8663744655472068048)
XLA Ops:
  0.6 0.0 copy-start
  0.6 0.0 copy-start.1
  0.7 0.8 copy-done.1
  1.5 0.0 copy-start.2
  1.5 0.7 copy-done.2
  2.2 0.7 shard_map.59
  2.9 22.7 %all_to_all.35.plane_ref = f32[32,8,128]{2,1,0:T(8,128)S(1)} all-to-all(f32[32,8,128]{2,1,0:T(8,128)S(1)} %get-tuple-element.30), channel_id=1, replica_groups=mesh['tgt_0'=4,'tgt_1'=8,'tgt_2'=2,'tgt_3'=2,'src'=4] {'tgt_0','tgt_1'}, dimensions={0} | all-to-all | bytes 262144 | tf_op jit(solution)/shard_map/all_to_all | solution.py:231
  25.5 9.2 %all-to-all-start.1 = ((f32[16,8,128]{2,1,0:T(8,128)}), f32[16,8,128]{2,1,0:T(8,128)S(1)}, u32[]{:S(2)}, u32[]{:S(2)}) async-start(f32[16,8,128]{2,1,0:T(8,128)} %get-tuple-element.31), calls=%async_computation.1 | async-start | bytes 131072 | tf_op jit(solution)/shard_map/all_to_all | solution.py:231
  34.7 0.0 copy-start.3
  34.7 0.8 copy-done.3
  35.5 0.6 shard_map.60
  36.1 6.2 %all-to-all-done.1.line_ref = f32[16,8,128]{2,1,0:T(8,128)S(1)} async-done(((f32[16,8,128]{2,1,0:T(8,128)}), f32[16,8,128]{2,1,0:T(8,128)S(1)}, u32[]{:S(2)}, u32[]{:S(2)}) %all-to-all-start.1) | async-done | bytes 65568 | tf_op jit(solution)/shard_map/all_to_all | solution.py:231
  42.3 4.1 %shard_map.61 = f32[16,8,128]{2,1,0:T(8,128)} custom-call(f32[16,8,128]{2,1,0:T(8,128)S(1)} %all-to-all-done.1.line_ref, bf16[32,4096]{1,0:T(8,128)(2,1)S(1)} %get-tuple-element.38.dist_ref, bf16[32,4096]{1,0:T(8,128)(2,1)S(1)} %get-tuple-element.39.proj_ref, bf16[16,4096]{1,0:T(8,128)(2,1)S(1)} %get-tuple-element.40.push_ref, ...), custom_call_target="tpu_custom_call" | custom-call | flops 419430400 | bytes 1048576 | tf_op jit(solution)/shard_map/pallas_call | solution.py:248
  46.4 3.7 %all-to-all-start.2 = ((f32[16,8,128]{2,1,0:T(8,128)}), f32[16,8,128]{2,1,0:T(8,128)S(1)}, u32[]{:S(2)}, u32[]{:S(2)}) async-start(f32[16,8,128]{2,1,0:T(8,128)} %shard_map.61), calls=%async_computation.2 | async-start | bytes 131072 | tf_op jit(solution)/shard_map/all_to_all | solution.py:231
  50.2 4.7 %shard_map.62.refs_0_ = f32[4,8,128]{2,1,0:T(8,128)S(1)} custom-call(f32[16,8,128]{2,1,0:T(8,128)S(1)} %all-to-all-done.1.line_ref, bf16[32,4096]{1,0:T(8,128)(2,1)S(1)} %get-tuple-element.38.dist_ref, bf16[32,4096]{1,0:T(8,128)(2,1)S(1)} %get-tuple-element.39.proj_ref, bf16[16,4096]{1,0:T(8,128)(2,1)S(1)} %get-tuple-element.40.push_ref, ...), custom_call_target="tpu_custom_call" | custom-call | flops 838860800 | bytes 1048576 | tf_op jit(solution)/shard_map/pallas_call | solution.py:258
  54.9 2.9 %all-to-all-done.2.parts_ref = f32[16,8,128]{2,1,0:T(8,128)S(1)} async-done(((f32[16,8,128]{2,1,0:T(8,128)}), f32[16,8,128]{2,1,0:T(8,128)S(1)}, u32[]{:S(2)}, u32[]{:S(2)}) %all-to-all-start.2) | async-done | bytes 65568 | tf_op jit(solution)/shard_map/all_to_all | solution.py:231
  57.7 0.7 shard_map.63
  58.4 3.9 %all-to-all-start.3 = ((bf16[32,16,128]{2,1,0:T(8,128)(2,1)}), bf16[32,16,128]{2,1,0:T(8,128)(2,1)S(1)}, u32[]{:S(2)}, u32[]{:S(2)}) async-start(bf16[32,16,128]{2,1,0:T(8,128)(2,1)} %shard_map.63), calls=%async_computation.3 | async-start | bytes 262144 | tf_op jit(solution)/shard_map/all_to_all | solution.py:231
  62.3 4.7 %shard_map.64.refs_1_ = f32[4,8,128]{2,1,0:T(8,128)S(1)} custom-call(f32[16,8,128]{2,1,0:T(8,128)S(1)} %all-to-all-done.1.line_ref, bf16[32,4096]{1,0:T(8,128)(2,1)S(1)} %get-tuple-element.38.dist_ref, bf16[32,4096]{1,0:T(8,128)(2,1)S(1)} %get-tuple-element.39.proj_ref, bf16[16,4096]{1,0:T(8,128)(2,1)S(1)} %get-tuple-element.40.push_ref, ...), custom_call_target="tpu_custom_call" | custom-call | flops 838860800 | bytes 1048576 | tf_op jit(solution)/shard_map/pallas_call | solution.py:258
  67.0 4.4 %all-to-all-done.3 = bf16[32,16,128]{2,1,0:T(8,128)(2,1)S(1)} async-done(((bf16[32,16,128]{2,1,0:T(8,128)(2,1)}), bf16[32,16,128]{2,1,0:T(8,128)(2,1)S(1)}, u32[]{:S(2)}, u32[]{:S(2)}) %all-to-all-start.3) | async-done | bytes 131104 | tf_op jit(solution)/shard_map/all_to_all | solution.py:231
  71.4 0.1 copy.6
  71.6 0.1 copy.7
  71.7 0.1 copy.9
  71.8 0.0 copy-done
  71.8 0.9 fusion
  72.7 0.1 reshape.22
  72.8 0.6 pad.4
  73.5 3.2 %all-to-all-start.4 = ((f32[4,8,128]{2,1,0:T(8,128)}), f32[4,8,128]{2,1,0:T(8,128)S(1)}, u32[]{:S(2)}, u32[]{:S(2)}) async-start(f32[4,8,128]{2,1,0:T(8,128)} %pad.4), calls=%async_computation.4 | async-start | bytes 32768 | tf_op jit(solution)/shard_map/all_to_all | solution.py:231
  76.7 4.7 %shard_map.65.refs_2_ = f32[4,8,128]{2,1,0:T(8,128)S(1)} custom-call(f32[16,8,128]{2,1,0:T(8,128)S(1)} %all-to-all-done.1.line_ref, bf16[32,4096]{1,0:T(8,128)(2,1)S(1)} %get-tuple-element.38.dist_ref, bf16[32,4096]{1,0:T(8,128)(2,1)S(1)} %get-tuple-element.39.proj_ref, bf16[16,4096]{1,0:T(8,128)(2,1)S(1)} %get-tuple-element.40.push_ref, ...), custom_call_target="tpu_custom_call" | custom-call | flops 838860800 | bytes 1048576 | tf_op jit(solution)/shard_map/pallas_call | solution.py:258
  81.4 0.0 all-to-all-done.4.parts_ref
  81.4 0.7 shard_map.66
  82.1 5.0 %all-to-all-start.5 = ((f32[32,8,128]{2,1,0:T(8,128)}), f32[32,8,128]{2,1,0:T(8,128)S(1)}, u32[]{:S(2)}, u32[]{:S(2)}) async-start(f32[32,8,128]{2,1,0:T(8,128)} %get-tuple-element.48), calls=%async_computation.5 | async-start | bytes 262144 | tf_op jit(solution)/shard_map/all_to_all | solution.py:231
  87.1 4.7 %shard_map.67.refs_3_ = f32[4,8,128]{2,1,0:T(8,128)S(1)} custom-call(f32[16,8,128]{2,1,0:T(8,128)S(1)} %all-to-all-done.1.line_ref, bf16[32,4096]{1,0:T(8,128)(2,1)S(1)} %get-tuple-element.38.dist_ref, bf16[32,4096]{1,0:T(8,128)(2,1)S(1)} %get-tuple-element.39.proj_ref, bf16[16,4096]{1,0:T(8,128)(2,1)S(1)} %get-tuple-element.40.push_ref, ...), custom_call_target="tpu_custom_call" | custom-call | flops 838860800 | bytes 1048576 | tf_op jit(solution)/shard_map/pallas_call | solution.py:258
  91.8 4.2 %all-to-all-done.5.density_ref = f32[32,8,128]{2,1,0:T(8,128)S(1)} async-done(((f32[32,8,128]{2,1,0:T(8,128)}), f32[32,8,128]{2,1,0:T(8,128)S(1)}, u32[]{:S(2)}, u32[]{:S(2)}) %all-to-all-start.5) | async-done | bytes 131104 | tf_op jit(solution)/shard_map/all_to_all | solution.py:231
  96.1 2.6 %shard_map.68 = f32[16,8,128]{2,1,0:T(8,128)S(1)} custom-call(f32[16,8,128]{2,1,0:T(8,128)S(1)} %all-to-all-done.1.line_ref, f32[8,512]{1,0:T(8,128)S(1)} %get-tuple-element.37.shell_ref, f32[32,8,128]{2,1,0:T(8,128)S(1)} %all-to-all-done.5.density_ref, f32[4,8,128]{2,1,0:T(8,128)S(1)} %shard_map.62.refs_0_, f32[4,8,128]{2,1,0:T(8,128)S(1)} %shard_map.64.refs_1_, ...), custom_call_target="tpu_custom_call" | custom-call | flops 419430400 | bytes 1048576 | tf_op jit(solution)/shard_map/pallas_call | solution.py:297
  98.7 14.8 %all_to_all.36.parts_ref = f32[16,8,128]{2,1,0:T(8,128)S(1)} all-to-all(f32[16,8,128]{2,1,0:T(8,128)S(1)} %shard_map.68), channel_id=1, replica_groups=mesh['tgt_0'=4,'tgt_1'=8,'tgt_2'=2,'tgt_3'=2,'src'=4] {'tgt_2','tgt_3','..., dimensions={0} | all-to-all | bytes 131072 | tf_op jit(solution)/shard_map/all_to_all | solution.py:231
  113.5 0.7 shard_map.69
  (3 shorter events, 0.0 us)
Async XLA Ops:
  0.6 71.2 %copy-start = (bf16[3,1,64,3,16,128]{5,4,3,2,1,0:T(8,128)(2,1)S(1)}, bf16[3,1,64,3,16,128]{5,4,3,2,1,0:T(8,128)(2,1)}, u32[]{:S(2)}) copy-start(bf16[3,1,64,3,16,128]{5,4,3,2,1,0:T(8,128)(2,1)} %param.7) | copy-start | bytes 7077892
  0.6 0.8 copy-start.1
  1.5 0.7 copy-start.2
  25.5 16.8 %all-to-all-start.1 = ((f32[16,8,128]{2,1,0:T(8,128)}), f32[16,8,128]{2,1,0:T(8,128)S(1)}, u32[]{:S(2)}, u32[]{:S(2)}) async-start(f32[16,8,128]{2,1,0:T(8,128)} %get-tuple-element.31), calls=%async_computation.1 | async-start | bytes 131072 | tf_op jit(solution)/shard_map/all_to_all | solution.py:231
  34.7 0.8 copy-start.3
  46.4 11.3 %all-to-all-start.2 = ((f32[16,8,128]{2,1,0:T(8,128)}), f32[16,8,128]{2,1,0:T(8,128)S(1)}, u32[]{:S(2)}, u32[]{:S(2)}) async-start(f32[16,8,128]{2,1,0:T(8,128)} %shard_map.61), calls=%async_computation.2 | async-start | bytes 131072 | tf_op jit(solution)/shard_map/all_to_all | solution.py:231
  58.4 13.0 %all-to-all-start.3 = ((bf16[32,16,128]{2,1,0:T(8,128)(2,1)}), bf16[32,16,128]{2,1,0:T(8,128)(2,1)S(1)}, u32[]{:S(2)}, u32[]{:S(2)}) async-start(bf16[32,16,128]{2,1,0:T(8,128)(2,1)} %shard_map.63), calls=%async_computation.3 | async-start | bytes 262144 | tf_op jit(solution)/shard_map/all_to_all | solution.py:231
  73.5 8.0 %all-to-all-start.4 = ((f32[4,8,128]{2,1,0:T(8,128)}), f32[4,8,128]{2,1,0:T(8,128)S(1)}, u32[]{:S(2)}, u32[]{:S(2)}) async-start(f32[4,8,128]{2,1,0:T(8,128)} %pad.4), calls=%async_computation.4 | async-start | bytes 32768 | tf_op jit(solution)/shard_map/all_to_all | solution.py:231
  82.1 14.0 %all-to-all-start.5 = ((f32[32,8,128]{2,1,0:T(8,128)}), f32[32,8,128]{2,1,0:T(8,128)S(1)}, u32[]{:S(2)}, u32[]{:S(2)}) async-start(f32[32,8,128]{2,1,0:T(8,128)} %get-tuple-element.48), calls=%async_computation.5 | async-start | bytes 262144 | tf_op jit(solution)/shard_map/all_to_all | solution.py:231

commit v3 on v2

--- a/solution.py
+++ b/solution.py
@@ -1,3 +1,4 @@
+import functools
 import math
 
 import jax
@@ -15,8 +16,8 @@
 N_LINE = 16
 N_PLANE = 32
 SOURCES = N_PLANE * 128
-SHELL_SOURCES = N_PLANE * 16
-CHUNKS = 4
+SHELL = 8192
+CHUNKS = ((0, (512, 256)), (6, (512, 512, 256)))
 STEP = 512
 ROWS = (((0,), (0,)), ((), ()))
 
@@ -69,12 +70,18 @@
     return right_rows(-2.0 * places, 1.0, square), right_rows(pushes, 0.0, -along), push_rows, place_rows
 
 
-def pair_sums(targets, count, dist_ref, proj_ref, push_ref, place_ref, unroll, fine):
+def pair_sums(targets, count, dist_ref, proj_ref, push_ref, place_ref, unroll, fine, halves=False):
     row = rows_of(targets)
     x = jnp.where(row < 3, targets * scale, 0.0)
     square = jnp.sum(x * x, axis=0, keepdims=True) + 1.0
     features = left_rows(x, square)
-    width = targets.shape[1]
+    if halves:
+        zero = jnp.zeros_like(features)
+        features = jnp.concatenate(
+            [jnp.concatenate([features, zero], axis=1), jnp.concatenate([zero, features], axis=1)], axis=0
+        )
+    width = features.shape[1]
+    rows = push_ref.shape[0]
     step = min(STEP, count)
 
     def add_block(k, sums):
@@ -97,8 +104,12 @@
             proj_sum += jnp.dot(place_ref[:, part], low, preferred_element_type=F32)
         return diag_sum, proj_sum
 
-    start = (jnp.zeros((16, width), F32), jnp.zeros((16, width), F32))
+    start = (jnp.zeros((rows, width), F32), jnp.zeros((rows, width), F32))
     diag_sum, proj_sum = lax.fori_loop(0, count // step, add_block, start, unroll=unroll)
+    if halves:
+        half = width // 2
+        diag_sum = diag_sum[:16, :half] + diag_sum[16:, half:]
+        proj_sum = proj_sum[:16, :half] + proj_sum[16:, half:]
     rest = proj_sum[8:16]
     moved = proj_sum[0:8] + rest + pltpu.roll(rest, 4, 0)
     return (diag_sum[0:8] + diag_sum[8:16] + x * moved[3:4] - moved) * mobility
@@ -130,7 +141,7 @@
     plane_ref[...] = jnp.broadcast_to(tile[None], plane_ref.shape)
 
 
-def source_kernel(plane_ref, bending_ref, dist_ref, proj_ref, push_ref, place_ref, shell_ref):
+def source_kernel(plane_ref, bending_ref, dist_ref, proj_ref, push_ref, place_ref):
     square = bending_ref[...]
     zero = jnp.zeros_like(square)
     both = jnp.concatenate(
@@ -143,10 +154,10 @@
     pushes = jnp.concatenate([pushes[8 * i : 8 * i + 8] for i in range(N_PLANE)], axis=1)
     places = side_by_side(plane_ref, 0, N_PLANE)
     dist_ref[...], proj_ref[...], push_ref[...], place_ref[...] = source_features(places, pushes)
-    shell_ref[...] = packed([plane_ref[i] for i in range(N_PLANE)], 3)
-
-
-def shell_kernel(line_ref, dist_ref, proj_ref, push_ref, place_ref, part_ref):
+
+
+def shell_kernel(line_ref, dist_ref, proj_ref, push_ref, place_ref, part_ref, shell_ref):
+    shell_ref[...] = packed([line_ref[i] for i in range(N_LINE)], 3)
     order = [pair * 4 + src for src in range(4) for pair in range(4)]
     targets = packed([line_ref[i] for i in order], 3)
     flow = pair_sums(targets, SOURCES, dist_ref, proj_ref, push_ref, place_ref, 4, True)
@@ -157,13 +168,23 @@
             part_ref[pair * 4 + src] = piece
 
 
-def fibre_kernel(line_ref, dist_ref, proj_ref, push_ref, place_ref, flow_ref):
-    count = N_LINE // CHUNKS
-    flow = pair_sums(
-        side_by_side(line_ref, 0, count), SOURCES, dist_ref, proj_ref, push_ref, place_ref, 4, False
-    )
-    for i in range(count):
-        flow_ref[i] = flow[:, 128 * i : 128 * i + 128]
+def fibre_kernel(first, widths, line_ref, dist_ref, proj_ref, push_ref, place_ref, flow_ref):
+    done = 0
+    for width in widths:
+        count = width // 128
+        flow = pair_sums(
+            side_by_side(line_ref, first + done, count),
+            SOURCES,
+            dist_ref,
+            proj_ref,
+            push_ref,
+            place_ref,
+            4,
+            False,
+        )
+        for i in range(count):
+            flow_ref[done + i] = flow[:, 128 * i : 128 * i + 128]
+        done += count
 
 
 def total_of(parts_ref):
@@ -179,36 +200,59 @@
     out_ref[...] = jnp.broadcast_to(total[None], out_ref.shape)
 
 
-def density_kernel(parts_ref, out_ref, density_ref):
-    total = total_of(parts_ref)
-    out_ref[...] = jnp.broadcast_to(total[None], out_ref.shape)
-    density_ref[:, 0, :] = total[0:3, 0:16]
-
-
-def velocity_kernel(parts_ref, out_ref):
-    total = total_of(parts_ref)
-    out_ref[:, 0, :] = total[0:3, 0:64]
-    out_ref[:, 1, :] = total[0:3, 64:128]
-
-
-def back_kernel(line_ref, shell_ref, density_ref, *refs):
-    flows, (part_ref, dist_ref, proj_ref, push_ref, place_ref) = refs[:CHUNKS], refs[CHUNKS:]
-    pushes = packed([density_ref[i] for i in range(N_PLANE)], 0)
-    dist_ref[...], proj_ref[...], push_ref[...], place_ref[...] = source_features(shell_ref[...], pushes)
-    count = N_LINE // CHUNKS
-    for chunk in range(CHUNKS):
-        flow = pair_sums(
-            side_by_side(line_ref, chunk * count, count),
-            SHELL_SOURCES,
-            dist_ref,
-            proj_ref,
-            push_ref,
-            place_ref,
-            1,
-            False,
-        )
-        for i in range(count):
-            part_ref[chunk * count + i] = flow[:, 128 * i : 128 * i + 128] + flows[chunk][i]
+def message_kernel(pair_ref, density_ref, *refs):
+    flows, out_ref = refs[:-1], refs[-1]
+    density = jnp.concatenate([density_ref[:, 0, :], jnp.zeros((3, 64), F32)], axis=1)
+    density = jnp.concatenate([jnp.zeros((3, 128), F32), density, jnp.zeros((2, 128), F32)], axis=0)
+    row = rows_of(density)
+    lane = lax.broadcasted_iota(jnp.int32, density.shape, 1)
+    pieces = []
+    for src in range(4):
+        own = jnp.where(lane // 16 == src, density, 0.0)
+        pieces.append(pltpu.roll(own, 64 - 16 * src, 1))
+    index = 0
+    for flow_ref in flows:
+        for i in range(flow_ref.shape[0]):
+            mine = (pair_ref[0] == index // 4).astype(F32)
+            out_ref[index] = jnp.where(row < 3, flow_ref[i], density + mine * pieces[index % 4])
+            index += 1
+
+
+def relay_kernel(parts_ref, shell_ref, out_ref, flow_ref, density_ref):
+    lane = lax.broadcasted_iota(jnp.int32, (8, 128), 1)
+    row = lax.broadcasted_iota(jnp.int32, (8, 128), 0)
+    pairs = []
+    for pair in range(4):
+        total = parts_ref[pair * 4]
+        for src in range(1, 4):
+            total += parts_ref[pair * 4 + src]
+        pairs.append(total)
+    flow = (pairs[0] + pairs[1]) + (pairs[2] + pairs[3])
+    flow_ref[...] = flow
+    density_ref[:, 0, :] = flow[3:6, 64:80]
+    places = shell_ref[...]
+    for half in range(2):
+        density = jnp.where(lane < 64, pairs[2 * half], pltpu.roll(pairs[2 * half + 1], 64, 1))
+        density = pltpu.roll(density, 5, 0)
+        place = pltpu.roll(places[:, 128 * half : 128 * half + 128], 3, 0)
+        tile = jnp.where(row < 3, density, place)
+        out_ref[:, :, 128 * half : 128 * half + 128] = jnp.broadcast_to(tile[None], (N_PLANE, 8, 128))
+
+
+def back_kernel(own_ref, plane_ref, flow_ref, out_ref, dist_ref, proj_ref, push_ref, place_ref):
+    for half in range(2):
+        tile = side_by_side(plane_ref, half * (N_PLANE // 2), N_PLANE // 2)
+        dist, proj, push, place = source_features(pltpu.roll(tile, 5, 0), tile)
+        dist_ref[32 * half : 32 * half + 32] = dist
+        proj_ref[32 * half : 32 * half + 32] = proj
+        push_ref[16 * half : 16 * half + 16] = push
+        place_ref[16 * half : 16 * half + 16] = place
+    back = pair_sums(
+        own_ref[0], SHELL // 2, dist_ref, proj_ref, push_ref, place_ref, 4, False, True
+    )
+    velocity = back + flow_ref[...]
+    out_ref[:, 0, :] = velocity[0:3, 0:64]
+    out_ref[:, 1, :] = velocity[0:3, 64:128]
 
 
 def tiles(count):
@@ -238,32 +282,28 @@
     plane = exchange(own_plane, PLANE)
     own_line, _ = lax.optimization_barrier((own_line, plane))
     features = [jax.ShapeDtypeStruct(s, t) for s, t in feature_shapes(SOURCES)]
-    *features, shell_places = pl.pallas_call(
+    features = pl.pallas_call(
         source_kernel,
-        out_shape=[*features, jax.ShapeDtypeStruct((8, SHELL_SOURCES), F32)],
+        out_shape=features,
         compiler_params=params(24),
         cost_estimate=cost(64 * SOURCES),
     )(plane, bending)
     line, features = lax.optimization_barrier((exchange(own_line, LINE), features))
-    shell_part = pl.pallas_call(
+    shell_part, shell_places = pl.pallas_call(
         shell_kernel,
-        out_shape=tiles(N_LINE),
+        out_shape=[tiles(N_LINE), jax.ShapeDtypeStruct((8, 256), F32)],
         compiler_params=params(24),
         cost_estimate=cost(256 * SOURCES),
     )(line, *features)
-    count = N_LINE // CHUNKS
 
     def fibre_chunk(chunk, after):
         held, _ = lax.optimization_barrier((line, after))
+        first, widths = CHUNKS[chunk]
         return pl.pallas_call(
-            fibre_kernel,
-            out_shape=tiles(count),
-            grid=(1,),
-            in_specs=[pl.BlockSpec((count, 8, 128), lambda i: (chunk, 0, 0))]
-            + [pl.BlockSpec(s, lambda i: (0, 0)) for s, _ in feature_shapes(SOURCES)],
-            out_specs=pl.BlockSpec((count, 8, 128), lambda i: (0, 0, 0)),
+            functools.partial(fibre_kernel, first, widths),
+            out_shape=tiles(sum(widths) // 128),
             compiler_params=params(24),
-            cost_estimate=cost(count * 128 * SOURCES),
+            cost_estimate=cost(sum(widths) * SOURCES),
         )(held, *features)
 
     flows = []
@@ -286,24 +326,28 @@
     density_rows = -jnp.einsum(
         "xaqcbn,cbn->xaq", shell_inverse, columns, preferred_element_type=F32
     )
-    pieces = density_rows.reshape(3, 4, 16).transpose(1, 0, 2)
-    pieces = jnp.pad(pieces, ((0, 0), (0, 5), (0, 112)))
-    density_own, density = pl.pallas_call(
-        density_kernel,
-        out_shape=[tiles(N_PLANE), jax.ShapeDtypeStruct((3, 1, 16), F32)],
+    pair = lax.axis_index("tgt_2") * 2 + lax.axis_index("tgt_3")
+    message = pl.pallas_call(
+        message_kernel,
+        out_shape=tiles(N_LINE),
+        in_specs=[pl.BlockSpec(memory_space=pltpu.SMEM)] + [pl.BlockSpec(memory_space=pltpu.VMEM)] * 3,
         compiler_params=params(2),
-    )(exchange_beside(pieces, "src"))
-    density_all = exchange_beside(density_own, PLANE)
-    part = pl.pallas_call(
+    )(pair.astype(jnp.int32).reshape(1), density_rows, *flows)
+    relay, fibre_flow, density = pl.pallas_call(
+        relay_kernel,
+        out_shape=[
+            jax.ShapeDtypeStruct((N_PLANE, 8, 256), F32),
+            jax.ShapeDtypeStruct((8, 128), F32),
+            jax.ShapeDtypeStruct((3, 1, 16), F32),
+        ],
+        compiler_params=params(2),
+    )(exchange(message, LINE), shell_places)
+    velocity = pl.pallas_call(
         back_kernel,
-        out_shape=tiles(N_LINE),
-        scratch_shapes=[pltpu.VMEM(s, t) for s, t in feature_shapes(SHELL_SOURCES)],
+        out_shape=jax.ShapeDtypeStruct((3, 2, 64), F32),
+        scratch_shapes=[pltpu.VMEM((2 * s[0], SHELL // 2), t) for s, t in feature_shapes(0)],
         compiler_params=params(24),
-        cost_estimate=cost(N_LINE * 128 * SHELL_SOURCES),
-    )(line, shell_places, density_all, *flows)
-    velocity = pl.pallas_call(
-        velocity_kernel, out_shape=jax.ShapeDtypeStruct((3, 2, 64), F32), compiler_params=params(2)
-    )(exchange(part, LINE))
+    )(own_line, exchange(relay, PLANE), fibre_flow)
     return velocity, density
 
 

time: 115 us -> 118 us (1.026); the launches traced: 114 us -> 116 us
  blocking collectives: 37.5 us -> 56.1 us
  waiting for transfers between devices: 17.8 us -> 6.25 us
  starting transfers between devices: 25 us -> 16.9 us
  Pallas kernels: 28.9 us -> 32.2 us
    all_to_all x2 -> x3, blocking collectives: 37.5 us -> 56.1 us  [exchange(): return lax.all_to_all(x, axes, 0, 0, tiled=True)]
    all_to_all x5 -> x3, waiting for transfers between devices: 17.8 us -> 6.25 us  [exchange(): return lax.all_to_all(x, axes, 0, 0, tiled=True)]
    all_to_all x5 -> x3, starting transfers between devices: 25 us -> 16.9 us  [exchange(): return lax.all_to_all(x, axes, 0, 0, tiled=True)]
    pallas_call x9 -> x7, Pallas kernels: 27.5 us -> 30.8 us  [the longest x2 20.1 us: fibre_chunk(): pl.pallas_call(functools.partial(fibre_kernel, first, widths), out_shape=...]
  transfers between devices with their start and end apart: 5 -> 3, of which waited for: 4 -> 1; matrix products, arithmetic and copies ran while one was open for 0% -> 0% of each run, Pallas kernels for 17% -> 18%
where the time goes in v3:
time: 118 us; the launch traced here: 116 us
  blocking collectives  56.1 us (48%)
  Pallas kernels  32.2 us (27%)
  starting transfers between devices  16.9 us (14%)
  waiting for transfers between devices  6.25 us (5%)
  local copies, waits for them, and re-layouts  2.64 us (2%)
    all_to_all x3, blocking collectives, exchange(): return lax.all_to_all(x, axes, 0, 0, tiled=True)  56.1 us
    pallas_call x2, Pallas kernels, fibre_chunk(): pl.pallas_call(functools.partial(fibre_kernel, first, widths), out_shape=...  20.1 us
    all_to_all x3, starting transfers between devices, exchange(): return lax.all_to_all(x, axes, 0, 0, tiled=True)  16.9 us
    all_to_all x3, waiting for transfers between devices, exchange(): return lax.all_to_all(x, axes, 0, 0, tiled=True)  6.25 us
    pallas_call x1, Pallas kernels, per_device(): pl.pallas_call(back_kernel, out_shape=jax.ShapeDtypeStruct((3, 2, 64), F3...  5.27 us
    pallas_call x1, Pallas kernels, per_device(): pl.pallas_call(shell_kernel, out_shape=[tiles(N_LINE), jax.ShapeDtypeStru...  4.12 us
  transfers between devices with their start and end apart: 3, of which 1 were waited for; matrix products, arithmetic and copies ran while one was open for 0% of the time, Pallas kernels for 18%

profile of v3, /device:TPU:1, one launch (start us, length us, event | category | flops | bytes accessed | tf_op | source)
XLA Modules:
  0.0 115.7 jit_solution(4758440629218757841)
XLA Ops:
  0.6 0.0 copy-start
  0.6 0.0 copy-start.1
  0.7 0.8 copy-done.1
  1.5 0.0 copy-start.2
  1.5 0.7 copy-done.2
  2.2 0.7 shard_map.59
  2.9 22.7 %all_to_all.30.plane_ref = f32[32,8,128]{2,1,0:T(8,128)S(1)} all-to-all(f32[32,8,128]{2,1,0:T(8,128)S(1)} %get-tuple-element.26), channel_id=1, replica_groups=mesh['tgt_0'=4,'tgt_1'=8,'tgt_2'=2,'tgt_3'=2,'src'=4] {'tgt_0','tgt_1'}, dimensions={0} | all-to-all | bytes 262144 | tf_op jit(solution)/shard_map/all_to_all | solution.py:275
  25.5 9.2 %all-to-all-start.1 = ((f32[16,8,128]{2,1,0:T(8,128)}), f32[16,8,128]{2,1,0:T(8,128)S(1)}, u32[]{:S(2)}, u32[]{:S(2)}) async-start(f32[16,8,128]{2,1,0:T(8,128)} %get-tuple-element.27.own_ref), calls=%async_computation.1 | async-start | bytes 131072 | tf_op jit(solution)/shard_map/all_to_all | solution.py:275
  34.7 0.0 copy-start.3
  34.7 0.8 copy-done.3
  35.5 0.6 shard_map.60
  36.1 6.2 %all-to-all-done.1.line_ref = f32[16,8,128]{2,1,0:T(8,128)S(1)} async-done(((f32[16,8,128]{2,1,0:T(8,128)}), f32[16,8,128]{2,1,0:T(8,128)S(1)}, u32[]{:S(2)}, u32[]{:S(2)}) %all-to-all-start.1) | async-done | bytes 65568 | tf_op jit(solution)/shard_map/all_to_all | solution.py:275
  42.3 4.1 %shard_map.61 = (f32[16,8,128]{2,1,0:T(8,128)}, f32[8,256]{1,0:T(8,128)S(1)}) custom-call(f32[16,8,128]{2,1,0:T(8,128)S(1)} %all-to-all-done.1.line_ref, bf16[32,4096]{1,0:T(8,128)(2,1)S(1)} %get-tuple-element.33.dist_ref, bf16[32,4096]{1,0:T(8,128)(2,1)S(1)} %get-tuple-element.34.proj_ref, bf16[16,4096]{1,0:T(8,128)(2,1)S(1)} %get-tuple-element.35.push_ref, ...), custom_call_target="tpu_custom_call" | custom-call | flops 419430400 | bytes 1048576 | tf_op jit(solution)/shard_map/pallas_call | solution.py:292
  46.4 3.7 %all-to-all-start.2 = ((f32[16,8,128]{2,1,0:T(8,128)}), f32[16,8,128]{2,1,0:T(8,128)S(1)}, u32[]{:S(2)}, u32[]{:S(2)}) async-start(f32[16,8,128]{2,1,0:T(8,128)} %get-tuple-element.37), calls=%async_computation.2 | async-start | bytes 131072 | tf_op jit(solution)/shard_map/all_to_all | solution.py:275
  50.1 7.7 %shard_map.62.refs_0_ = f32[6,8,128]{2,1,0:T(8,128)S(1)} custom-call(f32[16,8,128]{2,1,0:T(8,128)S(1)} %all-to-all-done.1.line_ref, bf16[32,4096]{1,0:T(8,128)(2,1)S(1)} %get-tuple-element.33.dist_ref, bf16[32,4096]{1,0:T(8,128)(2,1)S(1)} %get-tuple-element.34.proj_ref, bf16[16,4096]{1,0:T(8,128)(2,1)S(1)} %get-tuple-element.35.push_ref, ...), custom_call_target="tpu_custom_call" | custom-call | flops 1258291200 | bytes 1048576 | tf_op jit(solution)/shard_map/pallas_call | solution.py:302
  57.8 0.0 all-to-all-done.2.parts_ref
  57.8 0.7 shard_map.63
  58.5 4.0 %all-to-all-start.3 = ((bf16[32,16,128]{2,1,0:T(8,128)(2,1)}), bf16[32,16,128]{2,1,0:T(8,128)(2,1)S(1)}, u32[]{:S(2)}, u32[]{:S(2)}) async-start(bf16[32,16,128]{2,1,0:T(8,128)(2,1)} %shard_map.63), calls=%async_computation.3 | async-start | bytes 262144 | tf_op jit(solution)/shard_map/all_to_all | solution.py:275
  62.6 12.4 %shard_map.64.refs_1_ = f32[10,8,128]{2,1,0:T(8,128)S(1)} custom-call(f32[16,8,128]{2,1,0:T(8,128)S(1)} %all-to-all-done.1.line_ref, bf16[32,4096]{1,0:T(8,128)(2,1)S(1)} %get-tuple-element.33.dist_ref, bf16[32,4096]{1,0:T(8,128)(2,1)S(1)} %get-tuple-element.34.proj_ref, bf16[16,4096]{1,0:T(8,128)(2,1)S(1)} %get-tuple-element.35.push_ref, ...), custom_call_target="tpu_custom_call" | custom-call | flops 2097152000 | bytes 1048576 | tf_op jit(solution)/shard_map/pallas_call | solution.py:302
  75.0 0.0 all-to-all-done.3
  75.0 0.1 copy.6
  75.1 0.1 copy.7
  75.2 0.1 copy.8
  75.3 0.0 copy-done
  75.4 0.9 fusion
  76.3 0.1 shard_map.65
  76.4 14.6 %all_to_all.31.parts_ref = f32[16,8,128]{2,1,0:T(8,128)S(1)} all-to-all(f32[16,8,128]{2,1,0:T(8,128)S(1)} %shard_map.65), channel_id=1, replica_groups=mesh['tgt_0'=4,'tgt_1'=8,'tgt_2'=2,'tgt_3'=2,'src'=4] {'tgt_2','tgt_3','..., dimensions={0} | all-to-all | bytes 131072 | tf_op jit(solution)/shard_map/all_to_all | solution.py:275
  91.0 0.7 shard_map.66
  91.7 18.8 %all_to_all.32.plane_ref = f32[32,8,256]{2,1,0:T(8,128)S(1)} all-to-all(f32[32,8,256]{2,1,0:T(8,128)S(1)} %get-tuple-element.45), channel_id=1, replica_groups=mesh['tgt_0'=4,'tgt_1'=8,'tgt_2'=2,'tgt_3'=2,'src'=4] {'tgt_0','tgt_1'}, dimensions={0} | all-to-all | bytes 524288 | tf_op jit(solution)/shard_map/all_to_all | solution.py:275
  110.5 5.3 %shard_map.67 = f32[3,2,64]{2,1,0:T(2,128)} custom-call(f32[16,8,128]{2,1,0:T(8,128)} %get-tuple-element.27.own_ref, f32[32,8,256]{2,1,0:T(8,128)S(1)} %all_to_all.32.plane_ref, f32[8,128]{1,0:T(8,128)S(1)} %get-tuple-element.46.flow_ref), custom_call_target="tpu_custom_call" | custom-call | tf_op jit(solution)/shard_map/pallas_call | solution.py:345
  (3 shorter events, 0.0 us)
Async XLA Ops:
  0.6 74.7 %copy-start = (bf16[3,1,64,3,16,128]{5,4,3,2,1,0:T(8,128)(2,1)S(1)}, bf16[3,1,64,3,16,128]{5,4,3,2,1,0:T(8,128)(2,1)}, u32[]{:S(2)}) copy-start(bf16[3,1,64,3,16,128]{5,4,3,2,1,0:T(8,128)(2,1)} %param.7) | copy-start | bytes 7077892
  0.6 0.8 copy-start.1
  1.5 0.7 copy-start.2
  25.5 16.8 %all-to-all-start.1 = ((f32[16,8,128]{2,1,0:T(8,128)}), f32[16,8,128]{2,1,0:T(8,128)S(1)}, u32[]{:S(2)}, u32[]{:S(2)}) async-start(f32[16,8,128]{2,1,0:T(8,128)} %get-tuple-element.27.own_ref), calls=%async_computation.1 | async-start | bytes 131072 | tf_op jit(solution)/shard_map/all_to_all | solution.py:275
  34.7 0.8 copy-start.3
  46.4 11.4 %all-to-all-start.2 = ((f32[16,8,128]{2,1,0:T(8,128)}), f32[16,8,128]{2,1,0:T(8,128)S(1)}, u32[]{:S(2)}, u32[]{:S(2)}) async-start(f32[16,8,128]{2,1,0:T(8,128)} %get-tuple-element.37), calls=%async_computation.2 | async-start | bytes 131072 | tf_op jit(solution)/shard_map/all_to_all | solution.py:275
  58.5 16.4 %all-to-all-start.3 = ((bf16[32,16,128]{2,1,0:T(8,128)(2,1)}), bf16[32,16,128]{2,1,0:T(8,128)(2,1)S(1)}, u32[]{:S(2)}, u32[]{:S(2)}) async-start(bf16[32,16,128]{2,1,0:T(8,128)(2,1)} %shard_map.63), calls=%async_computation.3 | async-start | bytes 262144 | tf_op jit(solution)/shard_map/all_to_all | solution.py:275

commit v4 on v3

--- a/solution.py
+++ b/solution.py
@@ -16,8 +16,8 @@
 N_LINE = 16
 N_PLANE = 32
 SOURCES = N_PLANE * 128
-SHELL = 8192
-CHUNKS = ((0, (512, 256)), (6, (512, 512, 256)))
+BACK_SOURCES = N_PLANE * 64
+CHUNKS = ((0, (512, 256)), (6, (512, 256)), (12, (512,)))
 STEP = 512
 ROWS = (((0,), (0,)), ((), ()))
 
@@ -70,18 +70,12 @@
     return right_rows(-2.0 * places, 1.0, square), right_rows(pushes, 0.0, -along), push_rows, place_rows
 
 
-def pair_sums(targets, count, dist_ref, proj_ref, push_ref, place_ref, unroll, fine, halves=False):
+def pair_sums(targets, count, dist_ref, proj_ref, push_ref, place_ref, unroll, level):
     row = rows_of(targets)
     x = jnp.where(row < 3, targets * scale, 0.0)
     square = jnp.sum(x * x, axis=0, keepdims=True) + 1.0
     features = left_rows(x, square)
-    if halves:
-        zero = jnp.zeros_like(features)
-        features = jnp.concatenate(
-            [jnp.concatenate([features, zero], axis=1), jnp.concatenate([zero, features], axis=1)], axis=0
-        )
     width = features.shape[1]
-    rows = push_ref.shape[0]
     step = min(STEP, count)
 
     def add_block(k, sums):
@@ -93,23 +87,20 @@
         inv_cubed = inv_root * inv_root * inv_root
         diag = inv_root + inv_cubed
         high = diag.astype(BF16)
-        low = (diag - high.astype(F32)).astype(BF16)
         diag_sum += jnp.dot(push_ref[:, part], high, preferred_element_type=F32)
-        diag_sum += jnp.dot(push_ref[:, part], low, preferred_element_type=F32)
+        if level > 0:
+            low = (diag - high.astype(F32)).astype(BF16)
+            diag_sum += jnp.dot(push_ref[:, part], low, preferred_element_type=F32)
         proj = along * inv_cubed
         high = proj.astype(BF16)
         proj_sum += jnp.dot(place_ref[:, part], high, preferred_element_type=F32)
-        if fine:
+        if level > 1:
             low = (proj - high.astype(F32)).astype(BF16)
             proj_sum += jnp.dot(place_ref[:, part], low, preferred_element_type=F32)
         return diag_sum, proj_sum
 
-    start = (jnp.zeros((rows, width), F32), jnp.zeros((rows, width), F32))
+    start = (jnp.zeros((16, width), F32), jnp.zeros((16, width), F32))
     diag_sum, proj_sum = lax.fori_loop(0, count // step, add_block, start, unroll=unroll)
-    if halves:
-        half = width // 2
-        diag_sum = diag_sum[:16, :half] + diag_sum[16:, half:]
-        proj_sum = proj_sum[:16, :half] + proj_sum[16:, half:]
     rest = proj_sum[8:16]
     moved = proj_sum[0:8] + rest + pltpu.roll(rest, 4, 0)
     return (diag_sum[0:8] + diag_sum[8:16] + x * moved[3:4] - moved) * mobility
@@ -160,7 +151,7 @@
     shell_ref[...] = packed([line_ref[i] for i in range(N_LINE)], 3)
     order = [pair * 4 + src for src in range(4) for pair in range(4)]
     targets = packed([line_ref[i] for i in order], 3)
-    flow = pair_sums(targets, SOURCES, dist_ref, proj_ref, push_ref, place_ref, 4, True)
+    flow = pair_sums(targets, SOURCES, dist_ref, proj_ref, push_ref, place_ref, 4, 2)
     for src in range(4):
         half = flow[:, 128 * (src // 2) : 128 * (src // 2) + 128]
         piece = pltpu.roll(half, 64, 1) if src % 2 else half
@@ -180,7 +171,7 @@
             push_ref,
             place_ref,
             4,
-            False,
+            1,
         )
         for i in range(count):
             flow_ref[done + i] = flow[:, 128 * i : 128 * i + 128]
@@ -200,59 +191,64 @@
     out_ref[...] = jnp.broadcast_to(total[None], out_ref.shape)
 
 
-def message_kernel(pair_ref, density_ref, *refs):
-    flows, out_ref = refs[:-1], refs[-1]
+def density_kernel(pair_ref, density_ref, shell_ref, out_ref):
     density = jnp.concatenate([density_ref[:, 0, :], jnp.zeros((3, 64), F32)], axis=1)
-    density = jnp.concatenate([jnp.zeros((3, 128), F32), density, jnp.zeros((2, 128), F32)], axis=0)
-    row = rows_of(density)
+    density = jnp.concatenate([density, jnp.zeros((5, 128), F32)], axis=0)
     lane = lax.broadcasted_iota(jnp.int32, density.shape, 1)
+    places = jnp.zeros_like(density)
+    for pair in range(4):
+        half = shell_ref[:, 128 * (pair // 2) : 128 * (pair // 2) + 128]
+        half = pltpu.roll(half, 64, 1) if pair % 2 else half
+        places += jnp.where((pair_ref[0] == pair) & (lane < 64), half, 0.0)
+    tile = density + pltpu.roll(places, 3, 0)
+    out_ref[...] = jnp.broadcast_to(tile[None], out_ref.shape)
+
+
+def back_kernel(pair_ref, line_ref, plane_ref, own_ref, *refs):
+    flows, (part_ref, dist_ref, proj_ref, push_ref, place_ref) = refs[: len(CHUNKS)], refs[len(CHUNKS) :]
+    lane = lax.broadcasted_iota(jnp.int32, (8, 128), 1)
+    row = lax.broadcasted_iota(jnp.int32, (8, 128), 0)
+    sources = [
+        jnp.where(lane < 64, plane_ref[2 * i], pltpu.roll(plane_ref[2 * i + 1], 64, 1))
+        for i in range(N_PLANE // 2)
+    ]
+    sources = jnp.concatenate(sources, axis=1)
+    dist_ref[...], proj_ref[...], push_ref[...], place_ref[...] = source_features(
+        pltpu.roll(sources, 5, 0), sources
+    )
+    own = pltpu.roll(own_ref[0], 3, 0)
     pieces = []
     for src in range(4):
-        own = jnp.where(lane // 16 == src, density, 0.0)
-        pieces.append(pltpu.roll(own, 64 - 16 * src, 1))
+        piece = pltpu.roll(own, 128 - 16 * src, 1) if src else own
+        pieces.append(jnp.where((row >= 3) & (lane < 16), piece, 0.0))
     index = 0
     for flow_ref in flows:
-        for i in range(flow_ref.shape[0]):
-            mine = (pair_ref[0] == index // 4).astype(F32)
-            out_ref[index] = jnp.where(row < 3, flow_ref[i], density + mine * pieces[index % 4])
-            index += 1
-
-
-def relay_kernel(parts_ref, shell_ref, out_ref, flow_ref, density_ref):
-    lane = lax.broadcasted_iota(jnp.int32, (8, 128), 1)
-    row = lax.broadcasted_iota(jnp.int32, (8, 128), 0)
-    pairs = []
-    for pair in range(4):
-        total = parts_ref[pair * 4]
-        for src in range(1, 4):
-            total += parts_ref[pair * 4 + src]
-        pairs.append(total)
-    flow = (pairs[0] + pairs[1]) + (pairs[2] + pairs[3])
-    flow_ref[...] = flow
-    density_ref[:, 0, :] = flow[3:6, 64:80]
-    places = shell_ref[...]
-    for half in range(2):
-        density = jnp.where(lane < 64, pairs[2 * half], pltpu.roll(pairs[2 * half + 1], 64, 1))
-        density = pltpu.roll(density, 5, 0)
-        place = pltpu.roll(places[:, 128 * half : 128 * half + 128], 3, 0)
-        tile = jnp.where(row < 3, density, place)
-        out_ref[:, :, 128 * half : 128 * half + 128] = jnp.broadcast_to(tile[None], (N_PLANE, 8, 128))
-
-
-def back_kernel(own_ref, plane_ref, flow_ref, out_ref, dist_ref, proj_ref, push_ref, place_ref):
-    for half in range(2):
-        tile = side_by_side(plane_ref, half * (N_PLANE // 2), N_PLANE // 2)
-        dist, proj, push, place = source_features(pltpu.roll(tile, 5, 0), tile)
-        dist_ref[32 * half : 32 * half + 32] = dist
-        proj_ref[32 * half : 32 * half + 32] = proj
-        push_ref[16 * half : 16 * half + 16] = push
-        place_ref[16 * half : 16 * half + 16] = place
-    back = pair_sums(
-        own_ref[0], SHELL // 2, dist_ref, proj_ref, push_ref, place_ref, 4, False, True
-    )
-    velocity = back + flow_ref[...]
-    out_ref[:, 0, :] = velocity[0:3, 0:64]
-    out_ref[:, 1, :] = velocity[0:3, 64:128]
+        done, count = 0, flow_ref.shape[0]
+        while done < count:
+            wide = min(4, count - done)
+            flow = pair_sums(
+                side_by_side(line_ref, index, wide),
+                BACK_SOURCES,
+                dist_ref,
+                proj_ref,
+                push_ref,
+                place_ref,
+                4,
+                0,
+            )
+            for i in range(wide):
+                mine = (pair_ref[0] == index // 4).astype(F32)
+                total = flow[:, 128 * i : 128 * i + 128] + flow_ref[done + i]
+                part_ref[index] = jnp.where(row < 3, total, mine * pieces[index % 4])
+                index += 1
+            done += wide
+
+
+def velocity_kernel(parts_ref, out_ref, density_ref):
+    total = total_of(parts_ref)
+    out_ref[:, 0, :] = total[0:3, 0:64]
+    out_ref[:, 1, :] = total[0:3, 64:128]
+    density_ref[:, 0, :] = total[3:6, 0:16]
 
 
 def tiles(count):
@@ -327,27 +323,40 @@
         "xaqcbn,cbn->xaq", shell_inverse, columns, preferred_element_type=F32
     )
     pair = lax.axis_index("tgt_2") * 2 + lax.axis_index("tgt_3")
-    message = pl.pallas_call(
-        message_kernel,
+    pair = pair.astype(jnp.int32).reshape(1)
+    scalar = pl.BlockSpec(memory_space=pltpu.SMEM)
+    vector = pl.BlockSpec(memory_space=pltpu.VMEM)
+    density_own = pl.pallas_call(
+        density_kernel,
+        out_shape=tiles(N_PLANE),
+        in_specs=[scalar, vector, vector],
+        compiler_params=params(2),
+    )(pair, density_rows, shell_places)
+    density_all = exchange_beside(density_own, PLANE)
+    part = pl.pallas_call(
+        back_kernel,
         out_shape=tiles(N_LINE),
-        in_specs=[pl.BlockSpec(memory_space=pltpu.SMEM)] + [pl.BlockSpec(memory_space=pltpu.VMEM)] * 3,
-        compiler_params=params(2),
-    )(pair.astype(jnp.int32).reshape(1), density_rows, *flows)
-    relay, fibre_flow, density = pl.pallas_call(
-        relay_kernel,
+        grid=(1,),
+        in_specs=[
+            scalar,
+            pl.BlockSpec((N_LINE, 8, 128), lambda i: (0, 0, 0)),
+            pl.BlockSpec((N_PLANE, 8, 128), lambda i: (0, 0, 0)),
+            pl.BlockSpec((1, 8, 128), lambda i: (0, 0, 0)),
+        ]
+        + [pl.BlockSpec(flow.shape, lambda i: (0, 0, 0)) for flow in flows],
+        out_specs=pl.BlockSpec((N_LINE, 8, 128), lambda i: (0, 0, 0)),
+        scratch_shapes=[pltpu.VMEM(s, t) for s, t in feature_shapes(BACK_SOURCES)],
+        compiler_params=params(24),
+        cost_estimate=cost(N_LINE * 128 * BACK_SOURCES),
+    )(pair, line, density_all, density_own, *flows)
+    velocity, density = pl.pallas_call(
+        velocity_kernel,
         out_shape=[
-            jax.ShapeDtypeStruct((N_PLANE, 8, 256), F32),
-            jax.ShapeDtypeStruct((8, 128), F32),
+            jax.ShapeDtypeStruct((3, 2, 64), F32),
             jax.ShapeDtypeStruct((3, 1, 16), F32),
         ],
         compiler_params=params(2),
-    )(exchange(message, LINE), shell_places)
-    velocity = pl.pallas_call(
-        back_kernel,
-        out_shape=jax.ShapeDtypeStruct((3, 2, 64), F32),
-        scratch_shapes=[pltpu.VMEM((2 * s[0], SHELL // 2), t) for s, t in feature_shapes(0)],
-        compiler_params=params(24),
-    )(own_line, exchange(relay, PLANE), fibre_flow)
+    )(exchange(part, LINE))
     return velocity, density
 
 

time: 118 us -> 117 us (level); the launches traced: 116 us -> 116 us
  blocking collectives: 56.1 us -> 38.9 us
  starting transfers between devices: 16.9 us -> 24.7 us
  waiting for transfers between devices: 6.25 us -> 12 us
  Pallas kernels: 32.2 us -> 36.1 us
    all_to_all x3 -> x2, blocking collectives: 56.1 us -> 38.9 us  [exchange(): return lax.all_to_all(x, axes, 0, 0, tiled=True)]
    all_to_all x3 -> x4, starting transfers between devices: 16.9 us -> 24.7 us  [exchange(): return lax.all_to_all(x, axes, 0, 0, tiled=True)]
    all_to_all x3 -> x4, waiting for transfers between devices: 6.25 us -> 12 us  [exchange(): return lax.all_to_all(x, axes, 0, 0, tiled=True)]
    pallas_call x3, Pallas kernels: 6.02 us -> 9.89 us  [the longest x1 8.48 us: per_device(): pl.pallas_call(back_kernel, out_shape=tiles(N_LINE), grid=(1,), in_specs=...]
    pallas_call x2 -> x3, Pallas kernels: 20.1 us -> 20.1 us  [fibre_chunk(): pl.pallas_call(functools.partial(fibre_kernel, first, widths), out_shape=...]
  transfers between devices with their start and end apart: 3 -> 4, of which waited for: 1 -> 3; matrix products, arithmetic and copies ran while one was open for 0% -> 0% of each run, Pallas kernels for 18% -> 18%
where the time goes in v4:
time: 117 us; the launch traced here: 116 us
  blocking collectives  38.9 us (33%)
  Pallas kernels  36.1 us (31%)
  starting transfers between devices  24.7 us (21%)
  waiting for transfers between devices  12 us (10%)
  local copies, waits for them, and re-layouts  2.64 us (2%)
    all_to_all x2, blocking collectives, exchange(): return lax.all_to_all(x, axes, 0, 0, tiled=True)  38.9 us
    all_to_all x4, starting transfers between devices, exchange(): return lax.all_to_all(x, axes, 0, 0, tiled=True)  24.7 us
    pallas_call x3, Pallas kernels, fibre_chunk(): pl.pallas_call(functools.partial(fibre_kernel, first, widths), out_shape=...  20.1 us
    all_to_all x4, waiting for transfers between devices, exchange(): return lax.all_to_all(x, axes, 0, 0, tiled=True)  12 us
    pallas_call x1, Pallas kernels, per_device(): pl.pallas_call(back_kernel, out_shape=tiles(N_LINE), grid=(1,), in_specs=...  8.48 us
    pallas_call x1, Pallas kernels, per_device(): pl.pallas_call(shell_kernel, out_shape=[tiles(N_LINE), jax.ShapeDtypeStru...  4.13 us
  transfers between devices with their start and end apart: 4, of which 3 were waited for; matrix products, arithmetic and copies ran while one was open for 0% of the time, Pallas kernels for 18%

profile of v4, /device:TPU:1, one launch (start us, length us, event | category | flops | bytes accessed | tf_op | source)
XLA Modules:
  0.0 116.0 jit_solution(14856287501043824309)
XLA Ops:
  0.6 0.0 copy-start
  0.6 0.0 copy-start.1
  0.7 0.8 copy-done.1
  1.5 0.0 copy-start.2
  1.5 0.7 copy-done.2
  2.2 0.7 shard_map.59
  2.9 22.7 %all_to_all.30.plane_ref = f32[32,8,128]{2,1,0:T(8,128)S(1)} all-to-all(f32[32,8,128]{2,1,0:T(8,128)S(1)} %get-tuple-element.26), channel_id=1, replica_groups=mesh['tgt_0'=4,'tgt_1'=8,'tgt_2'=2,'tgt_3'=2,'src'=4] {'tgt_0','tgt_1'}, dimensions={0} | all-to-all | bytes 262144 | tf_op jit(solution)/shard_map/all_to_all | solution.py:271
  25.5 9.2 %all-to-all-start.1 = ((f32[16,8,128]{2,1,0:T(8,128)}), f32[16,8,128]{2,1,0:T(8,128)S(1)}, u32[]{:S(2)}, u32[]{:S(2)}) async-start(f32[16,8,128]{2,1,0:T(8,128)} %get-tuple-element.27), calls=%async_computation.1 | async-start | bytes 131072 | tf_op jit(solution)/shard_map/all_to_all | solution.py:271
  34.7 0.0 copy-start.3
  34.7 0.8 copy-done.3
  35.5 0.6 shard_map.60
  36.1 6.2 %all-to-all-done.1.line_ref = f32[16,8,128]{2,1,0:T(8,128)S(1)} async-done(((f32[16,8,128]{2,1,0:T(8,128)}), f32[16,8,128]{2,1,0:T(8,128)S(1)}, u32[]{:S(2)}, u32[]{:S(2)}) %all-to-all-start.1) | async-done | bytes 65568 | tf_op jit(solution)/shard_map/all_to_all | solution.py:271
  42.3 4.1 %shard_map.61 = (f32[16,8,128]{2,1,0:T(8,128)}, f32[8,256]{1,0:T(8,128)S(1)}) custom-call(f32[16,8,128]{2,1,0:T(8,128)S(1)} %all-to-all-done.1.line_ref, bf16[32,4096]{1,0:T(8,128)(2,1)S(1)} %get-tuple-element.33.dist_ref, bf16[32,4096]{1,0:T(8,128)(2,1)S(1)} %get-tuple-element.34.proj_ref, bf16[16,4096]{1,0:T(8,128)(2,1)S(1)} %get-tuple-element.35.push_ref, ...), custom_call_target="tpu_custom_call" | custom-call | flops 419430400 | bytes 1048576 | tf_op jit(solution)/shard_map/pallas_call | solution.py:288
  46.4 3.7 %all-to-all-start.2 = ((f32[16,8,128]{2,1,0:T(8,128)}), f32[16,8,128]{2,1,0:T(8,128)S(1)}, u32[]{:S(2)}, u32[]{:S(2)}) async-start(f32[16,8,128]{2,1,0:T(8,128)} %get-tuple-element.37), calls=%async_computation.2 | async-start | bytes 131072 | tf_op jit(solution)/shard_map/all_to_all | solution.py:271
  50.1 7.7 %shard_map.62.refs_0_ = f32[6,8,128]{2,1,0:T(8,128)S(1)} custom-call(f32[16,8,128]{2,1,0:T(8,128)S(1)} %all-to-all-done.1.line_ref, bf16[32,4096]{1,0:T(8,128)(2,1)S(1)} %get-tuple-element.33.dist_ref, bf16[32,4096]{1,0:T(8,128)(2,1)S(1)} %get-tuple-element.34.proj_ref, bf16[16,4096]{1,0:T(8,128)(2,1)S(1)} %get-tuple-element.35.push_ref, ...), custom_call_target="tpu_custom_call" | custom-call | flops 1258291200 | bytes 1048576 | tf_op jit(solution)/shard_map/pallas_call | solution.py:298
  57.8 0.0 all-to-all-done.2.parts_ref
  57.8 0.7 shard_map.63
  58.5 3.8 %all-to-all-start.3 = ((bf16[32,16,128]{2,1,0:T(8,128)(2,1)}), bf16[32,16,128]{2,1,0:T(8,128)(2,1)S(1)}, u32[]{:S(2)}, u32[]{:S(2)}) async-start(bf16[32,16,128]{2,1,0:T(8,128)(2,1)} %shard_map.63), calls=%async_computation.3 | async-start | bytes 262144 | tf_op jit(solution)/shard_map/all_to_all | solution.py:271
  62.4 7.7 %shard_map.64.refs_1_ = f32[6,8,128]{2,1,0:T(8,128)S(1)} custom-call(f32[16,8,128]{2,1,0:T(8,128)S(1)} %all-to-all-done.1.line_ref, bf16[32,4096]{1,0:T(8,128)(2,1)S(1)} %get-tuple-element.33.dist_ref, bf16[32,4096]{1,0:T(8,128)(2,1)S(1)} %get-tuple-element.34.proj_ref, bf16[16,4096]{1,0:T(8,128)(2,1)S(1)} %get-tuple-element.35.push_ref, ...), custom_call_target="tpu_custom_call" | custom-call | flops 1258291200 | bytes 1048576 | tf_op jit(solution)/shard_map/pallas_call | solution.py:298
  70.1 1.5 %all-to-all-done.3 = bf16[32,16,128]{2,1,0:T(8,128)(2,1)S(1)} async-done(((bf16[32,16,128]{2,1,0:T(8,128)(2,1)}), bf16[32,16,128]{2,1,0:T(8,128)(2,1)S(1)}, u32[]{:S(2)}, u32[]{:S(2)}) %all-to-all-start.3) | async-done | bytes 131104 | tf_op jit(solution)/shard_map/all_to_all | solution.py:271
  71.5 0.1 copy.6
  71.6 0.1 copy.7
  71.8 0.1 copy.8
  71.9 0.0 copy-done
  71.9 0.9 fusion
  72.8 0.7 shard_map.65.own_ref
  73.6 8.0 %all-to-all-start.4 = ((f32[32,8,128]{2,1,0:T(8,128)}), f32[32,8,128]{2,1,0:T(8,128)S(1)}, u32[]{:S(2)}, u32[]{:S(2)}) async-start(f32[32,8,128]{2,1,0:T(8,128)} %shard_map.65.own_ref), calls=%async_computation.4 | async-start | bytes 262144 | tf_op jit(solution)/shard_map/all_to_all | solution.py:271
  81.6 4.7 %shard_map.66.refs_2_ = f32[4,8,128]{2,1,0:T(8,128)S(1)} custom-call(f32[16,8,128]{2,1,0:T(8,128)S(1)} %all-to-all-done.1.line_ref, bf16[32,4096]{1,0:T(8,128)(2,1)S(1)} %get-tuple-element.33.dist_ref, bf16[32,4096]{1,0:T(8,128)(2,1)S(1)} %get-tuple-element.34.proj_ref, bf16[16,4096]{1,0:T(8,128)(2,1)S(1)} %get-tuple-element.35.push_ref, ...), custom_call_target="tpu_custom_call" | custom-call | flops 838860800 | bytes 1048576 | tf_op jit(solution)/shard_map/pallas_call | solution.py:298
  86.3 4.3 %all-to-all-done.4.plane_ref = f32[32,8,128]{2,1,0:T(8,128)S(1)} async-done(((f32[32,8,128]{2,1,0:T(8,128)}), f32[32,8,128]{2,1,0:T(8,128)S(1)}, u32[]{:S(2)}, u32[]{:S(2)}) %all-to-all-start.4) | async-done | bytes 131104 | tf_op jit(solution)/shard_map/all_to_all | solution.py:271
  90.6 8.5 %shard_map.67 = f32[16,8,128]{2,1,0:T(8,128)S(1)} custom-call(s32[1]{0:T(128)} %bitcast.pair_ref, f32[16,8,128]{2,1,0:T(8,128)S(1)} %all-to-all-done.1.line_ref, f32[32,8,128]{2,1,0:T(8,128)S(1)} %all-to-all-done.4.plane_ref, f32[32,8,128]{2,1,0:T(8,128)} %shard_map.65.own_ref, f32[6,8,128]{2,1,0:T(8,128)S(1)} %shard_map.62.refs_0_, ...), custom_call_target="tpu_custom_call" | custom-call | flops 1677721600 | bytes 1048576 | tf_op jit(solution)/shard_map/pallas_call | solution.py:336
  99.1 16.2 %all_to_all.31.parts_ref = f32[16,8,128]{2,1,0:T(8,128)S(1)} all-to-all(f32[16,8,128]{2,1,0:T(8,128)S(1)} %shard_map.67), channel_id=1, replica_groups=mesh['tgt_0'=4,'tgt_1'=8,'tgt_2'=2,'tgt_3'=2,'src'=4] {'tgt_2','tgt_3','..., dimensions={0} | all-to-all | bytes 131072 | tf_op jit(solution)/shard_map/all_to_all | solution.py:271
  115.3 0.7 shard_map.68
  (3 shorter events, 0.0 us)
Async XLA Ops:
  0.6 71.3 %copy-start = (bf16[3,1,64,3,16,128]{5,4,3,2,1,0:T(8,128)(2,1)S(1)}, bf16[3,1,64,3,16,128]{5,4,3,2,1,0:T(8,128)(2,1)}, u32[]{:S(2)}) copy-start(bf16[3,1,64,3,16,128]{5,4,3,2,1,0:T(8,128)(2,1)} %param.7) | copy-start | bytes 7077892
  0.6 0.8 copy-start.1
  1.5 0.7 copy-start.2
  25.5 16.8 %all-to-all-start.1 = ((f32[16,8,128]{2,1,0:T(8,128)}), f32[16,8,128]{2,1,0:T(8,128)S(1)}, u32[]{:S(2)}, u32[]{:S(2)}) async-start(f32[16,8,128]{2,1,0:T(8,128)} %get-tuple-element.27), calls=%async_computation.1 | async-start | bytes 131072 | tf_op jit(solution)/shard_map/all_to_all | solution.py:271
  34.7 0.8 copy-start.3
  46.4 11.4 %all-to-all-start.2 = ((f32[16,8,128]{2,1,0:T(8,128)}), f32[16,8,128]{2,1,0:T(8,128)S(1)}, u32[]{:S(2)}, u32[]{:S(2)}) async-start(f32[16,8,128]{2,1,0:T(8,128)} %get-tuple-element.37), calls=%async_computation.2 | async-start | bytes 131072 | tf_op jit(solution)/shard_map/all_to_all | solution.py:271
  58.5 13.0 %all-to-all-start.3 = ((bf16[32,16,128]{2,1,0:T(8,128)(2,1)}), bf16[32,16,128]{2,1,0:T(8,128)(2,1)S(1)}, u32[]{:S(2)}, u32[]{:S(2)}) async-start(bf16[32,16,128]{2,1,0:T(8,128)(2,1)} %shard_map.63), calls=%async_computation.3 | async-start | bytes 262144 | tf_op jit(solution)/shard_map/all_to_all | solution.py:271
  73.6 17.0 %all-to-all-start.4 = ((f32[32,8,128]{2,1,0:T(8,128)}), f32[32,8,128]{2,1,0:T(8,128)S(1)}, u32[]{:S(2)}, u32[]{:S(2)}) async-start(f32[32,8,128]{2,1,0:T(8,128)} %shard_map.65.own_ref), calls=%async_computation.4 | async-start | bytes 262144 | tf_op jit(solution)/shard_map/all_to_all | solution.py:271

commit v5 on v4

--- a/solution.py
+++ b/solution.py
@@ -17,7 +17,7 @@
 N_PLANE = 32
 SOURCES = N_PLANE * 128
 BACK_SOURCES = N_PLANE * 64
-CHUNKS = ((0, (512, 256)), (6, (512, 256)), (12, (512,)))
+CHUNKS = ((0, (512,)), (4, (768,)), (10, (768,)))
 STEP = 512
 ROWS = (((0,), (0,)), ((), ()))
 
@@ -171,7 +171,7 @@
             push_ref,
             place_ref,
             4,
-            1,
+            0,
         )
         for i in range(count):
             flow_ref[done + i] = flow[:, 128 * i : 128 * i + 128]
@@ -187,13 +187,37 @@
 
 def columns_kernel(parts_ref, out_ref):
     total = total_of(parts_ref)
-    total = jnp.concatenate([total, jnp.zeros_like(total)], axis=0).astype(BF16)
+    total = total.astype(BF16).astype(F32)
     out_ref[...] = jnp.broadcast_to(total[None], out_ref.shape)
 
 
-def density_kernel(pair_ref, density_ref, shell_ref, out_ref):
-    density = jnp.concatenate([density_ref[:, 0, :], jnp.zeros((3, 64), F32)], axis=1)
-    density = jnp.concatenate([density, jnp.zeros((5, 128), F32)], axis=0)
+def density_kernel(pair_ref, columns_ref, inverse_ref, shell_ref, out_ref):
+    columns = jnp.concatenate([columns_ref[:, c, :] for c in range(3)], axis=1).astype(BF16)
+    here = lax.broadcasted_iota(jnp.int32, (N_PLANE, 512), 0)
+    there = lax.broadcasted_iota(jnp.int32, (N_PLANE, 512), 1)
+    pick = (there % 128 == 4 * here + there // 128).astype(F32).astype(BF16)
+    spread = lax.dot_general(columns, pick, ROWS, preferred_element_type=F32)
+    parts = []
+    for c in range(3):
+        part = jnp.zeros((16, 128), F32)
+        for pair in range(4):
+            first = 128 * c + 16 * pair
+            part += spread[first : first + 16, 128 * pair : 128 * pair + 128]
+        parts.append(part)
+    ones = jnp.ones((8, 128), F32)
+    row = lax.broadcasted_iota(jnp.int32, (8, 64), 0)
+    density = jnp.zeros((8, 64), F32)
+    for x in range(3):
+        total = jnp.zeros((64, 8, 128), F32)
+        for c in range(3):
+            block = inverse_ref[x, 0, :, c].astype(F32) * parts[c][None]
+            total += block[:, 0:8] + block[:, 8:16]
+        sums = jnp.sum(total, axis=1)
+        line = lax.dot_general(
+            ones, sums, (((1,), (1,)), ((), ())), precision=lax.Precision.HIGHEST, preferred_element_type=F32
+        )
+        density -= jnp.where(row == x, line, 0.0)
+    density = jnp.concatenate([density, jnp.zeros((8, 64), F32)], axis=1)
     lane = lax.broadcasted_iota(jnp.int32, density.shape, 1)
     places = jnp.zeros_like(density)
     for pair in range(4):
@@ -225,7 +249,7 @@
     for flow_ref in flows:
         done, count = 0, flow_ref.shape[0]
         while done < count:
-            wide = min(4, count - done)
+            wide = 6 if count % 6 == 0 else 4
             flow = pair_sums(
                 side_by_side(line_ref, index, wide),
                 BACK_SOURCES,
@@ -273,7 +297,7 @@
 
 def per_device(fibre_points, shell_points, bending, shell_inverse):
     own_line, own_plane = pl.pallas_call(
-        own_kernel, out_shape=[tiles(N_LINE), tiles(N_PLANE)], compiler_params=params(2)
+        own_kernel, out_shape=[tiles(N_LINE), tiles(N_PLANE)], compiler_params=params(62)
     )(fibre_points, shell_points)
     plane = exchange(own_plane, PLANE)
     own_line, _ = lax.optimization_barrier((own_line, plane))
@@ -313,15 +337,10 @@
     shell_parts = exchange_beside(shell_part, LINE)
     shell_own = pl.pallas_call(
         columns_kernel,
-        out_shape=jax.ShapeDtypeStruct((N_PLANE, 16, 128), BF16),
+        out_shape=tiles(N_PLANE),
         compiler_params=params(2),
     )(shell_parts)
     shell_all = exchange_beside(shell_own, PLANE)
-    columns = shell_all[:, :3, :64].reshape(N_PLANE, 3, 4, 16)
-    columns = columns.transpose(1, 3, 0, 2).reshape(3, 16, 128)
-    density_rows = -jnp.einsum(
-        "xaqcbn,cbn->xaq", shell_inverse, columns, preferred_element_type=F32
-    )
     pair = lax.axis_index("tgt_2") * 2 + lax.axis_index("tgt_3")
     pair = pair.astype(jnp.int32).reshape(1)
     scalar = pl.BlockSpec(memory_space=pltpu.SMEM)
@@ -329,9 +348,9 @@
     density_own = pl.pallas_call(
         density_kernel,
         out_shape=tiles(N_PLANE),
-        in_specs=[scalar, vector, vector],
-        compiler_params=params(2),
-    )(pair, density_rows, shell_places)
+        in_specs=[scalar, vector, vector, vector],
+        compiler_params=params(12),
+    )(pair, shell_all, shell_inverse, shell_places)
     density_all = exchange_beside(density_own, PLANE)
     part = pl.pallas_call(
         back_kernel,

time: 117 us -> 110 us (0.940)
  waiting for transfers between devices: 12 us -> 17.1 us
  blocking collectives: 38.9 us -> 35.3 us
  Pallas kernels: 36.1 us -> 32.7 us
  starting transfers between devices: 24.7 us -> 22.5 us
  local copies, waits for them, and re-layouts: 2.64 us -> 0.76 us
    pallas_call x3, Pallas kernels: 20.1 us -> 14.8 us  [fibre_chunk(): pl.pallas_call(functools.partial(fibre_kernel, first, widths), out_shape=...]
    all_to_all x4, waiting for transfers between devices: 12 us -> 17.1 us  [exchange(): return lax.all_to_all(x, axes, 0, 0, tiled=True)]
    all_to_all x2, blocking collectives: 38.9 us -> 35.3 us  [exchange(): return lax.all_to_all(x, axes, 0, 0, tiled=True)]
    all_to_all x4, starting transfers between devices: 24.7 us -> 22.5 us  [exchange(): return lax.all_to_all(x, axes, 0, 0, tiled=True)]
    unnamed x8 -> x4, local copies, waits for them, and re-layouts: 2.28 us -> 0.76 us
  transfers between devices with their start and end apart: 4 -> 4, of which waited for: 3 -> 4; matrix products, arithmetic and copies ran while one was open for 0% -> 0% of each run, Pallas kernels for 18% -> 14%
where the time goes in v5:
time: 110 us; the launch traced here: 109 us
  blocking collectives  35.3 us (32%)
  Pallas kernels  32.7 us (30%)
  starting transfers between devices  22.5 us (20%)
  waiting for transfers between devices  17.1 us (16%)
    all_to_all x2, blocking collectives, exchange(): return lax.all_to_all(x, axes, 0, 0, tiled=True)  35.3 us
    all_to_all x4, starting transfers between devices, exchange(): return lax.all_to_all(x, axes, 0, 0, tiled=True)  22.5 us
    all_to_all x4, waiting for transfers between devices, exchange(): return lax.all_to_all(x, axes, 0, 0, tiled=True)  17.1 us
    pallas_call x3, Pallas kernels, fibre_chunk(): pl.pallas_call(functools.partial(fibre_kernel, first, widths), out_shape=...  14.8 us
    pallas_call x1, Pallas kernels, per_device(): pl.pallas_call(back_kernel, out_shape=tiles(N_LINE), grid=(1,), in_specs=...  8.61 us
    pallas_call x1, Pallas kernels, per_device(): pl.pallas_call(shell_kernel, out_shape=[tiles(N_LINE), jax.ShapeDtypeStru...  4.14 us
  transfers between devices with their start and end apart: 4, of which 4 were waited for; matrix products, arithmetic and copies ran while one was open for 0% of the time, Pallas kernels for 14%

profile of v5, /device:TPU:1, one launch (start us, length us, event | category | flops | bytes accessed | tf_op | source)
XLA Modules:
  0.0 109.1 jit_solution(765189895922510223)
XLA Ops:
  0.6 1.5 %shard_map.59 = (f32[16,8,128]{2,1,0:T(8,128)}, f32[32,8,128]{2,1,0:T(8,128)}) custom-call(f32[3,2,64]{2,1,0:T(2,128)} %fibre_ref.1, f32[3,1,16]{2,1,0:T(1,128)} %shell_ref.1), custom_call_target="tpu_custom_call" | custom-call | tf_op jit(solution)/shard_map/pallas_call | solution.py:299
  2.1 22.9 %all_to_all.30.plane_ref = f32[32,8,128]{2,1,0:T(8,128)S(1)} all-to-all(f32[32,8,128]{2,1,0:T(8,128)} %get-tuple-element.26), channel_id=1, replica_groups=mesh['tgt_0'=4,'tgt_1'=8,'tgt_2'=2,'tgt_3'=2,'src'=4] {'tgt_0','tgt_1'}, dimensions={0} | all-to-all | bytes 262144 | tf_op jit(solution)/shard_map/all_to_all | solution.py:295
  25.0 9.2 %all-to-all-start.1 = ((f32[16,8,128]{2,1,0:T(8,128)}), f32[16,8,128]{2,1,0:T(8,128)S(1)}, u32[]{:S(2)}, u32[]{:S(2)}) async-start(f32[16,8,128]{2,1,0:T(8,128)} %get-tuple-element.27), calls=%async_computation.1 | async-start | bytes 131072 | tf_op jit(solution)/shard_map/all_to_all | solution.py:295
  34.1 0.0 copy-start.1
  34.1 0.8 copy-done.1
  34.9 0.6 shard_map.60
  35.5 6.2 %all-to-all-done.1.line_ref = f32[16,8,128]{2,1,0:T(8,128)S(1)} async-done(((f32[16,8,128]{2,1,0:T(8,128)}), f32[16,8,128]{2,1,0:T(8,128)S(1)}, u32[]{:S(2)}, u32[]{:S(2)}) %all-to-all-start.1) | async-done | bytes 65568 | tf_op jit(solution)/shard_map/all_to_all | solution.py:295
  41.7 4.1 %shard_map.61 = (f32[16,8,128]{2,1,0:T(8,128)}, f32[8,256]{1,0:T(8,128)S(1)}) custom-call(f32[16,8,128]{2,1,0:T(8,128)S(1)} %all-to-all-done.1.line_ref, bf16[32,4096]{1,0:T(8,128)(2,1)S(1)} %get-tuple-element.33.dist_ref, bf16[32,4096]{1,0:T(8,128)(2,1)S(1)} %get-tuple-element.34.proj_ref, bf16[16,4096]{1,0:T(8,128)(2,1)S(1)} %get-tuple-element.35.push_ref, ...), custom_call_target="tpu_custom_call" | custom-call | flops 419430400 | bytes 1048576 | tf_op jit(solution)/shard_map/pallas_call | solution.py:312
  45.9 3.7 %all-to-all-start.2 = ((f32[16,8,128]{2,1,0:T(8,128)}), f32[16,8,128]{2,1,0:T(8,128)S(1)}, u32[]{:S(2)}, u32[]{:S(2)}) async-start(f32[16,8,128]{2,1,0:T(8,128)} %get-tuple-element.37), calls=%async_computation.2 | async-start | bytes 131072 | tf_op jit(solution)/shard_map/all_to_all | solution.py:295
  49.6 3.7 %shard_map.62.refs_0_ = f32[4,8,128]{2,1,0:T(8,128)S(1)} custom-call(f32[16,8,128]{2,1,0:T(8,128)S(1)} %all-to-all-done.1.line_ref, bf16[32,4096]{1,0:T(8,128)(2,1)S(1)} %get-tuple-element.33.dist_ref, bf16[32,4096]{1,0:T(8,128)(2,1)S(1)} %get-tuple-element.34.proj_ref, bf16[16,4096]{1,0:T(8,128)(2,1)S(1)} %get-tuple-element.35.push_ref, ...), custom_call_target="tpu_custom_call" | custom-call | flops 838860800 | bytes 1048576 | tf_op jit(solution)/shard_map/pallas_call | solution.py:322
  53.3 3.9 %all-to-all-done.2.parts_ref = f32[16,8,128]{2,1,0:T(8,128)S(1)} async-done(((f32[16,8,128]{2,1,0:T(8,128)}), f32[16,8,128]{2,1,0:T(8,128)S(1)}, u32[]{:S(2)}, u32[]{:S(2)}) %all-to-all-start.2) | async-done | bytes 65568 | tf_op jit(solution)/shard_map/all_to_all | solution.py:295
  57.1 0.7 shard_map.63
  57.8 3.8 %all-to-all-start.3 = ((f32[32,8,128]{2,1,0:T(8,128)}), f32[32,8,128]{2,1,0:T(8,128)S(1)}, u32[]{:S(2)}, u32[]{:S(2)}) async-start(f32[32,8,128]{2,1,0:T(8,128)} %shard_map.63), calls=%async_computation.3 | async-start | bytes 262144 | tf_op jit(solution)/shard_map/all_to_all | solution.py:295
  61.7 0.0 copy-start
  61.7 5.5 %shard_map.64.refs_1_ = f32[6,8,128]{2,1,0:T(8,128)S(1)} custom-call(f32[16,8,128]{2,1,0:T(8,128)S(1)} %all-to-all-done.1.line_ref, bf16[32,4096]{1,0:T(8,128)(2,1)S(1)} %get-tuple-element.33.dist_ref, bf16[32,4096]{1,0:T(8,128)(2,1)S(1)} %get-tuple-element.34.proj_ref, bf16[16,4096]{1,0:T(8,128)(2,1)S(1)} %get-tuple-element.35.push_ref, ...), custom_call_target="tpu_custom_call" | custom-call | flops 1258291200 | bytes 1048576 | tf_op jit(solution)/shard_map/pallas_call | solution.py:322
  67.2 3.6 %all-to-all-done.3.columns_ref = f32[32,8,128]{2,1,0:T(8,128)S(1)} async-done(((f32[32,8,128]{2,1,0:T(8,128)}), f32[32,8,128]{2,1,0:T(8,128)S(1)}, u32[]{:S(2)}, u32[]{:S(2)}) %all-to-all-start.3) | async-done | bytes 131104 | tf_op jit(solution)/shard_map/all_to_all | solution.py:295
  70.8 0.0 copy-done
  70.8 1.8 %shard_map.65.own_ref = f32[32,8,128]{2,1,0:T(8,128)} custom-call(s32[1]{0:T(128)} %bitcast.pair_ref, f32[32,8,128]{2,1,0:T(8,128)S(1)} %all-to-all-done.3.columns_ref, bf16[3,1,64,3,16,128]{5,4,3,2,1,0:T(8,128)(2,1)S(1)} %copy-done, f32[8,256]{1,0:T(8,128)S(1)} %get-tuple-element.42.shell_ref), custom_call_target="tpu_custom_call" | custom-call | tf_op jit(solution)/shard_map/pallas_call | solution.py:348
  72.6 5.8 %all-to-all-start.4 = ((f32[32,8,128]{2,1,0:T(8,128)}), f32[32,8,128]{2,1,0:T(8,128)S(1)}, u32[]{:S(2)}, u32[]{:S(2)}) async-start(f32[32,8,128]{2,1,0:T(8,128)} %shard_map.65.own_ref), calls=%async_computation.4 | async-start | bytes 262144 | tf_op jit(solution)/shard_map/all_to_all | solution.py:295
  78.4 5.5 %shard_map.66.refs_2_ = f32[6,8,128]{2,1,0:T(8,128)S(1)} custom-call(f32[16,8,128]{2,1,0:T(8,128)S(1)} %all-to-all-done.1.line_ref, bf16[32,4096]{1,0:T(8,128)(2,1)S(1)} %get-tuple-element.33.dist_ref, bf16[32,4096]{1,0:T(8,128)(2,1)S(1)} %get-tuple-element.34.proj_ref, bf16[16,4096]{1,0:T(8,128)(2,1)S(1)} %get-tuple-element.35.push_ref, ...), custom_call_target="tpu_custom_call" | custom-call | flops 1258291200 | bytes 1048576 | tf_op jit(solution)/shard_map/pallas_call | solution.py:322
  84.0 3.4 %all-to-all-done.4.plane_ref = f32[32,8,128]{2,1,0:T(8,128)S(1)} async-done(((f32[32,8,128]{2,1,0:T(8,128)}), f32[32,8,128]{2,1,0:T(8,128)S(1)}, u32[]{:S(2)}, u32[]{:S(2)}) %all-to-all-start.4) | async-done | bytes 131104 | tf_op jit(solution)/shard_map/all_to_all | solution.py:295
  87.4 8.6 %shard_map.67 = f32[16,8,128]{2,1,0:T(8,128)S(1)} custom-call(s32[1]{0:T(128)} %bitcast.pair_ref, f32[16,8,128]{2,1,0:T(8,128)S(1)} %all-to-all-done.1.line_ref, f32[32,8,128]{2,1,0:T(8,128)S(1)} %all-to-all-done.4.plane_ref, f32[32,8,128]{2,1,0:T(8,128)} %shard_map.65.own_ref, f32[4,8,128]{2,1,0:T(8,128)S(1)} %shard_map.62.refs_0_, ...), custom_call_target="tpu_custom_call" | custom-call | flops 1677721600 | bytes 1048576 | tf_op jit(solution)/shard_map/pallas_call | solution.py:355
  96.0 12.4 %all_to_all.31.parts_ref = f32[16,8,128]{2,1,0:T(8,128)S(1)} all-to-all(f32[16,8,128]{2,1,0:T(8,128)S(1)} %shard_map.67), channel_id=1, replica_groups=mesh['tgt_0'=4,'tgt_1'=8,'tgt_2'=2,'tgt_3'=2,'src'=4] {'tgt_2','tgt_3','..., dimensions={0} | all-to-all | bytes 131072 | tf_op jit(solution)/shard_map/all_to_all | solution.py:295
  108.5 0.7 shard_map.68
Async XLA Ops:
  25.0 16.8 %all-to-all-start.1 = ((f32[16,8,128]{2,1,0:T(8,128)}), f32[16,8,128]{2,1,0:T(8,128)S(1)}, u32[]{:S(2)}, u32[]{:S(2)}) async-start(f32[16,8,128]{2,1,0:T(8,128)} %get-tuple-element.27), calls=%async_computation.1 | async-start | bytes 131072 | tf_op jit(solution)/shard_map/all_to_all | solution.py:295
  34.1 0.8 copy-start.1
  45.9 11.3 %all-to-all-start.2 = ((f32[16,8,128]{2,1,0:T(8,128)}), f32[16,8,128]{2,1,0:T(8,128)S(1)}, u32[]{:S(2)}, u32[]{:S(2)}) async-start(f32[16,8,128]{2,1,0:T(8,128)} %get-tuple-element.37), calls=%async_computation.2 | async-start | bytes 131072 | tf_op jit(solution)/shard_map/all_to_all | solution.py:295
  57.8 13.0 %all-to-all-start.3 = ((f32[32,8,128]{2,1,0:T(8,128)}), f32[32,8,128]{2,1,0:T(8,128)S(1)}, u32[]{:S(2)}, u32[]{:S(2)}) async-start(f32[32,8,128]{2,1,0:T(8,128)} %shard_map.63), calls=%async_computation.3 | async-start | bytes 262144 | tf_op jit(solution)/shard_map/all_to_all | solution.py:295
  61.7 9.1 %copy-start = (bf16[3,1,64,3,16,128]{5,4,3,2,1,0:T(8,128)(2,1)S(1)}, bf16[3,1,64,3,16,128]{5,4,3,2,1,0:T(8,128)(2,1)}, u32[]{:S(2)}) copy-start(bf16[3,1,64,3,16,128]{5,4,3,2,1,0:T(8,128)(2,1)} %inverse_ref.1) | copy-start | bytes 7077892
  72.6 14.8 %all-to-all-start.4 = ((f32[32,8,128]{2,1,0:T(8,128)}), f32[32,8,128]{2,1,0:T(8,128)S(1)}, u32[]{:S(2)}, u32[]{:S(2)}) async-start(f32[32,8,128]{2,1,0:T(8,128)} %shard_map.65.own_ref), calls=%async_computation.4 | async-start | bytes 262144 | tf_op jit(solution)/shard_map/all_to_all | solution.py:295

commit v6 on v5

--- a/solution.py
+++ b/solution.py
@@ -17,8 +17,7 @@
 N_PLANE = 32
 SOURCES = N_PLANE * 128
 BACK_SOURCES = N_PLANE * 64
-CHUNKS = ((0, (512,)), (4, (768,)), (10, (768,)))
-STEP = 512
+CHUNKS = ((0, (512, 512)), (8, (512, 512)))
 ROWS = (((0,), (0,)), ((), ()))
 
 F32 = jnp.float32
@@ -59,51 +58,56 @@
 
 def source_features(places, pushes):
     row = rows_of(places)
-    places = jnp.where(row < 3, places * scale, 0.0)
+    center = jnp.mean(places, axis=1, keepdims=True)
+    places = jnp.where(row < 3, (places - center) * scale, 0.0)
     pushes = jnp.where(row < 3, pushes, 0.0)
     square = jnp.sum(places * places, axis=0, keepdims=True)
     along = jnp.sum(places * pushes, axis=0, keepdims=True)
     a, b, _ = three_parts(pushes)
     push_rows = jnp.concatenate([a, b], axis=0).astype(BF16)
-    a, b, c = three_parts(jnp.where(row == 3, 1.0, places))
-    place_rows = jnp.concatenate([a, b + pltpu.roll(c, 4, 0)], axis=0).astype(BF16)
-    return right_rows(-2.0 * places, 1.0, square), right_rows(pushes, 0.0, -along), push_rows, place_rows
-
-
-def pair_sums(targets, count, dist_ref, proj_ref, push_ref, place_ref, unroll, level):
+    y, g = places[0:3], pushes[0:3]
+    form = jnp.concatenate(
+        [g, along, along * y, g[2:3] * y[2:3], g[0:1] * y, g[1:2] * y, g[2:3] * y[0:2]], axis=0
+    )
+    form_rows = jnp.concatenate(three_parts(form), axis=0).astype(BF16)
+    center = jnp.broadcast_to(center, (8, 128))
+    return right_rows(-2.0 * places, 1.0, square), push_rows, form_rows, center
+
+
+def pair_sums(targets, count, dist_ref, push_ref, form_ref, center_ref, step, unroll, fine):
     row = rows_of(targets)
-    x = jnp.where(row < 3, targets * scale, 0.0)
+    x = jnp.where(row < 3, (targets - center_ref[:, 0:1]) * scale, 0.0)
     square = jnp.sum(x * x, axis=0, keepdims=True) + 1.0
     features = left_rows(x, square)
     width = features.shape[1]
-    step = min(STEP, count)
 
     def add_block(k, sums):
-        diag_sum, proj_sum = sums
+        root_sum, cube_sum = sums
         part = pl.ds(pl.multiple_of(k * step, step), step)
         dist_sq = lax.dot_general(dist_ref[:, part], features, ROWS, preferred_element_type=F32)
-        along = lax.dot_general(proj_ref[:, part], features, ROWS, preferred_element_type=F32)
-        inv_root = lax.rsqrt(dist_sq)
-        inv_cubed = inv_root * inv_root * inv_root
-        diag = inv_root + inv_cubed
-        high = diag.astype(BF16)
-        diag_sum += jnp.dot(push_ref[:, part], high, preferred_element_type=F32)
-        if level > 0:
-            low = (diag - high.astype(F32)).astype(BF16)
-            diag_sum += jnp.dot(push_ref[:, part], low, preferred_element_type=F32)
-        proj = along * inv_cubed
-        high = proj.astype(BF16)
-        proj_sum += jnp.dot(place_ref[:, part], high, preferred_element_type=F32)
-        if level > 1:
-            low = (proj - high.astype(F32)).astype(BF16)
-            proj_sum += jnp.dot(place_ref[:, part], low, preferred_element_type=F32)
-        return diag_sum, proj_sum
-
-    start = (jnp.zeros((16, width), F32), jnp.zeros((16, width), F32))
-    diag_sum, proj_sum = lax.fori_loop(0, count // step, add_block, start, unroll=unroll)
-    rest = proj_sum[8:16]
-    moved = proj_sum[0:8] + rest + pltpu.roll(rest, 4, 0)
-    return (diag_sum[0:8] + diag_sum[8:16] + x * moved[3:4] - moved) * mobility
+        root = lax.rsqrt(dist_sq)
+        high = root.astype(BF16)
+        root_sum += jnp.dot(push_ref[:, part], high, preferred_element_type=F32)
+        if fine:
+            low = (root - high.astype(F32)).astype(BF16)
+            root_sum += jnp.dot(push_ref[:, part], low, preferred_element_type=F32)
+        cube = root * root * root
+        high = cube.astype(BF16)
+        cube_sum += jnp.dot(form_ref[:, part], high, preferred_element_type=F32)
+        if fine:
+            low = (cube - high.astype(F32)).astype(BF16)
+            cube_sum += jnp.dot(form_ref[:, part], low, preferred_element_type=F32)
+        return root_sum, cube_sum
+
+    start = (jnp.zeros((16, width), F32), jnp.zeros((48, width), F32))
+    root_sum, cube_sum = lax.fori_loop(0, count // step, add_block, start, unroll=unroll)
+    form = cube_sum[0:16] + cube_sum[16:32] + cube_sum[32:48]
+    x0, x1, x2 = x[0:1], x[1:2], x[2:3]
+    pull = x0 * form[0:1] + x1 * form[1:2] + x2 * form[2:3] - form[3:4]
+    last = jnp.concatenate([form[14:16], form[7:8]], axis=0)
+    moved = x0 * form[8:11] + x1 * form[11:14] + x2 * last - form[4:7]
+    flow = root_sum[0:3] + root_sum[8:11] + form[0:3] + (x[0:3] * pull - moved)
+    return jnp.concatenate([flow * mobility, jnp.zeros((5, width), F32)], axis=0)
 
 
 def side_by_side(ref, first, count):
@@ -132,7 +136,7 @@
     plane_ref[...] = jnp.broadcast_to(tile[None], plane_ref.shape)
 
 
-def source_kernel(plane_ref, bending_ref, dist_ref, proj_ref, push_ref, place_ref):
+def source_kernel(plane_ref, bending_ref, dist_ref, push_ref, form_ref, center_ref):
     square = bending_ref[...]
     zero = jnp.zeros_like(square)
     both = jnp.concatenate(
@@ -144,14 +148,14 @@
     )
     pushes = jnp.concatenate([pushes[8 * i : 8 * i + 8] for i in range(N_PLANE)], axis=1)
     places = side_by_side(plane_ref, 0, N_PLANE)
-    dist_ref[...], proj_ref[...], push_ref[...], place_ref[...] = source_features(places, pushes)
-
-
-def shell_kernel(line_ref, dist_ref, proj_ref, push_ref, place_ref, part_ref, shell_ref):
+    dist_ref[...], push_ref[...], form_ref[...], center_ref[...] = source_features(places, pushes)
+
+
+def shell_kernel(line_ref, dist_ref, push_ref, form_ref, center_ref, part_ref, shell_ref):
     shell_ref[...] = packed([line_ref[i] for i in range(N_LINE)], 3)
     order = [pair * 4 + src for src in range(4) for pair in range(4)]
     targets = packed([line_ref[i] for i in order], 3)
-    flow = pair_sums(targets, SOURCES, dist_ref, proj_ref, push_ref, place_ref, 4, 2)
+    flow = pair_sums(targets, SOURCES, dist_ref, push_ref, form_ref, center_ref, 1024, 4, True)
     for src in range(4):
         half = flow[:, 128 * (src // 2) : 128 * (src // 2) + 128]
         piece = pltpu.roll(half, 64, 1) if src % 2 else half
@@ -159,7 +163,7 @@
             part_ref[pair * 4 + src] = piece
 
 
-def fibre_kernel(first, widths, line_ref, dist_ref, proj_ref, push_ref, place_ref, flow_ref):
+def fibre_kernel(first, widths, line_ref, dist_ref, push_ref, form_ref, center_ref, flow_ref):
     done = 0
     for width in widths:
         count = width // 128
@@ -167,11 +171,12 @@
             side_by_side(line_ref, first + done, count),
             SOURCES,
             dist_ref,
-            proj_ref,
             push_ref,
-            place_ref,
+            form_ref,
+            center_ref,
+            1024,
             4,
-            0,
+            False,
         )
         for i in range(count):
             flow_ref[done + i] = flow[:, 128 * i : 128 * i + 128]
@@ -229,7 +234,7 @@
 
 
 def back_kernel(pair_ref, line_ref, plane_ref, own_ref, *refs):
-    flows, (part_ref, dist_ref, proj_ref, push_ref, place_ref) = refs[: len(CHUNKS)], refs[len(CHUNKS) :]
+    flows, (part_ref, dist_ref, push_ref, form_ref, center_ref) = refs[: len(CHUNKS)], refs[len(CHUNKS) :]
     lane = lax.broadcasted_iota(jnp.int32, (8, 128), 1)
     row = lax.broadcasted_iota(jnp.int32, (8, 128), 0)
     sources = [
@@ -237,7 +242,7 @@
         for i in range(N_PLANE // 2)
     ]
     sources = jnp.concatenate(sources, axis=1)
-    dist_ref[...], proj_ref[...], push_ref[...], place_ref[...] = source_features(
+    dist_ref[...], push_ref[...], form_ref[...], center_ref[...] = source_features(
         pltpu.roll(sources, 5, 0), sources
     )
     own = pltpu.roll(own_ref[0], 3, 0)
@@ -249,16 +254,17 @@
     for flow_ref in flows:
         done, count = 0, flow_ref.shape[0]
         while done < count:
-            wide = 6 if count % 6 == 0 else 4
+            wide = min(4, count - done)
             flow = pair_sums(
                 side_by_side(line_ref, index, wide),
                 BACK_SOURCES,
                 dist_ref,
-                proj_ref,
                 push_ref,
-                place_ref,
-                4,
-                0,
+                form_ref,
+                center_ref,
+                1024,
+                2,
+                False,
             )
             for i in range(wide):
                 mine = (pair_ref[0] == index // 4).astype(F32)
@@ -288,7 +294,7 @@
 
 
 def feature_shapes(count):
-    return [((32, count), BF16), ((32, count), BF16), ((16, count), BF16), ((16, count), BF16)]
+    return [((32, count), BF16), ((16, count), BF16), ((48, count), BF16), ((8, 128), F32)]
 
 
 def exchange(x, axes):
@@ -334,7 +340,7 @@
         flows.append(flow)
         return x
 
-    shell_parts = exchange_beside(shell_part, LINE)
+    shell_parts = exchange(shell_part, LINE)
     shell_own = pl.pallas_call(
         columns_kernel,
         out_shape=tiles(N_PLANE),

time: 110 us -> 104 us (0.945)
  blocking collectives: 35.3 us -> 45.3 us
  Pallas kernels: 32.7 us -> 24.2 us
  starting transfers between devices: 22.5 us -> 18.5 us
  waiting for transfers between devices: 17.1 us -> 14.1 us
    all_to_all x2 -> x3, blocking collectives: 35.3 us -> 45.3 us  [exchange(): return lax.all_to_all(x, axes, 0, 0, tiled=True)]
    pallas_call x3 -> x2, Pallas kernels: 14.8 us -> 10.3 us  [fibre_chunk(): pl.pallas_call(functools.partial(fibre_kernel, first, widths), out_shape=...]
    all_to_all x4 -> x3, starting transfers between devices: 22.5 us -> 18.5 us  [exchange(): return lax.all_to_all(x, axes, 0, 0, tiled=True)]
    all_to_all x4 -> x3, waiting for transfers between devices: 17.1 us -> 14.1 us  [exchange(): return lax.all_to_all(x, axes, 0, 0, tiled=True)]
    pallas_call x1, Pallas kernels: 8.61 us -> 6.19 us  [per_device(): pl.pallas_call(back_kernel, out_shape=tiles(N_LINE), grid=(1,), in_specs=...]
    pallas_call x1, Pallas kernels: 4.14 us -> 2.58 us  [per_device(): pl.pallas_call(shell_kernel, out_shape=[tiles(N_LINE), jax.ShapeDtypeStru...]
  transfers between devices with their start and end apart: 4 -> 3, of which waited for: 4 -> 3; matrix products, arithmetic and copies ran while one was open for 0% -> 0% of each run, Pallas kernels for 14% -> 10%
where the time goes in v6:
time: 104 us
  blocking collectives  45.3 us (44%)
  Pallas kernels  24.2 us (23%)
  starting transfers between devices  18.5 us (18%)
  waiting for transfers between devices  14.1 us (14%)
    all_to_all x3, blocking collectives, exchange(): return lax.all_to_all(x, axes, 0, 0, tiled=True)  45.3 us
    all_to_all x3, starting transfers between devices, exchange(): return lax.all_to_all(x, axes, 0, 0, tiled=True)  18.5 us
    all_to_all x3, waiting for transfers between devices, exchange(): return lax.all_to_all(x, axes, 0, 0, tiled=True)  14.1 us
    pallas_call x2, Pallas kernels, fibre_chunk(): pl.pallas_call(functools.partial(fibre_kernel, first, widths), out_shape=...  10.3 us
    pallas_call x1, Pallas kernels, per_device(): pl.pallas_call(back_kernel, out_shape=tiles(N_LINE), grid=(1,), in_specs=...  6.19 us
    pallas_call x1, Pallas kernels, per_device(): pl.pallas_call(shell_kernel, out_shape=[tiles(N_LINE), jax.ShapeDtypeStru...  2.58 us
  transfers between devices with their start and end apart: 3, of which 3 were waited for; matrix products, arithmetic and copies ran while one was open for 0% of the time, Pallas kernels for 10%

profile of v6, /device:TPU:1, one launch (start us, length us, event | category | flops | bytes accessed | tf_op | source)
XLA Modules:
  0.0 103.5 jit_solution(8518604221513647041)
XLA Ops:
  0.6 1.4 %shard_map.59 = (f32[16,8,128]{2,1,0:T(8,128)}, f32[32,8,128]{2,1,0:T(8,128)}) custom-call(f32[3,2,64]{2,1,0:T(2,128)} %fibre_ref.1, f32[3,1,16]{2,1,0:T(1,128)} %shell_ref.1), custom_call_target="tpu_custom_call" | custom-call | tf_op jit(solution)/shard_map/pallas_call | solution.py:305
  2.1 22.9 %all_to_all.30.plane_ref = f32[32,8,128]{2,1,0:T(8,128)S(1)} all-to-all(f32[32,8,128]{2,1,0:T(8,128)} %get-tuple-element.23), channel_id=1, replica_groups=mesh['tgt_0'=4,'tgt_1'=8,'tgt_2'=2,'tgt_3'=2,'src'=4] {'tgt_0','tgt_1'}, dimensions={0} | all-to-all | bytes 262144 | tf_op jit(solution)/shard_map/all_to_all | solution.py:301
  24.9 9.2 %all-to-all-start.1 = ((f32[16,8,128]{2,1,0:T(8,128)}), f32[16,8,128]{2,1,0:T(8,128)S(1)}, u32[]{:S(2)}, u32[]{:S(2)}) async-start(f32[16,8,128]{2,1,0:T(8,128)} %get-tuple-element.24), calls=%async_computation.1 | async-start | bytes 131072 | tf_op jit(solution)/shard_map/all_to_all | solution.py:301
  34.1 0.0 copy-start.1
  34.1 0.8 copy-done.1
  34.9 0.6 shard_map.60
  35.5 6.2 %all-to-all-done.1.line_ref = f32[16,8,128]{2,1,0:T(8,128)S(1)} async-done(((f32[16,8,128]{2,1,0:T(8,128)}), f32[16,8,128]{2,1,0:T(8,128)S(1)}, u32[]{:S(2)}, u32[]{:S(2)}) %all-to-all-start.1) | async-done | bytes 65568 | tf_op jit(solution)/shard_map/all_to_all | solution.py:301
  41.7 2.6 %shard_map.61 = (f32[16,8,128]{2,1,0:T(8,128)S(1)}, f32[8,256]{1,0:T(8,128)S(1)}) custom-call(f32[16,8,128]{2,1,0:T(8,128)S(1)} %all-to-all-done.1.line_ref, bf16[32,4096]{1,0:T(8,128)(2,1)S(1)} %get-tuple-element.30.dist_ref, bf16[16,4096]{1,0:T(8,128)(2,1)S(1)} %get-tuple-element.31.push_ref, bf16[48,4096]{1,0:T(8,128)(2,1)S(1)} %get-tuple-element.32.form_ref, ...), custom_call_target="tpu_custom_call" | custom-call | flops 419430400 | bytes 1048576 | tf_op jit(solution)/shard_map/pallas_call | solution.py:318
  44.3 10.4 %all_to_all.31.parts_ref = f32[16,8,128]{2,1,0:T(8,128)S(1)} all-to-all(f32[16,8,128]{2,1,0:T(8,128)S(1)} %get-tuple-element.34), channel_id=1, replica_groups=mesh['tgt_0'=4,'tgt_1'=8,'tgt_2'=2,'tgt_3'=2,'src'=4] {'tgt_2','tgt_3','..., dimensions={0} | all-to-all | bytes 131072 | tf_op jit(solution)/shard_map/all_to_all | solution.py:301
  54.7 0.7 shard_map.62
  55.4 3.9 %all-to-all-start.3 = ((f32[32,8,128]{2,1,0:T(8,128)}), f32[32,8,128]{2,1,0:T(8,128)S(1)}, u32[]{:S(2)}, u32[]{:S(2)}) async-start(f32[32,8,128]{2,1,0:T(8,128)} %shard_map.62), calls=%async_computation.3 | async-start | bytes 262144 | tf_op jit(solution)/shard_map/all_to_all | solution.py:301
  59.2 0.0 copy-start
  59.3 5.1 %shard_map.63.refs_0_ = f32[8,8,128]{2,1,0:T(8,128)S(1)} custom-call(f32[16,8,128]{2,1,0:T(8,128)S(1)} %all-to-all-done.1.line_ref, bf16[32,4096]{1,0:T(8,128)(2,1)S(1)} %get-tuple-element.30.dist_ref, bf16[16,4096]{1,0:T(8,128)(2,1)S(1)} %get-tuple-element.31.push_ref, bf16[48,4096]{1,0:T(8,128)(2,1)S(1)} %get-tuple-element.32.form_ref, ...), custom_call_target="tpu_custom_call" | custom-call | flops 1677721600 | bytes 1048576 | tf_op jit(solution)/shard_map/pallas_call | solution.py:328
  64.4 4.0 %all-to-all-done.3.columns_ref = f32[32,8,128]{2,1,0:T(8,128)S(1)} async-done(((f32[32,8,128]{2,1,0:T(8,128)}), f32[32,8,128]{2,1,0:T(8,128)S(1)}, u32[]{:S(2)}, u32[]{:S(2)}) %all-to-all-start.3) | async-done | bytes 131104 | tf_op jit(solution)/shard_map/all_to_all | solution.py:301
  68.4 0.0 copy-done
  68.4 1.8 %shard_map.64.own_ref = f32[32,8,128]{2,1,0:T(8,128)} custom-call(s32[1]{0:T(128)} %bitcast.pair_ref, f32[32,8,128]{2,1,0:T(8,128)S(1)} %all-to-all-done.3.columns_ref, bf16[3,1,64,3,16,128]{5,4,3,2,1,0:T(8,128)(2,1)S(1)} %copy-done, f32[8,256]{1,0:T(8,128)S(1)} %get-tuple-element.37.shell_ref), custom_call_target="tpu_custom_call" | custom-call | tf_op jit(solution)/shard_map/pallas_call | solution.py:354
  70.2 5.4 %all-to-all-start.4 = ((f32[32,8,128]{2,1,0:T(8,128)}), f32[32,8,128]{2,1,0:T(8,128)S(1)}, u32[]{:S(2)}, u32[]{:S(2)}) async-start(f32[32,8,128]{2,1,0:T(8,128)} %shard_map.64.own_ref), calls=%async_computation.4 | async-start | bytes 262144 | tf_op jit(solution)/shard_map/all_to_all | solution.py:301
  75.6 5.1 %shard_map.65.refs_1_ = f32[8,8,128]{2,1,0:T(8,128)S(1)} custom-call(f32[16,8,128]{2,1,0:T(8,128)S(1)} %all-to-all-done.1.line_ref, bf16[32,4096]{1,0:T(8,128)(2,1)S(1)} %get-tuple-element.30.dist_ref, bf16[16,4096]{1,0:T(8,128)(2,1)S(1)} %get-tuple-element.31.push_ref, bf16[48,4096]{1,0:T(8,128)(2,1)S(1)} %get-tuple-element.32.form_ref, ...), custom_call_target="tpu_custom_call" | custom-call | flops 1677721600 | bytes 1048576 | tf_op jit(solution)/shard_map/pallas_call | solution.py:328
  80.7 3.8 %all-to-all-done.4.plane_ref = f32[32,8,128]{2,1,0:T(8,128)S(1)} async-done(((f32[32,8,128]{2,1,0:T(8,128)}), f32[32,8,128]{2,1,0:T(8,128)S(1)}, u32[]{:S(2)}, u32[]{:S(2)}) %all-to-all-start.4) | async-done | bytes 131104 | tf_op jit(solution)/shard_map/all_to_all | solution.py:301
  84.6 6.2 %shard_map.66 = f32[16,8,128]{2,1,0:T(8,128)S(1)} custom-call(s32[1]{0:T(128)} %bitcast.pair_ref, f32[16,8,128]{2,1,0:T(8,128)S(1)} %all-to-all-done.1.line_ref, f32[32,8,128]{2,1,0:T(8,128)S(1)} %all-to-all-done.4.plane_ref, f32[32,8,128]{2,1,0:T(8,128)} %shard_map.64.own_ref, f32[8,8,128]{2,1,0:T(8,128)S(1)} %shard_map.63.refs_0_, ...), custom_call_target="tpu_custom_call" | custom-call | flops 1677721600 | bytes 1048576 | tf_op jit(solution)/shard_map/pallas_call | solution.py:361
  90.8 12.1 %all_to_all.32.parts_ref = f32[16,8,128]{2,1,0:T(8,128)S(1)} all-to-all(f32[16,8,128]{2,1,0:T(8,128)S(1)} %shard_map.66), channel_id=1, replica_groups=mesh['tgt_0'=4,'tgt_1'=8,'tgt_2'=2,'tgt_3'=2,'src'=4] {'tgt_2','tgt_3','..., dimensions={0} | all-to-all | bytes 131072 | tf_op jit(solution)/shard_map/all_to_all | solution.py:301
  102.9 0.7 shard_map.67
Async XLA Ops:
  24.9 16.8 %all-to-all-start.1 = ((f32[16,8,128]{2,1,0:T(8,128)}), f32[16,8,128]{2,1,0:T(8,128)S(1)}, u32[]{:S(2)}, u32[]{:S(2)}) async-start(f32[16,8,128]{2,1,0:T(8,128)} %get-tuple-element.24), calls=%async_computation.1 | async-start | bytes 131072 | tf_op jit(solution)/shard_map/all_to_all | solution.py:301
  34.1 0.8 copy-start.1
  55.4 13.0 %all-to-all-start.3 = ((f32[32,8,128]{2,1,0:T(8,128)}), f32[32,8,128]{2,1,0:T(8,128)S(1)}, u32[]{:S(2)}, u32[]{:S(2)}) async-start(f32[32,8,128]{2,1,0:T(8,128)} %shard_map.62), calls=%async_computation.3 | async-start | bytes 262144 | tf_op jit(solution)/shard_map/all_to_all | solution.py:301
  59.2 9.1 %copy-start = (bf16[3,1,64,3,16,128]{5,4,3,2,1,0:T(8,128)(2,1)S(1)}, bf16[3,1,64,3,16,128]{5,4,3,2,1,0:T(8,128)(2,1)}, u32[]{:S(2)}) copy-start(bf16[3,1,64,3,16,128]{5,4,3,2,1,0:T(8,128)(2,1)} %inverse_ref.1) | copy-start | bytes 7077892
  70.2 14.4 %all-to-all-start.4 = ((f32[32,8,128]{2,1,0:T(8,128)}), f32[32,8,128]{2,1,0:T(8,128)S(1)}, u32[]{:S(2)}, u32[]{:S(2)}) async-start(f32[32,8,128]{2,1,0:T(8,128)} %shard_map.64.own_ref), calls=%async_computation.4 | async-start | bytes 262144 | tf_op jit(solution)/shard_map/all_to_all | solution.py:301

commit v7 on v6

--- a/solution.py
+++ b/solution.py
@@ -16,8 +16,10 @@
 N_LINE = 16
 N_PLANE = 32
 SOURCES = N_PLANE * 128
-BACK_SOURCES = N_PLANE * 64
-CHUNKS = ((0, (512, 512)), (8, (512, 512)))
+LINE_SOURCES = N_LINE * 128
+CHUNKS = ((0, 1), (4, 5), (24, 2))
+WIDE = 4
+ROW_SOURCES = 256
 ROWS = (((0,), (0,)), ((), ()))
 
 F32 = jnp.float32
@@ -136,18 +138,22 @@
     plane_ref[...] = jnp.broadcast_to(tile[None], plane_ref.shape)
 
 
-def source_kernel(plane_ref, bending_ref, dist_ref, push_ref, form_ref, center_ref):
+def source_kernel(tiles_ref, bending_ref, dist_ref, push_ref, form_ref, center_ref):
+    count = tiles_ref.shape[0]
     square = bending_ref[...]
     zero = jnp.zeros_like(square)
     both = jnp.concatenate(
         [jnp.concatenate([square, zero], axis=1), jnp.concatenate([zero, square], axis=1)], axis=0
     )
-    places = plane_ref[...].reshape(N_PLANE * 8, 128)
     pushes = -lax.dot_general(
-        places, both, (((1,), (1,)), ((), ())), precision=lax.Precision.HIGHEST, preferred_element_type=F32
+        tiles_ref[...].reshape(count * 8, 128),
+        both,
+        (((1,), (1,)), ((), ())),
+        precision=lax.Precision.HIGHEST,
+        preferred_element_type=F32,
     )
-    pushes = jnp.concatenate([pushes[8 * i : 8 * i + 8] for i in range(N_PLANE)], axis=1)
-    places = side_by_side(plane_ref, 0, N_PLANE)
+    pushes = jnp.concatenate([pushes[8 * i : 8 * i + 8] for i in range(count)], axis=1)
+    places = side_by_side(tiles_ref, 0, count)
     dist_ref[...], push_ref[...], form_ref[...], center_ref[...] = source_features(places, pushes)
 
 
@@ -163,24 +169,21 @@
             part_ref[pair * 4 + src] = piece
 
 
-def fibre_kernel(first, widths, line_ref, dist_ref, push_ref, form_ref, center_ref, flow_ref):
-    done = 0
-    for width in widths:
-        count = width // 128
+def fibre_kernel(first, parts, plane_ref, dist_ref, push_ref, form_ref, center_ref, flow_ref):
+    for part in range(parts):
         flow = pair_sums(
-            side_by_side(line_ref, first + done, count),
-            SOURCES,
+            side_by_side(plane_ref, first + part * WIDE, WIDE),
+            LINE_SOURCES,
             dist_ref,
             push_ref,
             form_ref,
             center_ref,
             1024,
-            4,
+            2,
             False,
         )
-        for i in range(count):
-            flow_ref[done + i] = flow[:, 128 * i : 128 * i + 128]
-        done += count
+        for i in range(WIDE):
+            flow_ref[part * WIDE + i] = flow[:, 128 * i : 128 * i + 128]
 
 
 def total_of(parts_ref):
@@ -196,7 +199,7 @@
     out_ref[...] = jnp.broadcast_to(total[None], out_ref.shape)
 
 
-def density_kernel(pair_ref, columns_ref, inverse_ref, shell_ref, out_ref):
+def density_kernel(pair_ref, columns_ref, inverse_ref, out_ref):
     columns = jnp.concatenate([columns_ref[:, c, :] for c in range(3)], axis=1).astype(BF16)
     here = lax.broadcasted_iota(jnp.int32, (N_PLANE, 512), 0)
     there = lax.broadcasted_iota(jnp.int32, (N_PLANE, 512), 1)
@@ -223,62 +226,57 @@
         )
         density -= jnp.where(row == x, line, 0.0)
     density = jnp.concatenate([density, jnp.zeros((8, 64), F32)], axis=1)
+    row = rows_of(density)
     lane = lax.broadcasted_iota(jnp.int32, density.shape, 1)
-    places = jnp.zeros_like(density)
+    lower = pltpu.roll(density, 3, 0)
+    for src in range(4):
+        piece = pltpu.roll(lower, 128 - 16 * src, 1) if src else lower
+        piece = jnp.where((row >= 3) & (lane < 16), piece, 0.0)
+        for pair in range(4):
+            mine = (pair_ref[0] == pair).astype(F32)
+            out_ref[pair * 4 + src] = density + mine * piece
+
+
+def back_kernel(parts_ref, shell_ref, plane_ref, *refs):
+    flows, refs = refs[: len(CHUNKS)], refs[len(CHUNKS) :]
+    part_ref, density_ref, dist_ref, push_ref, form_ref, center_ref = refs
+    lane = lax.broadcasted_iota(jnp.int32, (8, 128), 1)
+    pairs = []
     for pair in range(4):
-        half = shell_ref[:, 128 * (pair // 2) : 128 * (pair // 2) + 128]
-        half = pltpu.roll(half, 64, 1) if pair % 2 else half
-        places += jnp.where((pair_ref[0] == pair) & (lane < 64), half, 0.0)
-    tile = density + pltpu.roll(places, 3, 0)
-    out_ref[...] = jnp.broadcast_to(tile[None], out_ref.shape)
-
-
-def back_kernel(pair_ref, line_ref, plane_ref, own_ref, *refs):
-    flows, (part_ref, dist_ref, push_ref, form_ref, center_ref) = refs[: len(CHUNKS)], refs[len(CHUNKS) :]
-    lane = lax.broadcasted_iota(jnp.int32, (8, 128), 1)
-    row = lax.broadcasted_iota(jnp.int32, (8, 128), 0)
-    sources = [
-        jnp.where(lane < 64, plane_ref[2 * i], pltpu.roll(plane_ref[2 * i + 1], 64, 1))
-        for i in range(N_PLANE // 2)
+        total = parts_ref[pair * 4]
+        for src in range(1, 4):
+            total += parts_ref[pair * 4 + src]
+        pairs.append(total)
+    whole = (pairs[0] + pairs[1]) + (pairs[2] + pairs[3])
+    density_ref[:, 0, :] = whole[3:6, 0:16]
+    halves = [
+        jnp.where(lane < 64, pairs[i], pltpu.roll(pairs[i + 1], 64, 1)) for i in (0, 2)
     ]
-    sources = jnp.concatenate(sources, axis=1)
     dist_ref[...], push_ref[...], form_ref[...], center_ref[...] = source_features(
-        pltpu.roll(sources, 5, 0), sources
+        shell_ref[...], jnp.concatenate(halves, axis=1)
     )
-    own = pltpu.roll(own_ref[0], 3, 0)
-    pieces = []
-    for src in range(4):
-        piece = pltpu.roll(own, 128 - 16 * src, 1) if src else own
-        pieces.append(jnp.where((row >= 3) & (lane < 16), piece, 0.0))
-    index = 0
-    for flow_ref in flows:
-        done, count = 0, flow_ref.shape[0]
-        while done < count:
-            wide = min(4, count - done)
+    for (first, parts), flow_ref in zip(CHUNKS, flows):
+        for part in range(parts):
+            index = first + part * WIDE
             flow = pair_sums(
-                side_by_side(line_ref, index, wide),
-                BACK_SOURCES,
+                side_by_side(plane_ref, index, WIDE),
+                ROW_SOURCES,
                 dist_ref,
                 push_ref,
                 form_ref,
                 center_ref,
-                1024,
-                2,
+                ROW_SOURCES,
+                1,
                 False,
             )
-            for i in range(wide):
-                mine = (pair_ref[0] == index // 4).astype(F32)
-                total = flow[:, 128 * i : 128 * i + 128] + flow_ref[done + i]
-                part_ref[index] = jnp.where(row < 3, total, mine * pieces[index % 4])
-                index += 1
-            done += wide
-
-
-def velocity_kernel(parts_ref, out_ref, density_ref):
+            for i in range(WIDE):
+                part_ref[index + i] = flow[:, 128 * i : 128 * i + 128] + flow_ref[part * WIDE + i]
+
+
+def velocity_kernel(parts_ref, out_ref):
     total = total_of(parts_ref)
     out_ref[:, 0, :] = total[0:3, 0:64]
     out_ref[:, 1, :] = total[0:3, 64:128]
-    density_ref[:, 0, :] = total[3:6, 0:16]
 
 
 def tiles(count):
@@ -307,13 +305,17 @@
     )(fibre_points, shell_points)
     plane = exchange(own_plane, PLANE)
     own_line, _ = lax.optimization_barrier((own_line, plane))
-    features = [jax.ShapeDtypeStruct(s, t) for s, t in feature_shapes(SOURCES)]
-    features = pl.pallas_call(
-        source_kernel,
-        out_shape=features,
-        compiler_params=params(24),
-        cost_estimate=cost(64 * SOURCES),
-    )(plane, bending)
+
+    def features_of(x):
+        count = x.shape[0] * 128
+        return pl.pallas_call(
+            source_kernel,
+            out_shape=[jax.ShapeDtypeStruct(s, t) for s, t in feature_shapes(count)],
+            compiler_params=params(24),
+            cost_estimate=cost(64 * count),
+        )(x, bending)
+
+    features = features_of(plane)
     line, features = lax.optimization_barrier((exchange(own_line, LINE), features))
     shell_part, shell_places = pl.pallas_call(
         shell_kernel,
@@ -321,67 +323,45 @@
         compiler_params=params(24),
         cost_estimate=cost(256 * SOURCES),
     )(line, *features)
-
-    def fibre_chunk(chunk, after):
-        held, _ = lax.optimization_barrier((line, after))
-        first, widths = CHUNKS[chunk]
-        return pl.pallas_call(
-            functools.partial(fibre_kernel, first, widths),
-            out_shape=tiles(sum(widths) // 128),
+    held, _ = lax.optimization_barrier((line, shell_part))
+    features = features_of(held)
+    flows = []
+
+    def exchange_beside(x, axes):
+        first, parts = CHUNKS[len(flows)]
+        held, _ = lax.optimization_barrier((plane, x))
+        flow = pl.pallas_call(
+            functools.partial(fibre_kernel, first, parts),
+            out_shape=tiles(parts * WIDE),
             compiler_params=params(24),
-            cost_estimate=cost(sum(widths) * SOURCES),
+            cost_estimate=cost(parts * WIDE * 128 * LINE_SOURCES),
         )(held, *features)
-
-    flows = []
-
-    def exchange_beside(x, axes):
-        flow = fibre_chunk(len(flows), x)
         x, flow = lax.optimization_barrier((exchange(x, axes), flow))
         flows.append(flow)
         return x
 
-    shell_parts = exchange(shell_part, LINE)
     shell_own = pl.pallas_call(
-        columns_kernel,
-        out_shape=tiles(N_PLANE),
-        compiler_params=params(2),
-    )(shell_parts)
+        columns_kernel, out_shape=tiles(N_PLANE), compiler_params=params(2)
+    )(exchange_beside(shell_part, LINE))
     shell_all = exchange_beside(shell_own, PLANE)
     pair = lax.axis_index("tgt_2") * 2 + lax.axis_index("tgt_3")
-    pair = pair.astype(jnp.int32).reshape(1)
-    scalar = pl.BlockSpec(memory_space=pltpu.SMEM)
-    vector = pl.BlockSpec(memory_space=pltpu.VMEM)
-    density_own = pl.pallas_call(
+    message = pl.pallas_call(
         density_kernel,
-        out_shape=tiles(N_PLANE),
-        in_specs=[scalar, vector, vector, vector],
+        out_shape=tiles(N_LINE),
+        in_specs=[pl.BlockSpec(memory_space=pltpu.SMEM)] + [pl.BlockSpec(memory_space=pltpu.VMEM)] * 2,
         compiler_params=params(12),
-    )(pair, shell_all, shell_inverse, shell_places)
-    density_all = exchange_beside(density_own, PLANE)
-    part = pl.pallas_call(
+    )(pair.astype(jnp.int32).reshape(1), shell_all, shell_inverse)
+    density_parts = exchange_beside(message, LINE)
+    part, density = pl.pallas_call(
         back_kernel,
-        out_shape=tiles(N_LINE),
-        grid=(1,),
-        in_specs=[
-            scalar,
-            pl.BlockSpec((N_LINE, 8, 128), lambda i: (0, 0, 0)),
-            pl.BlockSpec((N_PLANE, 8, 128), lambda i: (0, 0, 0)),
-            pl.BlockSpec((1, 8, 128), lambda i: (0, 0, 0)),
-        ]
-        + [pl.BlockSpec(flow.shape, lambda i: (0, 0, 0)) for flow in flows],
-        out_specs=pl.BlockSpec((N_LINE, 8, 128), lambda i: (0, 0, 0)),
-        scratch_shapes=[pltpu.VMEM(s, t) for s, t in feature_shapes(BACK_SOURCES)],
+        out_shape=[tiles(N_PLANE), jax.ShapeDtypeStruct((3, 1, 16), F32)],
+        scratch_shapes=[pltpu.VMEM(s, t) for s, t in feature_shapes(ROW_SOURCES)],
         compiler_params=params(24),
-        cost_estimate=cost(N_LINE * 128 * BACK_SOURCES),
-    )(pair, line, density_all, density_own, *flows)
-    velocity, density = pl.pallas_call(
-        velocity_kernel,
-        out_shape=[
-            jax.ShapeDtypeStruct((3, 2, 64), F32),
-            jax.ShapeDtypeStruct((3, 1, 16), F32),
-        ],
-        compiler_params=params(2),
-    )(exchange(part, LINE))
+        cost_estimate=cost(ROW_SOURCES * SOURCES),
+    )(density_parts, shell_places, plane, *flows)
+    velocity = pl.pallas_call(
+        velocity_kernel, out_shape=jax.ShapeDtypeStruct((3, 2, 64), F32), compiler_params=params(2)
+    )(exchange(part, PLANE))
     return velocity, density
 
 

time: 104 us -> 103 us (level)
  blocking collectives: 45.3 us -> 37.1 us
  waiting for transfers between devices: 14.1 us -> 19.2 us
  starting transfers between devices: 18.5 us -> 22.3 us
  Pallas kernels: 24.2 us -> 22.4 us
    all_to_all x3 -> x2, blocking collectives: 45.3 us -> 37.1 us  [exchange(): return lax.all_to_all(x, axes, 0, 0, tiled=True)]
    all_to_all x3 -> x4, waiting for transfers between devices: 14.1 us -> 19.2 us  [exchange(): return lax.all_to_all(x, axes, 0, 0, tiled=True)]
    all_to_all x3 -> x4, starting transfers between devices: 18.5 us -> 22.3 us  [exchange(): return lax.all_to_all(x, axes, 0, 0, tiled=True)]
    pallas_call x6 -> x8, Pallas kernels: 19.5 us -> 17.1 us  [the longest x3 10.7 us: exchange_beside(): pl.pallas_call(functools.partial(fibre_kernel, first, parts), out_shape=t...]
  transfers between devices with their start and end apart: 3 -> 4, of which waited for: 3 -> 4; matrix products, arithmetic and copies ran while one was open for 0% -> 0% of each run, Pallas kernels for 10% -> 11%
where the time goes in v7:
time: 103 us; the launch traced here: 102 us
  blocking collectives  37.1 us (36%)
  Pallas kernels  22.4 us (22%)
  starting transfers between devices  22.3 us (22%)
  waiting for transfers between devices  19.2 us (19%)
    all_to_all x2, blocking collectives, exchange(): return lax.all_to_all(x, axes, 0, 0, tiled=True)  37.1 us
    all_to_all x4, starting transfers between devices, exchange(): return lax.all_to_all(x, axes, 0, 0, tiled=True)  22.3 us
    all_to_all x4, waiting for transfers between devices, exchange(): return lax.all_to_all(x, axes, 0, 0, tiled=True)  19.2 us
    pallas_call x3, Pallas kernels, exchange_beside(): pl.pallas_call(functools.partial(fibre_kernel, first, parts), out_shape=t...  10.7 us
    pallas_call x1, Pallas kernels, per_device(): pl.pallas_call(shell_kernel, out_shape=[tiles(N_LINE), jax.ShapeDtypeStru...  3.21 us
    pallas_call x1, Pallas kernels, per_device(): pl.pallas_call(back_kernel, out_shape=[tiles(N_PLANE), jax.ShapeDtypeStru...  2.84 us
  transfers between devices with their start and end apart: 4, of which 4 were waited for; matrix products, arithmetic and copies ran while one was open for 0% of the time, Pallas kernels for 11%

profile of v7, /device:TPU:1, one launch (start us, length us, event | category | flops | bytes accessed | tf_op | source)
XLA Modules:
  0.0 102.5 jit_solution(15809685526875442970)
XLA Ops:
  0.6 0.0 copy-start.2
  0.6 1.5 %shard_map.59 = (f32[16,8,128]{2,1,0:T(8,128)}, f32[32,8,128]{2,1,0:T(8,128)}) custom-call(f32[3,2,64]{2,1,0:T(2,128)} %fibre_ref.1, f32[3,1,16]{2,1,0:T(1,128)} %shell_ref.1), custom_call_target="tpu_custom_call" | custom-call | tf_op jit(solution)/shard_map/pallas_call | solution.py:303
  2.1 22.9 %all_to_all.30.tiles_ref.plane_ref = f32[32,8,128]{2,1,0:T(8,128)S(1)} all-to-all(f32[32,8,128]{2,1,0:T(8,128)} %get-tuple-element.33), channel_id=1, replica_groups=mesh['tgt_0'=4,'tgt_1'=8,'tgt_2'=2,'tgt_3'=2,'src'=4] {'tgt_0','tgt_1'}, dimensions={0} | all-to-all | bytes 262144 | tf_op jit(solution)/shard_map/all_to_all | solution.py:299
  25.0 9.2 %all-to-all-start.1 = ((f32[16,8,128]{2,1,0:T(8,128)}), f32[16,8,128]{2,1,0:T(8,128)S(1)}, u32[]{:S(2)}, u32[]{:S(2)}) async-start(f32[16,8,128]{2,1,0:T(8,128)} %get-tuple-element.34), calls=%async_computation.1 | async-start | bytes 131072 | tf_op jit(solution)/shard_map/all_to_all | solution.py:299
  34.2 0.0 copy-start.1
  34.2 0.8 copy-done.1
  34.9 0.6 shard_map.60
  35.5 6.2 %all-to-all-done.1.line_ref.tiles_ref = f32[16,8,128]{2,1,0:T(8,128)S(1)} async-done(((f32[16,8,128]{2,1,0:T(8,128)}), f32[16,8,128]{2,1,0:T(8,128)S(1)}, u32[]{:S(2)}, u32[]{:S(2)}) %all-to-all-start.1) | async-done | bytes 65568 | tf_op jit(solution)/shard_map/all_to_all | solution.py:299
  41.7 3.2 %shard_map.61 = (f32[16,8,128]{2,1,0:T(8,128)}, f32[8,256]{1,0:T(8,128)S(1)}) custom-call(f32[16,8,128]{2,1,0:T(8,128)S(1)} %all-to-all-done.1.line_ref.tiles_ref, bf16[32,4096]{1,0:T(8,128)(2,1)S(1)} %get-tuple-element.40.dist_ref, bf16[16,4096]{1,0:T(8,128)(2,1)S(1)} %get-tuple-element.41.push_ref, bf16[48,4096]{1,0:T(8,128)(2,1)S(1)} %get-tuple-element.42.form_ref, ...), custom_call_target="tpu_custom_call" | custom-call | flops 419430400 | bytes 1048576 | tf_op jit(solution)/shard_map/pallas_call | solution.py:320
  45.0 3.7 %all-to-all-start.2 = ((f32[16,8,128]{2,1,0:T(8,128)}), f32[16,8,128]{2,1,0:T(8,128)S(1)}, u32[]{:S(2)}, u32[]{:S(2)}) async-start(f32[16,8,128]{2,1,0:T(8,128)} %get-tuple-element.44), calls=%async_computation.2 | async-start | bytes 131072 | tf_op jit(solution)/shard_map/all_to_all | solution.py:299
  48.7 0.0 copy-done.2
  48.7 0.4 shard_map.62
  49.1 1.4 %shard_map.63.refs_0_ = f32[4,8,128]{2,1,0:T(8,128)S(1)} custom-call(f32[32,8,128]{2,1,0:T(8,128)S(1)} %all_to_all.30.tiles_ref.plane_ref, bf16[32,2048]{1,0:T(8,128)(2,1)S(1)} %get-tuple-element.47.dist_ref, bf16[16,2048]{1,0:T(8,128)(2,1)S(1)} %get-tuple-element.48.push_ref, bf16[48,2048]{1,0:T(8,128)(2,1)S(1)} %get-tuple-element.49.form_ref, ...), custom_call_target="tpu_custom_call" | custom-call | flops 419430400 | bytes 1048576 | tf_op jit(solution)/shard_map/pallas_call | solution.py:333
  50.5 5.8 %all-to-all-done.2.parts_ref = f32[16,8,128]{2,1,0:T(8,128)S(1)} async-done(((f32[16,8,128]{2,1,0:T(8,128)}), f32[16,8,128]{2,1,0:T(8,128)S(1)}, u32[]{:S(2)}, u32[]{:S(2)}) %all-to-all-start.2) | async-done | bytes 65568 | tf_op jit(solution)/shard_map/all_to_all | solution.py:299
  56.2 0.7 shard_map.64
  56.9 4.0 %all-to-all-start.3 = ((f32[32,8,128]{2,1,0:T(8,128)}), f32[32,8,128]{2,1,0:T(8,128)S(1)}, u32[]{:S(2)}, u32[]{:S(2)}) async-start(f32[32,8,128]{2,1,0:T(8,128)} %shard_map.64), calls=%async_computation.3 | async-start | bytes 262144 | tf_op jit(solution)/shard_map/all_to_all | solution.py:299
  61.0 0.0 copy-start
  61.0 6.6 %shard_map.65.refs_1_ = f32[20,8,128]{2,1,0:T(8,128)S(1)} custom-call(f32[32,8,128]{2,1,0:T(8,128)S(1)} %all_to_all.30.tiles_ref.plane_ref, bf16[32,2048]{1,0:T(8,128)(2,1)S(1)} %get-tuple-element.47.dist_ref, bf16[16,2048]{1,0:T(8,128)(2,1)S(1)} %get-tuple-element.48.push_ref, bf16[48,2048]{1,0:T(8,128)(2,1)S(1)} %get-tuple-element.49.form_ref, ...), custom_call_target="tpu_custom_call" | custom-call | flops 2097152000 | bytes 1048576 | tf_op jit(solution)/shard_map/pallas_call | solution.py:333
  67.6 2.3 %all-to-all-done.3.columns_ref = f32[32,8,128]{2,1,0:T(8,128)S(1)} async-done(((f32[32,8,128]{2,1,0:T(8,128)}), f32[32,8,128]{2,1,0:T(8,128)S(1)}, u32[]{:S(2)}, u32[]{:S(2)}) %all-to-all-start.3) | async-done | bytes 131104 | tf_op jit(solution)/shard_map/all_to_all | solution.py:299
  69.9 0.0 copy-done
  69.9 1.8 %shard_map.66 = f32[16,8,128]{2,1,0:T(8,128)} custom-call(s32[1]{0:T(128)} %bitcast.pair_ref, f32[32,8,128]{2,1,0:T(8,128)S(1)} %all-to-all-done.3.columns_ref, bf16[3,1,64,3,16,128]{5,4,3,2,1,0:T(8,128)(2,1)S(1)} %copy-done), custom_call_target="tpu_custom_call" | custom-call | tf_op jit(solution)/shard_map/pallas_call | solution.py:348
  71.7 5.4 %all-to-all-start.4 = ((f32[16,8,128]{2,1,0:T(8,128)}), f32[16,8,128]{2,1,0:T(8,128)S(1)}, u32[]{:S(2)}, u32[]{:S(2)}) async-start(f32[16,8,128]{2,1,0:T(8,128)} %shard_map.66), calls=%async_computation.4 | async-start | bytes 131072 | tf_op jit(solution)/shard_map/all_to_all | solution.py:299
  77.1 2.7 %shard_map.67.refs_2_ = f32[8,8,128]{2,1,0:T(8,128)S(1)} custom-call(f32[32,8,128]{2,1,0:T(8,128)S(1)} %all_to_all.30.tiles_ref.plane_ref, bf16[32,2048]{1,0:T(8,128)(2,1)S(1)} %get-tuple-element.47.dist_ref, bf16[16,2048]{1,0:T(8,128)(2,1)S(1)} %get-tuple-element.48.push_ref, bf16[48,2048]{1,0:T(8,128)(2,1)S(1)} %get-tuple-element.49.form_ref, ...), custom_call_target="tpu_custom_call" | custom-call | flops 838860800 | bytes 1048576 | tf_op jit(solution)/shard_map/pallas_call | solution.py:333
  79.9 4.8 %all-to-all-done.4.parts_ref = f32[16,8,128]{2,1,0:T(8,128)S(1)} async-done(((f32[16,8,128]{2,1,0:T(8,128)}), f32[16,8,128]{2,1,0:T(8,128)S(1)}, u32[]{:S(2)}, u32[]{:S(2)}) %all-to-all-start.4) | async-done | bytes 65568 | tf_op jit(solution)/shard_map/all_to_all | solution.py:299
  84.7 2.8 %shard_map.68 = (f32[32,8,128]{2,1,0:T(8,128)S(1)}, f32[3,1,16]{2,1,0:T(1,128)}) custom-call(f32[16,8,128]{2,1,0:T(8,128)S(1)} %all-to-all-done.4.parts_ref, f32[8,256]{1,0:T(8,128)S(1)} %get-tuple-element.56.shell_ref, f32[32,8,128]{2,1,0:T(8,128)S(1)} %all_to_all.30.tiles_ref.plane_ref, f32[4,8,128]{2,1,0:T(8,128)S(1)} %shard_map.63.refs_0_, ...), custom_call_target="tpu_custom_call" | custom-call | flops 419430400 | bytes 1048576 | tf_op jit(solution)/shard_map/pallas_call | solution.py:355
  87.6 14.2 %all_to_all.31.parts_ref = f32[32,8,128]{2,1,0:T(8,128)S(1)} all-to-all(f32[32,8,128]{2,1,0:T(8,128)S(1)} %get-tuple-element.60), channel_id=1, replica_groups=mesh['tgt_0'=4,'tgt_1'=8,'tgt_2'=2,'tgt_3'=2,'src'=4] {'tgt_0','tgt_1'}, dimensions={0} | all-to-all | bytes 262144 | tf_op jit(solution)/shard_map/all_to_all | solution.py:299
  101.8 0.7 shard_map.69
Async XLA Ops:
  0.6 48.0 %copy-start.2 = (f32[64,64]{1,0:T(8,128)S(1)}, f32[64,64]{1,0:T(8,128)}, u32[]{:S(2)}) copy-start(f32[64,64]{1,0:T(8,128)} %bending_ref.3) | copy-start | bytes 49156
  25.0 16.8 %all-to-all-start.1 = ((f32[16,8,128]{2,1,0:T(8,128)}), f32[16,8,128]{2,1,0:T(8,128)S(1)}, u32[]{:S(2)}, u32[]{:S(2)}) async-start(f32[16,8,128]{2,1,0:T(8,128)} %get-tuple-element.34), calls=%async_computation.1 | async-start | bytes 131072 | tf_op jit(solution)/shard_map/all_to_all | solution.py:299
  34.2 0.8 copy-start.1
  45.0 11.3 %all-to-all-start.2 = ((f32[16,8,128]{2,1,0:T(8,128)}), f32[16,8,128]{2,1,0:T(8,128)S(1)}, u32[]{:S(2)}, u32[]{:S(2)}) async-start(f32[16,8,128]{2,1,0:T(8,128)} %get-tuple-element.44), calls=%async_computation.2 | async-start | bytes 131072 | tf_op jit(solution)/shard_map/all_to_all | solution.py:299
  56.9 13.0 %all-to-all-start.3 = ((f32[32,8,128]{2,1,0:T(8,128)}), f32[32,8,128]{2,1,0:T(8,128)S(1)}, u32[]{:S(2)}, u32[]{:S(2)}) async-start(f32[32,8,128]{2,1,0:T(8,128)} %shard_map.64), calls=%async_computation.3 | async-start | bytes 262144 | tf_op jit(solution)/shard_map/all_to_all | solution.py:299
  61.0 9.0 %copy-start = (bf16[3,1,64,3,16,128]{5,4,3,2,1,0:T(8,128)(2,1)S(1)}, bf16[3,1,64,3,16,128]{5,4,3,2,1,0:T(8,128)(2,1)}, u32[]{:S(2)}) copy-start(bf16[3,1,64,3,16,128]{5,4,3,2,1,0:T(8,128)(2,1)} %inverse_ref.1) | copy-start | bytes 7077892
  71.7 13.0 %all-to-all-start.4 = ((f32[16,8,128]{2,1,0:T(8,128)}), f32[16,8,128]{2,1,0:T(8,128)S(1)}, u32[]{:S(2)}, u32[]{:S(2)}) async-start(f32[16,8,128]{2,1,0:T(8,128)} %shard_map.66), calls=%async_computation.4 | async-start | bytes 131072 | tf_op jit(solution)/shard_map/all_to_all | solution.py:299

commit v8 on v7

--- a/solution.py
+++ b/solution.py
@@ -19,6 +19,7 @@
 LINE_SOURCES = N_LINE * 128
 CHUNKS = ((0, 1), (4, 5), (24, 2))
 WIDE = 4
+BROAD = 16
 ROW_SOURCES = 256
 ROWS = (((0,), (0,)), ((), ()))
 
@@ -255,22 +256,21 @@
     dist_ref[...], push_ref[...], form_ref[...], center_ref[...] = source_features(
         shell_ref[...], jnp.concatenate(halves, axis=1)
     )
-    for (first, parts), flow_ref in zip(CHUNKS, flows):
-        for part in range(parts):
-            index = first + part * WIDE
-            flow = pair_sums(
-                side_by_side(plane_ref, index, WIDE),
-                ROW_SOURCES,
-                dist_ref,
-                push_ref,
-                form_ref,
-                center_ref,
-                ROW_SOURCES,
-                1,
-                False,
-            )
-            for i in range(WIDE):
-                part_ref[index + i] = flow[:, 128 * i : 128 * i + 128] + flow_ref[part * WIDE + i]
+    fibre = [flow_ref[i] for flow_ref in flows for i in range(flow_ref.shape[0])]
+    for index in range(0, N_PLANE, BROAD):
+        flow = pair_sums(
+            side_by_side(plane_ref, index, BROAD),
+            ROW_SOURCES,
+            dist_ref,
+            push_ref,
+            form_ref,
+            center_ref,
+            ROW_SOURCES,
+            1,
+            False,
+        )
+        for i in range(BROAD):
+            part_ref[index + i] = flow[:, 128 * i : 128 * i + 128] + fibre[index + i]
 
 
 def velocity_kernel(parts_ref, out_ref):

time: 103 us -> 102 us (level)
  transfers between devices with their start and end apart: 4 -> 4, of which waited for: 4 -> 4; matrix products, arithmetic and copies ran while one was open for 0% -> 0% of each run, Pallas kernels for 11% -> 12%
where the time goes in v8:
time: 102 us
  blocking collectives  37.1 us (36%)
  starting transfers between devices  22.3 us (22%)
  Pallas kernels  21.6 us (21%)
  waiting for transfers between devices  19.2 us (19%)
    all_to_all x2, blocking collectives, exchange(): return lax.all_to_all(x, axes, 0, 0, tiled=True)  37.1 us
    all_to_all x4, starting transfers between devices, exchange(): return lax.all_to_all(x, axes, 0, 0, tiled=True)  22.3 us
    all_to_all x4, waiting for transfers between devices, exchange(): return lax.all_to_all(x, axes, 0, 0, tiled=True)  19.2 us
    pallas_call x3, Pallas kernels, exchange_beside(): pl.pallas_call(functools.partial(fibre_kernel, first, parts), out_shape=t...  10.7 us
    pallas_call x1, Pallas kernels, per_device(): pl.pallas_call(shell_kernel, out_shape=[tiles(N_LINE), jax.ShapeDtypeStru...  3.21 us
  transfers between devices with their start and end apart: 4, of which 4 were waited for; matrix products, arithmetic and copies ran while one was open for 0% of the time, Pallas kernels for 12%

profile of v8, /device:TPU:1, one launch (start us, length us, event | category | flops | bytes accessed | tf_op | source)
XLA Modules:
  0.0 101.7 jit_solution(18272912981254510380)
XLA Ops:
  0.6 0.0 copy-start.2
  0.6 1.5 %shard_map.59 = (f32[16,8,128]{2,1,0:T(8,128)}, f32[32,8,128]{2,1,0:T(8,128)}) custom-call(f32[3,2,64]{2,1,0:T(2,128)} %fibre_ref.1, f32[3,1,16]{2,1,0:T(1,128)} %shell_ref.1), custom_call_target="tpu_custom_call" | custom-call | tf_op jit(solution)/shard_map/pallas_call | solution.py:303
  2.1 22.9 %all_to_all.30.tiles_ref.plane_ref = f32[32,8,128]{2,1,0:T(8,128)S(1)} all-to-all(f32[32,8,128]{2,1,0:T(8,128)} %get-tuple-element.33), channel_id=1, replica_groups=mesh['tgt_0'=4,'tgt_1'=8,'tgt_2'=2,'tgt_3'=2,'src'=4] {'tgt_0','tgt_1'}, dimensions={0} | all-to-all | bytes 262144 | tf_op jit(solution)/shard_map/all_to_all | solution.py:299
  25.0 9.2 %all-to-all-start.1 = ((f32[16,8,128]{2,1,0:T(8,128)}), f32[16,8,128]{2,1,0:T(8,128)S(1)}, u32[]{:S(2)}, u32[]{:S(2)}) async-start(f32[16,8,128]{2,1,0:T(8,128)} %get-tuple-element.34), calls=%async_computation.1 | async-start | bytes 131072 | tf_op jit(solution)/shard_map/all_to_all | solution.py:299
  34.2 0.0 copy-start.1
  34.2 0.8 copy-done.1
  34.9 0.6 shard_map.60
  35.5 6.2 %all-to-all-done.1.line_ref.tiles_ref = f32[16,8,128]{2,1,0:T(8,128)S(1)} async-done(((f32[16,8,128]{2,1,0:T(8,128)}), f32[16,8,128]{2,1,0:T(8,128)S(1)}, u32[]{:S(2)}, u32[]{:S(2)}) %all-to-all-start.1) | async-done | bytes 65568 | tf_op jit(solution)/shard_map/all_to_all | solution.py:299
  41.7 3.2 %shard_map.61 = (f32[16,8,128]{2,1,0:T(8,128)}, f32[8,256]{1,0:T(8,128)S(1)}) custom-call(f32[16,8,128]{2,1,0:T(8,128)S(1)} %all-to-all-done.1.line_ref.tiles_ref, bf16[32,4096]{1,0:T(8,128)(2,1)S(1)} %get-tuple-element.40.dist_ref, bf16[16,4096]{1,0:T(8,128)(2,1)S(1)} %get-tuple-element.41.push_ref, bf16[48,4096]{1,0:T(8,128)(2,1)S(1)} %get-tuple-element.42.form_ref, ...), custom_call_target="tpu_custom_call" | custom-call | flops 419430400 | bytes 1048576 | tf_op jit(solution)/shard_map/pallas_call | solution.py:320
  45.0 3.7 %all-to-all-start.2 = ((f32[16,8,128]{2,1,0:T(8,128)}), f32[16,8,128]{2,1,0:T(8,128)S(1)}, u32[]{:S(2)}, u32[]{:S(2)}) async-start(f32[16,8,128]{2,1,0:T(8,128)} %get-tuple-element.44), calls=%async_computation.2 | async-start | bytes 131072 | tf_op jit(solution)/shard_map/all_to_all | solution.py:299
  48.7 0.0 copy-done.2
  48.7 0.4 shard_map.62
  49.1 1.4 %shard_map.63.refs_0_ = f32[4,8,128]{2,1,0:T(8,128)S(1)} custom-call(f32[32,8,128]{2,1,0:T(8,128)S(1)} %all_to_all.30.tiles_ref.plane_ref, bf16[32,2048]{1,0:T(8,128)(2,1)S(1)} %get-tuple-element.47.dist_ref, bf16[16,2048]{1,0:T(8,128)(2,1)S(1)} %get-tuple-element.48.push_ref, bf16[48,2048]{1,0:T(8,128)(2,1)S(1)} %get-tuple-element.49.form_ref, ...), custom_call_target="tpu_custom_call" | custom-call | flops 419430400 | bytes 1048576 | tf_op jit(solution)/shard_map/pallas_call | solution.py:333
  50.5 5.8 %all-to-all-done.2.parts_ref = f32[16,8,128]{2,1,0:T(8,128)S(1)} async-done(((f32[16,8,128]{2,1,0:T(8,128)}), f32[16,8,128]{2,1,0:T(8,128)S(1)}, u32[]{:S(2)}, u32[]{:S(2)}) %all-to-all-start.2) | async-done | bytes 65568 | tf_op jit(solution)/shard_map/all_to_all | solution.py:299
  56.2 0.7 shard_map.64
  56.9 4.0 %all-to-all-start.3 = ((f32[32,8,128]{2,1,0:T(8,128)}), f32[32,8,128]{2,1,0:T(8,128)S(1)}, u32[]{:S(2)}, u32[]{:S(2)}) async-start(f32[32,8,128]{2,1,0:T(8,128)} %shard_map.64), calls=%async_computation.3 | async-start | bytes 262144 | tf_op jit(solution)/shard_map/all_to_all | solution.py:299
  61.0 0.0 copy-start
  61.0 6.6 %shard_map.65.refs_1_ = f32[20,8,128]{2,1,0:T(8,128)S(1)} custom-call(f32[32,8,128]{2,1,0:T(8,128)S(1)} %all_to_all.30.tiles_ref.plane_ref, bf16[32,2048]{1,0:T(8,128)(2,1)S(1)} %get-tuple-element.47.dist_ref, bf16[16,2048]{1,0:T(8,128)(2,1)S(1)} %get-tuple-element.48.push_ref, bf16[48,2048]{1,0:T(8,128)(2,1)S(1)} %get-tuple-element.49.form_ref, ...), custom_call_target="tpu_custom_call" | custom-call | flops 2097152000 | bytes 1048576 | tf_op jit(solution)/shard_map/pallas_call | solution.py:333
  67.6 2.3 %all-to-all-done.3.columns_ref = f32[32,8,128]{2,1,0:T(8,128)S(1)} async-done(((f32[32,8,128]{2,1,0:T(8,128)}), f32[32,8,128]{2,1,0:T(8,128)S(1)}, u32[]{:S(2)}, u32[]{:S(2)}) %all-to-all-start.3) | async-done | bytes 131104 | tf_op jit(solution)/shard_map/all_to_all | solution.py:299
  69.9 0.0 copy-done
  69.9 1.8 %shard_map.66 = f32[16,8,128]{2,1,0:T(8,128)} custom-call(s32[1]{0:T(128)} %bitcast.pair_ref, f32[32,8,128]{2,1,0:T(8,128)S(1)} %all-to-all-done.3.columns_ref, bf16[3,1,64,3,16,128]{5,4,3,2,1,0:T(8,128)(2,1)S(1)} %copy-done), custom_call_target="tpu_custom_call" | custom-call | tf_op jit(solution)/shard_map/pallas_call | solution.py:348
  71.7 5.4 %all-to-all-start.4 = ((f32[16,8,128]{2,1,0:T(8,128)}), f32[16,8,128]{2,1,0:T(8,128)S(1)}, u32[]{:S(2)}, u32[]{:S(2)}) async-start(f32[16,8,128]{2,1,0:T(8,128)} %shard_map.66), calls=%async_computation.4 | async-start | bytes 131072 | tf_op jit(solution)/shard_map/all_to_all | solution.py:299
  77.1 2.7 %shard_map.67.refs_2_ = f32[8,8,128]{2,1,0:T(8,128)S(1)} custom-call(f32[32,8,128]{2,1,0:T(8,128)S(1)} %all_to_all.30.tiles_ref.plane_ref, bf16[32,2048]{1,0:T(8,128)(2,1)S(1)} %get-tuple-element.47.dist_ref, bf16[16,2048]{1,0:T(8,128)(2,1)S(1)} %get-tuple-element.48.push_ref, bf16[48,2048]{1,0:T(8,128)(2,1)S(1)} %get-tuple-element.49.form_ref, ...), custom_call_target="tpu_custom_call" | custom-call | flops 838860800 | bytes 1048576 | tf_op jit(solution)/shard_map/pallas_call | solution.py:333
  79.9 4.8 %all-to-all-done.4.parts_ref = f32[16,8,128]{2,1,0:T(8,128)S(1)} async-done(((f32[16,8,128]{2,1,0:T(8,128)}), f32[16,8,128]{2,1,0:T(8,128)S(1)}, u32[]{:S(2)}, u32[]{:S(2)}) %all-to-all-start.4) | async-done | bytes 65568 | tf_op jit(solution)/shard_map/all_to_all | solution.py:299
  84.7 2.0 %shard_map.68 = (f32[32,8,128]{2,1,0:T(8,128)S(1)}, f32[3,1,16]{2,1,0:T(1,128)}) custom-call(f32[16,8,128]{2,1,0:T(8,128)S(1)} %all-to-all-done.4.parts_ref, f32[8,256]{1,0:T(8,128)S(1)} %get-tuple-element.56.shell_ref, f32[32,8,128]{2,1,0:T(8,128)S(1)} %all_to_all.30.tiles_ref.plane_ref, f32[4,8,128]{2,1,0:T(8,128)S(1)} %shard_map.63.refs_0_, ...), custom_call_target="tpu_custom_call" | custom-call | flops 419430400 | bytes 1048576 | tf_op jit(solution)/shard_map/pallas_call | solution.py:355
  86.8 14.2 %all_to_all.31.parts_ref = f32[32,8,128]{2,1,0:T(8,128)S(1)} all-to-all(f32[32,8,128]{2,1,0:T(8,128)S(1)} %get-tuple-element.60), channel_id=1, replica_groups=mesh['tgt_0'=4,'tgt_1'=8,'tgt_2'=2,'tgt_3'=2,'src'=4] {'tgt_0','tgt_1'}, dimensions={0} | all-to-all | bytes 262144 | tf_op jit(solution)/shard_map/all_to_all | solution.py:299
  101.0 0.7 shard_map.69
Async XLA Ops:
  0.6 48.0 %copy-start.2 = (f32[64,64]{1,0:T(8,128)S(1)}, f32[64,64]{1,0:T(8,128)}, u32[]{:S(2)}) copy-start(f32[64,64]{1,0:T(8,128)} %bending_ref.3) | copy-start | bytes 49156
  25.0 16.8 %all-to-all-start.1 = ((f32[16,8,128]{2,1,0:T(8,128)}), f32[16,8,128]{2,1,0:T(8,128)S(1)}, u32[]{:S(2)}, u32[]{:S(2)}) async-start(f32[16,8,128]{2,1,0:T(8,128)} %get-tuple-element.34), calls=%async_computation.1 | async-start | bytes 131072 | tf_op jit(solution)/shard_map/all_to_all | solution.py:299
  34.2 0.8 copy-start.1
  45.0 11.3 %all-to-all-start.2 = ((f32[16,8,128]{2,1,0:T(8,128)}), f32[16,8,128]{2,1,0:T(8,128)S(1)}, u32[]{:S(2)}, u32[]{:S(2)}) async-start(f32[16,8,128]{2,1,0:T(8,128)} %get-tuple-element.44), calls=%async_computation.2 | async-start | bytes 131072 | tf_op jit(solution)/shard_map/all_to_all | solution.py:299
  56.9 13.0 %all-to-all-start.3 = ((f32[32,8,128]{2,1,0:T(8,128)}), f32[32,8,128]{2,1,0:T(8,128)S(1)}, u32[]{:S(2)}, u32[]{:S(2)}) async-start(f32[32,8,128]{2,1,0:T(8,128)} %shard_map.64), calls=%async_computation.3 | async-start | bytes 262144 | tf_op jit(solution)/shard_map/all_to_all | solution.py:299
  61.0 9.0 %copy-start = (bf16[3,1,64,3,16,128]{5,4,3,2,1,0:T(8,128)(2,1)S(1)}, bf16[3,1,64,3,16,128]{5,4,3,2,1,0:T(8,128)(2,1)}, u32[]{:S(2)}) copy-start(bf16[3,1,64,3,16,128]{5,4,3,2,1,0:T(8,128)(2,1)} %inverse_ref.1) | copy-start | bytes 7077892
  71.7 13.0 %all-to-all-start.4 = ((f32[16,8,128]{2,1,0:T(8,128)}), f32[16,8,128]{2,1,0:T(8,128)S(1)}, u32[]{:S(2)}, u32[]{:S(2)}) async-start(f32[16,8,128]{2,1,0:T(8,128)} %shard_map.66), calls=%async_computation.4 | async-start | bytes 131072 | tf_op jit(solution)/shard_map/all_to_all | solution.py:299

commit v9 on v8

--- a/solution.py
+++ b/solution.py
@@ -17,8 +17,7 @@
 N_PLANE = 32
 SOURCES = N_PLANE * 128
 LINE_SOURCES = N_LINE * 128
-CHUNKS = ((0, 1), (4, 5), (24, 2))
-WIDE = 4
+CHUNKS = ((0, 1, 4, 1024), (4, 2, 10, 512), (24, 1, 8, 512))
 BROAD = 16
 ROW_SOURCES = 256
 ROWS = (((0,), (0,)), ((), ()))
@@ -170,21 +169,22 @@
             part_ref[pair * 4 + src] = piece
 
 
-def fibre_kernel(first, parts, plane_ref, dist_ref, push_ref, form_ref, center_ref, flow_ref):
+def fibre_kernel(chunk, plane_ref, dist_ref, push_ref, form_ref, center_ref, flow_ref):
+    first, parts, wide, step = chunk
     for part in range(parts):
         flow = pair_sums(
-            side_by_side(plane_ref, first + part * WIDE, WIDE),
+            side_by_side(plane_ref, first + part * wide, wide),
             LINE_SOURCES,
             dist_ref,
             push_ref,
             form_ref,
             center_ref,
-            1024,
-            2,
+            step,
+            2048 // step,
             False,
         )
-        for i in range(WIDE):
-            flow_ref[part * WIDE + i] = flow[:, 128 * i : 128 * i + 128]
+        for i in range(wide):
+            flow_ref[part * wide + i] = flow[:, 128 * i : 128 * i + 128]
 
 
 def total_of(parts_ref):
@@ -328,13 +328,14 @@
     flows = []
 
     def exchange_beside(x, axes):
-        first, parts = CHUNKS[len(flows)]
+        chunk = CHUNKS[len(flows)]
+        count = chunk[1] * chunk[2]
         held, _ = lax.optimization_barrier((plane, x))
         flow = pl.pallas_call(
-            functools.partial(fibre_kernel, first, parts),
-            out_shape=tiles(parts * WIDE),
+            functools.partial(fibre_kernel, chunk),
+            out_shape=tiles(count),
             compiler_params=params(24),
-            cost_estimate=cost(parts * WIDE * 128 * LINE_SOURCES),
+            cost_estimate=cost(count * 128 * LINE_SOURCES),
         )(held, *features)
         x, flow = lax.optimization_barrier((exchange(x, axes), flow))
         flows.append(flow)

time: 102 us -> 102 us (level)
  transfers between devices with their start and end apart: 4 -> 4, of which waited for: 4 -> 4; matrix products, arithmetic and copies ran while one was open for 0% -> 0% of each run, Pallas kernels for 12% -> 11%
where the time goes in v9:
time: 102 us; the launch traced here: 101 us
  blocking collectives  36.6 us (36%)
  starting transfers between devices  22.3 us (22%)
  Pallas kernels  21 us (21%)
  waiting for transfers between devices  19.8 us (19%)
    all_to_all x2, blocking collectives, exchange(): return lax.all_to_all(x, axes, 0, 0, tiled=True)  36.6 us
    all_to_all x4, starting transfers between devices, exchange(): return lax.all_to_all(x, axes, 0, 0, tiled=True)  22.3 us
    all_to_all x4, waiting for transfers between devices, exchange(): return lax.all_to_all(x, axes, 0, 0, tiled=True)  19.8 us
    pallas_call x3, Pallas kernels, exchange_beside(): pl.pallas_call(functools.partial(fibre_kernel, chunk), out_shape=tiles(co...  10.1 us
    pallas_call x1, Pallas kernels, per_device(): pl.pallas_call(shell_kernel, out_shape=[tiles(N_LINE), jax.ShapeDtypeStru...  3.21 us
  transfers between devices with their start and end apart: 4, of which 4 were waited for; matrix products, arithmetic and copies ran while one was open for 0% of the time, Pallas kernels for 11%

profile of v9, /device:TPU:1, one launch (start us, length us, event | category | flops | bytes accessed | tf_op | source)
XLA Modules:
  0.0 101.2 jit_solution(8553654987242277403)
XLA Ops:
  0.6 0.0 copy-start.2
  0.6 1.5 %shard_map.59 = (f32[16,8,128]{2,1,0:T(8,128)}, f32[32,8,128]{2,1,0:T(8,128)}) custom-call(f32[3,2,64]{2,1,0:T(2,128)} %fibre_ref.1, f32[3,1,16]{2,1,0:T(1,128)} %shell_ref.1), custom_call_target="tpu_custom_call" | custom-call | tf_op jit(solution)/shard_map/pallas_call | solution.py:303
  2.1 22.9 %all_to_all.30.tiles_ref.plane_ref = f32[32,8,128]{2,1,0:T(8,128)S(1)} all-to-all(f32[32,8,128]{2,1,0:T(8,128)} %get-tuple-element.33), channel_id=1, replica_groups=mesh['tgt_0'=4,'tgt_1'=8,'tgt_2'=2,'tgt_3'=2,'src'=4] {'tgt_0','tgt_1'}, dimensions={0} | all-to-all | bytes 262144 | tf_op jit(solution)/shard_map/all_to_all | solution.py:299
  25.0 9.2 %all-to-all-start.1 = ((f32[16,8,128]{2,1,0:T(8,128)}), f32[16,8,128]{2,1,0:T(8,128)S(1)}, u32[]{:S(2)}, u32[]{:S(2)}) async-start(f32[16,8,128]{2,1,0:T(8,128)} %get-tuple-element.34), calls=%async_computation.1 | async-start | bytes 131072 | tf_op jit(solution)/shard_map/all_to_all | solution.py:299
  34.2 0.0 copy-start.1
  34.2 0.8 copy-done.1
  34.9 0.6 shard_map.60
  35.5 6.2 %all-to-all-done.1.line_ref.tiles_ref = f32[16,8,128]{2,1,0:T(8,128)S(1)} async-done(((f32[16,8,128]{2,1,0:T(8,128)}), f32[16,8,128]{2,1,0:T(8,128)S(1)}, u32[]{:S(2)}, u32[]{:S(2)}) %all-to-all-start.1) | async-done | bytes 65568 | tf_op jit(solution)/shard_map/all_to_all | solution.py:299
  41.7 3.2 %shard_map.61 = (f32[16,8,128]{2,1,0:T(8,128)}, f32[8,256]{1,0:T(8,128)S(1)}) custom-call(f32[16,8,128]{2,1,0:T(8,128)S(1)} %all-to-all-done.1.line_ref.tiles_ref, bf16[32,4096]{1,0:T(8,128)(2,1)S(1)} %get-tuple-element.40.dist_ref, bf16[16,4096]{1,0:T(8,128)(2,1)S(1)} %get-tuple-element.41.push_ref, bf16[48,4096]{1,0:T(8,128)(2,1)S(1)} %get-tuple-element.42.form_ref, ...), custom_call_target="tpu_custom_call" | custom-call | flops 419430400 | bytes 1048576 | tf_op jit(solution)/shard_map/pallas_call | solution.py:320
  45.0 3.7 %all-to-all-start.2 = ((f32[16,8,128]{2,1,0:T(8,128)}), f32[16,8,128]{2,1,0:T(8,128)S(1)}, u32[]{:S(2)}, u32[]{:S(2)}) async-start(f32[16,8,128]{2,1,0:T(8,128)} %get-tuple-element.44), calls=%async_computation.2 | async-start | bytes 131072 | tf_op jit(solution)/shard_map/all_to_all | solution.py:299
  48.7 0.0 copy-done.2
  48.7 0.4 shard_map.62
  49.1 1.4 %shard_map.63.refs_0_ = f32[4,8,128]{2,1,0:T(8,128)S(1)} custom-call(f32[32,8,128]{2,1,0:T(8,128)S(1)} %all_to_all.30.tiles_ref.plane_ref, bf16[32,2048]{1,0:T(8,128)(2,1)S(1)} %get-tuple-element.47.dist_ref, bf16[16,2048]{1,0:T(8,128)(2,1)S(1)} %get-tuple-element.48.push_ref, bf16[48,2048]{1,0:T(8,128)(2,1)S(1)} %get-tuple-element.49.form_ref, ...), custom_call_target="tpu_custom_call" | custom-call | flops 419430400 | bytes 1048576 | tf_op jit(solution)/shard_map/pallas_call | solution.py:334
  50.5 5.8 %all-to-all-done.2.parts_ref = f32[16,8,128]{2,1,0:T(8,128)S(1)} async-done(((f32[16,8,128]{2,1,0:T(8,128)}), f32[16,8,128]{2,1,0:T(8,128)S(1)}, u32[]{:S(2)}, u32[]{:S(2)}) %all-to-all-start.2) | async-done | bytes 65568 | tf_op jit(solution)/shard_map/all_to_all | solution.py:299
  56.2 0.7 shard_map.64
  56.9 4.0 %all-to-all-start.3 = ((f32[32,8,128]{2,1,0:T(8,128)}), f32[32,8,128]{2,1,0:T(8,128)S(1)}, u32[]{:S(2)}, u32[]{:S(2)}) async-start(f32[32,8,128]{2,1,0:T(8,128)} %shard_map.64), calls=%async_computation.3 | async-start | bytes 262144 | tf_op jit(solution)/shard_map/all_to_all | solution.py:299
  61.0 0.0 copy-start
  61.0 6.1 %shard_map.65.refs_1_ = f32[20,8,128]{2,1,0:T(8,128)S(1)} custom-call(f32[32,8,128]{2,1,0:T(8,128)S(1)} %all_to_all.30.tiles_ref.plane_ref, bf16[32,2048]{1,0:T(8,128)(2,1)S(1)} %get-tuple-element.47.dist_ref, bf16[16,2048]{1,0:T(8,128)(2,1)S(1)} %get-tuple-element.48.push_ref, bf16[48,2048]{1,0:T(8,128)(2,1)S(1)} %get-tuple-element.49.form_ref, ...), custom_call_target="tpu_custom_call" | custom-call | flops 2097152000 | bytes 1048576 | tf_op jit(solution)/shard_map/pallas_call | solution.py:334
  67.1 2.8 %all-to-all-done.3.columns_ref = f32[32,8,128]{2,1,0:T(8,128)S(1)} async-done(((f32[32,8,128]{2,1,0:T(8,128)}), f32[32,8,128]{2,1,0:T(8,128)S(1)}, u32[]{:S(2)}, u32[]{:S(2)}) %all-to-all-start.3) | async-done | bytes 131104 | tf_op jit(solution)/shard_map/all_to_all | solution.py:299
  69.9 0.0 copy-done
  69.9 1.8 %shard_map.66 = f32[16,8,128]{2,1,0:T(8,128)} custom-call(s32[1]{0:T(128)} %bitcast.pair_ref, f32[32,8,128]{2,1,0:T(8,128)S(1)} %all-to-all-done.3.columns_ref, bf16[3,1,64,3,16,128]{5,4,3,2,1,0:T(8,128)(2,1)S(1)} %copy-done), custom_call_target="tpu_custom_call" | custom-call | tf_op jit(solution)/shard_map/pallas_call | solution.py:349
  71.7 5.4 %all-to-all-start.4 = ((f32[16,8,128]{2,1,0:T(8,128)}), f32[16,8,128]{2,1,0:T(8,128)S(1)}, u32[]{:S(2)}, u32[]{:S(2)}) async-start(f32[16,8,128]{2,1,0:T(8,128)} %shard_map.66), calls=%async_computation.4 | async-start | bytes 131072 | tf_op jit(solution)/shard_map/all_to_all | solution.py:299
  77.1 2.6 %shard_map.67.refs_2_ = f32[8,8,128]{2,1,0:T(8,128)S(1)} custom-call(f32[32,8,128]{2,1,0:T(8,128)S(1)} %all_to_all.30.tiles_ref.plane_ref, bf16[32,2048]{1,0:T(8,128)(2,1)S(1)} %get-tuple-element.47.dist_ref, bf16[16,2048]{1,0:T(8,128)(2,1)S(1)} %get-tuple-element.48.push_ref, bf16[48,2048]{1,0:T(8,128)(2,1)S(1)} %get-tuple-element.49.form_ref, ...), custom_call_target="tpu_custom_call" | custom-call | flops 838860800 | bytes 1048576 | tf_op jit(solution)/shard_map/pallas_call | solution.py:334
  79.8 5.0 %all-to-all-done.4.parts_ref = f32[16,8,128]{2,1,0:T(8,128)S(1)} async-done(((f32[16,8,128]{2,1,0:T(8,128)}), f32[16,8,128]{2,1,0:T(8,128)S(1)}, u32[]{:S(2)}, u32[]{:S(2)}) %all-to-all-start.4) | async-done | bytes 65568 | tf_op jit(solution)/shard_map/all_to_all | solution.py:299
  84.7 2.0 %shard_map.68 = (f32[32,8,128]{2,1,0:T(8,128)S(1)}, f32[3,1,16]{2,1,0:T(1,128)}) custom-call(f32[16,8,128]{2,1,0:T(8,128)S(1)} %all-to-all-done.4.parts_ref, f32[8,256]{1,0:T(8,128)S(1)} %get-tuple-element.56.shell_ref, f32[32,8,128]{2,1,0:T(8,128)S(1)} %all_to_all.30.tiles_ref.plane_ref, f32[4,8,128]{2,1,0:T(8,128)S(1)} %shard_map.63.refs_0_, ...), custom_call_target="tpu_custom_call" | custom-call | flops 419430400 | bytes 1048576 | tf_op jit(solution)/shard_map/pallas_call | solution.py:356
  86.8 13.7 %all_to_all.31.parts_ref = f32[32,8,128]{2,1,0:T(8,128)S(1)} all-to-all(f32[32,8,128]{2,1,0:T(8,128)S(1)} %get-tuple-element.60), channel_id=1, replica_groups=mesh['tgt_0'=4,'tgt_1'=8,'tgt_2'=2,'tgt_3'=2,'src'=4] {'tgt_0','tgt_1'}, dimensions={0} | all-to-all | bytes 262144 | tf_op jit(solution)/shard_map/all_to_all | solution.py:299
  100.5 0.7 shard_map.69
Async XLA Ops:
  0.6 48.0 %copy-start.2 = (f32[64,64]{1,0:T(8,128)S(1)}, f32[64,64]{1,0:T(8,128)}, u32[]{:S(2)}) copy-start(f32[64,64]{1,0:T(8,128)} %bending_ref.3) | copy-start | bytes 49156
  25.0 16.8 %all-to-all-start.1 = ((f32[16,8,128]{2,1,0:T(8,128)}), f32[16,8,128]{2,1,0:T(8,128)S(1)}, u32[]{:S(2)}, u32[]{:S(2)}) async-start(f32[16,8,128]{2,1,0:T(8,128)} %get-tuple-element.34), calls=%async_computation.1 | async-start | bytes 131072 | tf_op jit(solution)/shard_map/all_to_all | solution.py:299
  34.2 0.8 copy-start.1
  45.0 11.3 %all-to-all-start.2 = ((f32[16,8,128]{2,1,0:T(8,128)}), f32[16,8,128]{2,1,0:T(8,128)S(1)}, u32[]{:S(2)}, u32[]{:S(2)}) async-start(f32[16,8,128]{2,1,0:T(8,128)} %get-tuple-element.44), calls=%async_computation.2 | async-start | bytes 131072 | tf_op jit(solution)/shard_map/all_to_all | solution.py:299
  56.9 13.0 %all-to-all-start.3 = ((f32[32,8,128]{2,1,0:T(8,128)}), f32[32,8,128]{2,1,0:T(8,128)S(1)}, u32[]{:S(2)}, u32[]{:S(2)}) async-start(f32[32,8,128]{2,1,0:T(8,128)} %shard_map.64), calls=%async_computation.3 | async-start | bytes 262144 | tf_op jit(solution)/shard_map/all_to_all | solution.py:299
  61.0 9.0 %copy-start = (bf16[3,1,64,3,16,128]{5,4,3,2,1,0:T(8,128)(2,1)S(1)}, bf16[3,1,64,3,16,128]{5,4,3,2,1,0:T(8,128)(2,1)}, u32[]{:S(2)}) copy-start(bf16[3,1,64,3,16,128]{5,4,3,2,1,0:T(8,128)(2,1)} %inverse_ref.1) | copy-start | bytes 7077892
  71.7 13.0 %all-to-all-start.4 = ((f32[16,8,128]{2,1,0:T(8,128)}), f32[16,8,128]{2,1,0:T(8,128)S(1)}, u32[]{:S(2)}, u32[]{:S(2)}) async-start(f32[16,8,128]{2,1,0:T(8,128)} %shard_map.66), calls=%async_computation.4 | async-start | bytes 131072 | tf_op jit(solution)/shard_map/all_to_all | solution.py:299

commit v10 on v9

--- a/solution.py
+++ b/solution.py
@@ -17,7 +17,7 @@
 N_PLANE = 32
 SOURCES = N_PLANE * 128
 LINE_SOURCES = N_LINE * 128
-CHUNKS = ((0, 1, 4, 1024), (4, 2, 10, 512), (24, 1, 8, 512))
+CHUNKS = ((0, 2, 11, 512), (22, 1, 10, 512))
 BROAD = 16
 ROW_SOURCES = 256
 ROWS = (((0,), (0,)), ((), ()))
@@ -323,7 +323,10 @@
         compiler_params=params(24),
         cost_estimate=cost(256 * SOURCES),
     )(line, *features)
-    held, _ = lax.optimization_barrier((line, shell_part))
+    shell_own = pl.pallas_call(
+        columns_kernel, out_shape=tiles(N_PLANE), compiler_params=params(2)
+    )(exchange(shell_part, LINE))
+    held, _ = lax.optimization_barrier((line, shell_own))
     features = features_of(held)
     flows = []
 
@@ -341,9 +344,6 @@
         flows.append(flow)
         return x
 
-    shell_own = pl.pallas_call(
-        columns_kernel, out_shape=tiles(N_PLANE), compiler_params=params(2)
-    )(exchange_beside(shell_part, LINE))
     shell_all = exchange_beside(shell_own, PLANE)
     pair = lax.axis_index("tgt_2") * 2 + lax.axis_index("tgt_3")
     message = pl.pallas_call(

time: 102 us -> 102 us (level)
  blocking collectives: 36.6 us -> 48.1 us
  waiting for transfers between devices: 19.8 us -> 12.6 us
  starting transfers between devices: 22.3 us -> 18.6 us
    all_to_all x2 -> x3, blocking collectives: 36.6 us -> 48.1 us  [exchange(): return lax.all_to_all(x, axes, 0, 0, tiled=True)]
    all_to_all x4 -> x3, waiting for transfers between devices: 19.8 us -> 12.6 us  [exchange(): return lax.all_to_all(x, axes, 0, 0, tiled=True)]
    all_to_all x4 -> x3, starting transfers between devices: 22.3 us -> 18.6 us  [exchange(): return lax.all_to_all(x, axes, 0, 0, tiled=True)]
    pallas_call x3 -> x2, Pallas kernels: 10.1 us -> 9.9 us  [exchange_beside(): pl.pallas_call(functools.partial(fibre_kernel, chunk), out_shape=tiles(co...]
  transfers between devices with their start and end apart: 4 -> 3, of which waited for: 4 -> 3; matrix products, arithmetic and copies ran while one was open for 0% -> 0% of each run, Pallas kernels for 11% -> 11%
where the time goes in v10:
time: 102 us; the launch traced here: 101 us
  blocking collectives  48.1 us (47%)
  Pallas kernels  20.2 us (20%)
  starting transfers between devices  18.6 us (18%)
  waiting for transfers between devices  12.6 us (12%)
    all_to_all x3, blocking collectives, exchange(): return lax.all_to_all(x, axes, 0, 0, tiled=True)  48.1 us
    all_to_all x3, starting transfers between devices, exchange(): return lax.all_to_all(x, axes, 0, 0, tiled=True)  18.6 us
    all_to_all x3, waiting for transfers between devices, exchange(): return lax.all_to_all(x, axes, 0, 0, tiled=True)  12.6 us
    pallas_call x2, Pallas kernels, exchange_beside(): pl.pallas_call(functools.partial(fibre_kernel, chunk), out_shape=tiles(co...  9.9 us
    pallas_call x1, Pallas kernels, per_device(): pl.pallas_call(shell_kernel, out_shape=[tiles(N_LINE), jax.ShapeDtypeStru...  2.59 us
  transfers between devices with their start and end apart: 3, of which 3 were waited for; matrix products, arithmetic and copies ran while one was open for 0% of the time, Pallas kernels for 11%

profile of v10, /device:TPU:1, one launch (start us, length us, event | category | flops | bytes accessed | tf_op | source)
XLA Modules:
  0.0 101.0 jit_solution(3758730888290060147)
XLA Ops:
  0.6 0.0 copy-start.2
  0.6 1.5 %shard_map.59 = (f32[16,8,128]{2,1,0:T(8,128)}, f32[32,8,128]{2,1,0:T(8,128)}) custom-call(f32[3,2,64]{2,1,0:T(2,128)} %fibre_ref.1, f32[3,1,16]{2,1,0:T(1,128)} %shell_ref.1), custom_call_target="tpu_custom_call" | custom-call | tf_op jit(solution)/shard_map/pallas_call | solution.py:303
  2.1 22.9 %all_to_all.30.tiles_ref.plane_ref = f32[32,8,128]{2,1,0:T(8,128)S(1)} all-to-all(f32[32,8,128]{2,1,0:T(8,128)} %get-tuple-element.30), channel_id=1, replica_groups=mesh['tgt_0'=4,'tgt_1'=8,'tgt_2'=2,'tgt_3'=2,'src'=4] {'tgt_0','tgt_1'}, dimensions={0} | all-to-all | bytes 262144 | tf_op jit(solution)/shard_map/all_to_all | solution.py:299
  25.0 9.2 %all-to-all-start.1 = ((f32[16,8,128]{2,1,0:T(8,128)}), f32[16,8,128]{2,1,0:T(8,128)S(1)}, u32[]{:S(2)}, u32[]{:S(2)}) async-start(f32[16,8,128]{2,1,0:T(8,128)} %get-tuple-element.31), calls=%async_computation.1 | async-start | bytes 131072 | tf_op jit(solution)/shard_map/all_to_all | solution.py:299
  34.2 0.0 copy-start.1
  34.2 0.8 copy-done.1
  34.9 0.6 shard_map.60
  35.5 6.2 %all-to-all-done.1.line_ref.tiles_ref = f32[16,8,128]{2,1,0:T(8,128)S(1)} async-done(((f32[16,8,128]{2,1,0:T(8,128)}), f32[16,8,128]{2,1,0:T(8,128)S(1)}, u32[]{:S(2)}, u32[]{:S(2)}) %all-to-all-start.1) | async-done | bytes 65568 | tf_op jit(solution)/shard_map/all_to_all | solution.py:299
  41.7 2.6 %shard_map.61 = (f32[16,8,128]{2,1,0:T(8,128)S(1)}, f32[8,256]{1,0:T(8,128)S(1)}) custom-call(f32[16,8,128]{2,1,0:T(8,128)S(1)} %all-to-all-done.1.line_ref.tiles_ref, bf16[32,4096]{1,0:T(8,128)(2,1)S(1)} %get-tuple-element.37.dist_ref, bf16[16,4096]{1,0:T(8,128)(2,1)S(1)} %get-tuple-element.38.push_ref, bf16[48,4096]{1,0:T(8,128)(2,1)S(1)} %get-tuple-element.39.form_ref, ...), custom_call_target="tpu_custom_call" | custom-call | flops 419430400 | bytes 1048576 | tf_op jit(solution)/shard_map/pallas_call | solution.py:320
  44.3 10.4 %all_to_all.31.parts_ref = f32[16,8,128]{2,1,0:T(8,128)S(1)} all-to-all(f32[16,8,128]{2,1,0:T(8,128)S(1)} %get-tuple-element.41), channel_id=1, replica_groups=mesh['tgt_0'=4,'tgt_1'=8,'tgt_2'=2,'tgt_3'=2,'src'=4] {'tgt_2','tgt_3','..., dimensions={0} | all-to-all | bytes 131072 | tf_op jit(solution)/shard_map/all_to_all | solution.py:299
  54.7 0.7 shard_map.62
  55.4 3.8 %all-to-all-start.3 = ((f32[32,8,128]{2,1,0:T(8,128)}), f32[32,8,128]{2,1,0:T(8,128)S(1)}, u32[]{:S(2)}, u32[]{:S(2)}) async-start(f32[32,8,128]{2,1,0:T(8,128)} %shard_map.62), calls=%async_computation.3 | async-start | bytes 262144 | tf_op jit(solution)/shard_map/all_to_all | solution.py:299
  59.3 0.0 copy-done.2
  59.3 0.4 shard_map.63
  59.7 0.0 copy-start
  59.7 6.8 %shard_map.64.refs_0_ = f32[22,8,128]{2,1,0:T(8,128)S(1)} custom-call(f32[32,8,128]{2,1,0:T(8,128)S(1)} %all_to_all.30.tiles_ref.plane_ref, bf16[32,2048]{1,0:T(8,128)(2,1)S(1)} %get-tuple-element.44.dist_ref, bf16[16,2048]{1,0:T(8,128)(2,1)S(1)} %get-tuple-element.45.push_ref, bf16[48,2048]{1,0:T(8,128)(2,1)S(1)} %get-tuple-element.46.form_ref, ...), custom_call_target="tpu_custom_call" | custom-call | flops 2306867200 | bytes 1048576 | tf_op jit(solution)/shard_map/pallas_call | solution.py:337
  66.5 1.9 %all-to-all-done.3.columns_ref = f32[32,8,128]{2,1,0:T(8,128)S(1)} async-done(((f32[32,8,128]{2,1,0:T(8,128)}), f32[32,8,128]{2,1,0:T(8,128)S(1)}, u32[]{:S(2)}, u32[]{:S(2)}) %all-to-all-start.3) | async-done | bytes 131104 | tf_op jit(solution)/shard_map/all_to_all | solution.py:299
  68.4 0.0 copy-done
  68.4 1.8 %shard_map.65 = f32[16,8,128]{2,1,0:T(8,128)} custom-call(s32[1]{0:T(128)} %bitcast.pair_ref, f32[32,8,128]{2,1,0:T(8,128)S(1)} %all-to-all-done.3.columns_ref, bf16[3,1,64,3,16,128]{5,4,3,2,1,0:T(8,128)(2,1)S(1)} %copy-done), custom_call_target="tpu_custom_call" | custom-call | tf_op jit(solution)/shard_map/pallas_call | solution.py:349
  70.2 5.6 %all-to-all-start.4 = ((f32[16,8,128]{2,1,0:T(8,128)}), f32[16,8,128]{2,1,0:T(8,128)S(1)}, u32[]{:S(2)}, u32[]{:S(2)}) async-start(f32[16,8,128]{2,1,0:T(8,128)} %shard_map.65), calls=%async_computation.4 | async-start | bytes 131072 | tf_op jit(solution)/shard_map/all_to_all | solution.py:299
  75.8 3.1 %shard_map.66.refs_1_ = f32[10,8,128]{2,1,0:T(8,128)S(1)} custom-call(f32[32,8,128]{2,1,0:T(8,128)S(1)} %all_to_all.30.tiles_ref.plane_ref, bf16[32,2048]{1,0:T(8,128)(2,1)S(1)} %get-tuple-element.44.dist_ref, bf16[16,2048]{1,0:T(8,128)(2,1)S(1)} %get-tuple-element.45.push_ref, bf16[48,2048]{1,0:T(8,128)(2,1)S(1)} %get-tuple-element.46.form_ref, ...), custom_call_target="tpu_custom_call" | custom-call | flops 1048576000 | bytes 1048576 | tf_op jit(solution)/shard_map/pallas_call | solution.py:337
  78.9 4.5 %all-to-all-done.4.parts_ref = f32[16,8,128]{2,1,0:T(8,128)S(1)} async-done(((f32[16,8,128]{2,1,0:T(8,128)}), f32[16,8,128]{2,1,0:T(8,128)S(1)}, u32[]{:S(2)}, u32[]{:S(2)}) %all-to-all-start.4) | async-done | bytes 65568 | tf_op jit(solution)/shard_map/all_to_all | solution.py:299
  83.4 2.0 %shard_map.67 = (f32[32,8,128]{2,1,0:T(8,128)S(1)}, f32[3,1,16]{2,1,0:T(1,128)}) custom-call(f32[16,8,128]{2,1,0:T(8,128)S(1)} %all-to-all-done.4.parts_ref, f32[8,256]{1,0:T(8,128)S(1)} %get-tuple-element.51.shell_ref, f32[32,8,128]{2,1,0:T(8,128)S(1)} %all_to_all.30.tiles_ref.plane_ref, f32[22,8,128]{2,1,0:T(8,128)S(1)} %shard_map.64.refs_0_, ...), custom_call_target="tpu_custom_call" | custom-call | flops 419430400 | bytes 1048576 | tf_op jit(solution)/shard_map/pallas_call | solution.py:356
  85.4 14.9 %all_to_all.32.parts_ref = f32[32,8,128]{2,1,0:T(8,128)S(1)} all-to-all(f32[32,8,128]{2,1,0:T(8,128)S(1)} %get-tuple-element.54), channel_id=1, replica_groups=mesh['tgt_0'=4,'tgt_1'=8,'tgt_2'=2,'tgt_3'=2,'src'=4] {'tgt_0','tgt_1'}, dimensions={0} | all-to-all | bytes 262144 | tf_op jit(solution)/shard_map/all_to_all | solution.py:299
  100.3 0.7 shard_map.68
Async XLA Ops:
  0.6 58.6 %copy-start.2 = (f32[64,64]{1,0:T(8,128)S(1)}, f32[64,64]{1,0:T(8,128)}, u32[]{:S(2)}) copy-start(f32[64,64]{1,0:T(8,128)} %bending_ref.3) | copy-start | bytes 49156
  25.0 16.8 %all-to-all-start.1 = ((f32[16,8,128]{2,1,0:T(8,128)}), f32[16,8,128]{2,1,0:T(8,128)S(1)}, u32[]{:S(2)}, u32[]{:S(2)}) async-start(f32[16,8,128]{2,1,0:T(8,128)} %get-tuple-element.31), calls=%async_computation.1 | async-start | bytes 131072 | tf_op jit(solution)/shard_map/all_to_all | solution.py:299
  34.2 0.8 copy-start.1
  55.4 13.0 %all-to-all-start.3 = ((f32[32,8,128]{2,1,0:T(8,128)}), f32[32,8,128]{2,1,0:T(8,128)S(1)}, u32[]{:S(2)}, u32[]{:S(2)}) async-start(f32[32,8,128]{2,1,0:T(8,128)} %shard_map.62), calls=%async_computation.3 | async-start | bytes 262144 | tf_op jit(solution)/shard_map/all_to_all | solution.py:299
  59.7 8.7 %copy-start = (bf16[3,1,64,3,16,128]{5,4,3,2,1,0:T(8,128)(2,1)S(1)}, bf16[3,1,64,3,16,128]{5,4,3,2,1,0:T(8,128)(2,1)}, u32[]{:S(2)}) copy-start(bf16[3,1,64,3,16,128]{5,4,3,2,1,0:T(8,128)(2,1)} %inverse_ref.1) | copy-start | bytes 7077892
  70.2 13.2 %all-to-all-start.4 = ((f32[16,8,128]{2,1,0:T(8,128)}), f32[16,8,128]{2,1,0:T(8,128)S(1)}, u32[]{:S(2)}, u32[]{:S(2)}) async-start(f32[16,8,128]{2,1,0:T(8,128)} %shard_map.65), calls=%async_computation.4 | async-start | bytes 131072 | tf_op jit(solution)/shard_map/all_to_all | solution.py:299
